TPU v7x, 32 devices: a whole 2x2x4 slice. The times are simulated.
32 devices in a mesh: section: 2 (over core), dp: 16 (over z, y, x).
Axes of the slice: x: 2, y: 2, z: 4, core: 2. Of those that a mesh axis runs over, the one named last changes fastest.
Arguments:
- tokens: bfloat16 [2, 2048, 768], P(None, 'dp'), may hold values from -6 to 6
- cotangent: bfloat16 [2, 2048, 768], P(None, 'dp'), may hold values from -6 to 6
- routes: int32 [2, 2, 2048, 2], P('section', None, 'dp'), may hold values from 0 to 15, all different within a row; in each aligned block of 128 rows (0 to 127, 128 to 255, ..., all dimensions but the last counted through in order) at most 32 rows name the same one
- rel_bucket: int32 [1024], replicated, may hold values from 0 to 31, as said below
- query_weight: bfloat16 [2, 768, 768], P('section', 'dp'), may hold values from -0.21875 to 0.21875
- key_weight: bfloat16 [2, 768, 768], P('section', 'dp'), may hold values from -0.21875 to 0.21875
- value_weight: bfloat16 [2, 768, 768], P('section', 'dp'), may hold values from -0.21875 to 0.21875
- output_weight: bfloat16 [2, 768, 768], P('section', 'dp'), may hold values from -0.875 to 0.875
- mixer_gain: bfloat16 [2, 768], P('section', 'dp'), may hold values from 0.5 to 1.5
- feed_gain: bfloat16 [2, 768], P('section', 'dp'), may hold values from 0.5 to 1.5
- router_weight: bfloat16 [2, 768, 16], P('section', 'dp'), may hold values from -0.15625 to 0.15625
- bias_table: bfloat16 [2, 384], P('section', 'dp'), may hold values from -3 to 3
- expert_in: bfloat16 [2, 16, 768, 3072], P('section', 'dp'), may hold values from -0.21875 to 0.21875
- expert_out: bfloat16 [2, 16, 3072, 768], P('section', 'dp'), may hold values from -0.15625 to 0.15625
Outputs:
- activations: bfloat16 [2, 2, 2048, 768], P('section', None, 'dp')
- input_grads: bfloat16 [2, 2, 2048, 768], P('section', None, 'dp')
- grad_query: float32 [2, 768, 768], P('section', 'dp')
- grad_key: float32 [2, 768, 768], P('section', 'dp')
- grad_value: float32 [2, 768, 768], P('section', 'dp')
- grad_output: float32 [2, 768, 768], P('section', 'dp')
- grad_mixer_gain: float32 [2, 768], P('section', 'dp')
- grad_feed_gain: float32 [2, 768], P('section', 'dp')
- grad_router: float32 [2, 768, 16], P('section', 'dp')
- grad_bias: float32 [2, 384], P('section', 'dp')
- grad_expert_in: float32 [2, 16, 768, 3072], P('section', 'dp')
- grad_expert_out: float32 [2, 16, 3072, 768], P('section', 'dp')
Inputs may be any that keep to these rules, and one draw needn't show every extreme that they name: `routes`: within the 128 rows of one device for one section and micro-batch, no expert is named by more than 32 rows, a bound that some block reaches; the two experts of a row differ. `rel_bucket`: buckets never fall as the distance grows; distance 0 has bucket 0 and distance 1024 - 1 has bucket 32 - 1.
All inputs are finite; a program needn't handle non-finite values.
Results may differ from a plain program's by a relative error of at most 0.023.
Values may be sent and summed in bfloat16 or wider, within the bound.
No kernel may reach another device: no remote copies, remote signals or barrier semaphores. Data moves between devices by JAX's collectives and lax.ppermute only.
A program may use at most 256 MiB of HBM per device.

v0:
```python
import jax
import jax.numpy as jnp
from jax import lax
from jax.sharding import PartitionSpec as P

HEADS = 12
HEAD_DIM = 64
BUCKETS = 32
SEQ_LEN = 1024


epsilon = 1e-06
score_scale = 0.125


def from_behind(block, axis, distance):
    devices = range(lax.axis_size(axis))
    route = [(i - distance, i) for i in devices if i - distance in devices]
    return lax.ppermute(block, axis, route)


def product(left, right):
    return jnp.dot(left, right, preferred_element_type=jnp.float32)


def first_contract(left, right):
    return lax.dot_general(
        left, right, (((0,), (0,)), ((), ())), preferred_element_type=jnp.float32
    )


def last_contract(left, right):
    return lax.dot_general(
        left, right, (((1,), (1,)), ((), ())), preferred_element_type=jnp.float32
    )


def norm_rows(values, gain):
    scale = lax.rsqrt(jnp.mean(values * values, axis=-1, keepdims=True) + epsilon)
    unit = values * scale
    return (unit * gain, unit, scale)


def norm_back(delta_out, unit, scale, gain):
    inner = delta_out * gain
    delta_in = scale * (inner - unit * jnp.mean(inner * unit, axis=-1, keepdims=True))
    return (delta_in, jnp.sum(delta_out * unit, axis=0))


def on_device(
    tokens,
    cotangent,
    routes,
    rel_bucket,
    query_weight,
    key_weight,
    value_weight,
    output_weight,
    mixer_gain,
    feed_gain,
    router_weight,
    bias_table,
    expert_in,
    expert_out,
):
    section = lax.axis_index("section")
    first = section == 0
    devices = lax.axis_size("dp")
    micro = tokens.shape[0]
    rows = tokens.shape[1]
    width = tokens.shape[2]
    span = SEQ_LEN // rows
    slots = max(2, 4 * rows // devices)
    pairs = 2 * rows
    gathered = (
        lax.all_gather(query_weight[0], "dp", axis=0, tiled=True),
        lax.all_gather(key_weight[0], "dp", axis=0, tiled=True),
        lax.all_gather(value_weight[0], "dp", axis=0, tiled=True),
        lax.all_gather(output_weight[0], "dp", axis=0, tiled=True),
        lax.all_gather(mixer_gain[0], "dp", axis=0, tiled=True),
        lax.all_gather(feed_gain[0], "dp", axis=0, tiled=True),
        lax.all_gather(router_weight[0], "dp", axis=0, tiled=True),
        lax.all_gather(bias_table[0], "dp", axis=0, tiled=True),
    )
    (
        weight_query,
        weight_key,
        weight_value,
        weight_output,
        gain_mixer,
        gain_feed,
        weight_router,
        table,
    ) = gathered
    gain_mixer = gain_mixer.astype(jnp.float32)
    gain_feed = gain_feed.astype(jnp.float32)
    experts = weight_router.shape[1]
    inner_weight = expert_in[0, 0]
    outer_weight = expert_out[0, 0]
    route_all = routes[0]
    local = lax.axis_index("dp") % span
    row_index = jnp.arange(rows, dtype=jnp.int32)
    column_index = jnp.arange(span * rows, dtype=jnp.int32)
    piece_index = column_index // rows
    distance = (piece_index * rows - column_index % rows)[None, :] + row_index[:, None]
    visible = (distance >= 0) & (piece_index[None, :] <= local)
    bucket_numbers = jnp.arange(BUCKETS, dtype=jnp.int32)
    starts = jnp.sum((rel_bucket[None, :] < bucket_numbers[:, None]).astype(jnp.int32), axis=1)
    clipped = jnp.clip(distance, 0, SEQ_LEN - 1).reshape(1, -1)
    reached = (clipped >= starts[:, None]).astype(jnp.int32)
    bucket_index = jnp.sum(reached[1:], axis=0)
    bucket_table = (bucket_numbers[:, None] == bucket_index[None, :]).astype(jnp.bfloat16)
    table_heads = jnp.transpose(table.reshape(BUCKETS, HEADS))
    bias = jnp.einsum(
        "hb,bn->hn", table_heads, bucket_table, preferred_element_type=jnp.float32
    ).reshape(HEADS, rows, span * rows)
    slot_index = jnp.arange(experts * slots, dtype=jnp.int32)
    expert_index = jnp.arange(experts, dtype=jnp.int32)

    def scores_of(query, context):
        query_heads = query.reshape(rows, HEADS, HEAD_DIM)
        key_heads = context[:, :width].reshape(-1, HEADS, HEAD_DIM)
        raw = jnp.einsum("ahd,chd->hac", query_heads, key_heads, preferred_element_type=jnp.float32)
        return jnp.where(visible[None], raw * score_scale + bias, -1e30)

    outputs = []
    caches = []
    arriving = jnp.zeros((rows, width), jnp.bfloat16)
    for step in range(micro + 1):
        if step < micro:
            fresh = tokens[step].astype(jnp.float32)
        else:
            fresh = jnp.zeros((rows, width), jnp.float32)
        inputs = jnp.where(first, fresh, arriving.astype(jnp.float32))
        route = lax.dynamic_index_in_dim(
            route_all, jnp.clip(step - section, 0, micro - 1), 0, keepdims=False
        )
        normed, unit_mixer, scale_mixer = norm_rows(inputs, gain_mixer)
        normed = normed.astype(jnp.bfloat16)
        forward_query = product(normed, weight_query).astype(jnp.bfloat16)
        own = jnp.concatenate(
            [
                product(normed, weight_key).astype(jnp.bfloat16),
                product(normed, weight_value).astype(jnp.bfloat16),
            ],
            axis=1,
        )
        pieces = [own]
        moving = own
        for offset in range(1, span):
            moving = from_behind(moving, "dp", 1)
            pieces.append(moving)
        forward_context = jnp.concatenate(pieces, axis=0)
        scores = scores_of(forward_query, forward_context)
        logsum = jnp.max(scores, axis=-1, keepdims=True)
        logsum = logsum + jnp.log(jnp.sum(jnp.exp(scores - logsum), axis=-1, keepdims=True))
        weights = jnp.exp(scores - logsum).astype(jnp.bfloat16)
        value_heads = forward_context[:, width:].reshape(-1, HEADS, HEAD_DIM)
        mixed = (
            jnp.einsum("hac,chd->ahd", weights, value_heads, preferred_element_type=jnp.float32)
            .reshape(rows, width)
            .astype(jnp.bfloat16)
        )
        hidden = inputs + product(mixed, weight_output)
        normed_feed, unit_feed, scale_feed = norm_rows(hidden, gain_feed)
        normed_feed = normed_feed.astype(jnp.bfloat16)
        chances = jax.nn.softmax(product(normed_feed, weight_router), axis=-1)
        choose = (route[:, :, None] == expert_index[None, None, :]).astype(jnp.float32)
        chosen = jnp.sum(chances[:, None, :] * choose, axis=-1)
        gate = chosen / jnp.sum(chosen, axis=1, keepdims=True)
        flat = route.reshape(-1)
        hot = (flat[:, None] == expert_index[None, :]).astype(jnp.int32)
        place = jnp.sum((jnp.cumsum(hot, axis=0) - hot) * hot, axis=1)
        placing = (slot_index[:, None] == (flat * slots + place)[None, :]).astype(jnp.bfloat16)
        outgoing = (
            product(placing, jnp.repeat(normed_feed, 2, axis=0))
            .astype(jnp.bfloat16)
            .reshape(experts, slots, width)
        )
        arrived = lax.all_to_all(outgoing, "dp", split_axis=0, concat_axis=0, tiled=True)
        sources = arrived.shape[0]
        items = arrived.shape[1]
        before = product(arrived.reshape(sources * items, width), inner_weight)
        result = product(jax.nn.gelu(before).astype(jnp.bfloat16), outer_weight).astype(
            jnp.bfloat16
        )
        result, before, arrived = (
            result.reshape(sources, items, width),
            before.reshape(sources, items, -1),
            arrived,
        )
        returned = lax.all_to_all(result, "dp", split_axis=0, concat_axis=0, tiled=True)
        back = first_contract(placing, returned.reshape(experts * slots, width)).reshape(
            rows, 2, width
        )
        output = hidden + jnp.sum(gate[:, :, None] * back, axis=1)
        cache = {
            "normed": normed,
            "unit_mixer": unit_mixer,
            "scale_mixer": scale_mixer,
            "query": forward_query,
            "context": forward_context,
            "logsum": logsum,
            "mixed": mixed,
            "normed_feed": normed_feed,
            "unit_feed": unit_feed,
            "scale_feed": scale_feed,
            "chances": chances,
            "choose": choose,
            "chosen": chosen,
            "gate": gate,
            "placing": placing,
            "back": back.astype(jnp.bfloat16),
            "before": before,
            "arrived": arrived,
        }
        output, cache = (output, cache)
        sent = output.astype(jnp.bfloat16)
        outputs.append(sent)
        caches.append(cache)
        if step < micro:
            arriving = from_behind(sent, "section", 1)
    totals = None
    expert_totals = None
    leavings = []
    returning = jnp.zeros((rows, width), jnp.bfloat16)
    for step in range(micro + 1):
        if step < micro:
            fresh = cotangent[step].astype(jnp.float32)
        else:
            fresh = jnp.zeros((rows, width), jnp.float32)
        delta_out = jnp.where(first, returning.astype(jnp.float32), fresh)
        early = caches[max(step - 1, 0)]
        late = caches[min(step + 1, micro)]
        cache = jax.tree.map(lambda left, right: jnp.where(first, left, right), early, late)
        backward_gate = cache["gate"]
        backward_chosen = cache["chosen"]
        backward_chances = cache["chances"]
        backward_placing = cache["placing"]
        delta_back = (
            (backward_gate[:, :, None] * delta_out[:, None, :])
            .astype(jnp.bfloat16)
            .reshape(pairs, width)
        )
        delta_gate = jnp.sum(delta_out[:, None, :] * cache["back"].astype(jnp.float32), axis=-1)
        backward_outgoing = (
            product(backward_placing, delta_back)
            .astype(jnp.bfloat16)
            .reshape(experts, slots, width)
        )
        arrived_delta = lax.all_to_all(
            backward_outgoing, "dp", split_axis=0, concat_axis=0, tiled=True
        ).reshape(devices * slots, width)
        backward_before = cache["before"].reshape(devices * slots, -1)
        activated, gelu_back = jax.vjp(jax.nn.gelu, backward_before)
        sum_outer = first_contract(activated.astype(jnp.bfloat16), arrived_delta)
        delta_before = gelu_back(last_contract(arrived_delta, outer_weight))[0].astype(jnp.bfloat16)
        sum_inner = first_contract(cache["arrived"].reshape(devices * slots, width), delta_before)
        leaving = (
            last_contract(delta_before, inner_weight)
            .astype(jnp.bfloat16)
            .reshape(devices, slots, width)
        )
        home = lax.all_to_all(leaving, "dp", split_axis=0, concat_axis=0, tiled=True)
        delta_feed = jnp.sum(
            first_contract(backward_placing, home.reshape(experts * slots, width)).reshape(
                rows, 2, width
            ),
            axis=1,
        )
        total = jnp.sum(backward_chosen, axis=1, keepdims=True)
        delta_chosen = delta_gate / total - jnp.sum(
            delta_gate * backward_chosen, axis=1, keepdims=True
        ) / (total * total)
        delta_chances = jnp.sum(delta_chosen[:, :, None] * cache["choose"], axis=1)
        delta_logits = (
            backward_chances
            * (delta_chances - jnp.sum(backward_chances * delta_chances, axis=-1, keepdims=True))
        ).astype(jnp.bfloat16)
        backward_normed_feed = cache["normed_feed"]
        sum_router = first_contract(backward_normed_feed, delta_logits)
        delta_feed = delta_feed + last_contract(delta_logits, weight_router)
        delta_hidden, sum_gain_feed = norm_back(
            delta_feed, cache["unit_feed"], cache["scale_feed"], gain_feed
        )
        delta_hidden = delta_hidden + delta_out
        delta_branch = delta_hidden.astype(jnp.bfloat16)
        sum_output = first_contract(cache["mixed"], delta_branch)
        delta_mixed = last_contract(delta_branch, weight_output).astype(jnp.bfloat16)
        backward_query = cache["query"]
        backward_context = cache["context"]
        weights_full = jnp.exp(scores_of(backward_query, backward_context) - cache["logsum"])
        backward_query_heads = backward_query.reshape(rows, HEADS, HEAD_DIM)
        backward_key_heads = backward_context[:, :width].reshape(-1, HEADS, HEAD_DIM)
        backward_value_heads = backward_context[:, width:].reshape(-1, HEADS, HEAD_DIM)
        delta_heads = delta_mixed.reshape(rows, HEADS, HEAD_DIM)
        delta_weights = jnp.einsum(
            "ahd,chd->hac", delta_heads, backward_value_heads, preferred_element_type=jnp.float32
        )
        delta_scores = (
            weights_full
            * (delta_weights - jnp.sum(weights_full * delta_weights, axis=-1, keepdims=True))
        ).astype(jnp.bfloat16)
        delta_query = (
            (
                jnp.einsum(
                    "hac,chd->ahd",
                    delta_scores,
                    backward_key_heads,
                    preferred_element_type=jnp.float32,
                )
                * score_scale
            )
            .reshape(rows, width)
            .astype(jnp.bfloat16)
        )
        delta_keys = (
            jnp.einsum(
                "hac,ahd->chd",
                delta_scores,
                backward_query_heads,
                preferred_element_type=jnp.float32,
            )
            * score_scale
        )
        delta_values = jnp.einsum(
            "hac,ahd->chd",
            weights_full.astype(jnp.bfloat16),
            delta_heads,
            preferred_element_type=jnp.float32,
        )
        delta_context = jnp.concatenate(
            [delta_keys.reshape(-1, width), delta_values.reshape(-1, width)], axis=1
        )
        carry = delta_context[(span - 1) * rows :]
        for backward_offset in range(span - 2, -1, -1):
            carry = (
                from_behind(carry.astype(jnp.bfloat16), "dp", -1).astype(carry.dtype)
                + delta_context[backward_offset * rows : (backward_offset + 1) * rows]
            )
        delta_own = carry.astype(jnp.bfloat16)
        backward_normed = cache["normed"]
        sum_query = first_contract(backward_normed, delta_query)
        sum_key = first_contract(backward_normed, delta_own[:, :width])
        sum_value = first_contract(backward_normed, delta_own[:, width:])
        delta_normed = (
            last_contract(delta_query, weight_query)
            + last_contract(delta_own[:, :width], weight_key)
            + last_contract(delta_own[:, width:], weight_value)
        )
        delta_inputs, sum_gain_mixer = norm_back(
            delta_normed, cache["unit_mixer"], cache["scale_mixer"], gain_mixer
        )
        delta_inputs = delta_inputs + delta_hidden
        bucket_sums = jnp.einsum(
            "hn,bn->hb",
            delta_scores.reshape(HEADS, -1),
            bucket_table,
            preferred_element_type=jnp.float32,
        )
        sum_table = jnp.transpose(bucket_sums).reshape(-1)
        partials = (
            sum_query,
            sum_key,
            sum_value,
            sum_output,
            sum_gain_mixer,
            sum_gain_feed,
            sum_router,
            sum_table,
        )
        delta_in, partials, expert_parts = (delta_inputs, partials, (sum_inner, sum_outer))
        leaving = delta_in.astype(jnp.bfloat16)
        leavings.append(leaving)
        if step < micro:
            returning = from_behind(leaving, "section", -1)
        expert_totals = (
            expert_parts
            if expert_totals is None
            else jax.tree.map(jnp.add, expert_totals, expert_parts)
        )
        shares = (
            lax.psum_scatter(partials[0], "dp", scatter_dimension=0, tiled=True),
            lax.psum_scatter(partials[1], "dp", scatter_dimension=0, tiled=True),
            lax.psum_scatter(partials[2], "dp", scatter_dimension=0, tiled=True),
            lax.psum_scatter(partials[3], "dp", scatter_dimension=0, tiled=True),
            lax.psum_scatter(partials[4], "dp", scatter_dimension=0, tiled=True),
            lax.psum_scatter(partials[5], "dp", scatter_dimension=0, tiled=True),
            lax.psum_scatter(partials[6], "dp", scatter_dimension=0, tiled=True),
            lax.psum_scatter(partials[7], "dp", scatter_dimension=0, tiled=True),
        )
        totals = shares if totals is None else jax.tree.map(jnp.add, totals, shares)
    activations = jnp.stack(
        [jnp.where(first, outputs[index], outputs[index + 1]) for index in range(micro)]
    )[None]
    input_grads = jnp.stack(
        [jnp.where(first, leavings[index + 1], leavings[index]) for index in range(micro)]
    )[None]
    return (
        activations,
        input_grads,
        totals[0][None],
        totals[1][None],
        totals[2][None],
        totals[3][None],
        totals[4][None],
        totals[5][None],
        totals[6][None],
        totals[7][None],
        expert_totals[0][None, None],
        expert_totals[1][None, None],
    )


def solution(mesh):
    in_specs = (
        P(None, "dp", None),
        P(None, "dp", None),
        P("section", None, "dp", None),
        P(),
        P("section", "dp", None),
        P("section", "dp", None),
        P("section", "dp", None),
        P("section", "dp", None),
        P("section", "dp"),
        P("section", "dp"),
        P("section", "dp", None),
        P("section", "dp"),
        P("section", "dp", None, None),
        P("section", "dp", None, None),
    )
    out_specs = (
        P("section", None, "dp", None),
        P("section", None, "dp", None),
        P("section", "dp", None),
        P("section", "dp", None),
        P("section", "dp", None),
        P("section", "dp", None),
        P("section", "dp"),
        P("section", "dp"),
        P("section", "dp", None),
        P("section", "dp"),
        P("section", "dp", None, None),
        P("section", "dp", None, None),
    )
    return jax.shard_map(
        on_device, mesh=mesh, in_specs=in_specs, out_specs=out_specs, check_vma=False
    )
```

profile of v0, /device:TPU:0, one launch (start us, length us, event | category | flops | bytes accessed | tf_op | source)
XLA Modules:
  0.0 1720.7 jit_solution(9842363417564597472)
XLA Ops:
  16.9 44.9 %all-reduce.7 = (bf16[768]{0:T(1024)(128)(2,1)S(1)}, bf16[384]{0:T(512)(128)(2,1)S(1)}, bf16[768]{0:T(1024)(128)(2,1)}) all-reduce(bf16[768]{0:T(1024)(128)(2,1)S(1)} %dynamic-update-slice, bf16[384]{0:T(512)(128)(2,1)S(1)} %dynamic-update-slice.1, bf16[768]{0:T(1024)(128)(2,1)S(1)} %dynamic-update-slice.2), channel_id=2, replica_groups=mesh['section'=2,'dp'=16] {'dp'}, use_global_device_ids=true, to_apply=%add | all-reduce | flops 1920 | bytes 7680
  72.3 55.3 %all-gather.13.cloned.1.call-done = bf16[1,768,768]{2,1,0:T(8,128)(2,1)} async-done(((bf16[1,48,768]{2,1,0:T(8,128)(2,1)}), bf16[1,768,768]{2,1,0:T(8,128)(2,1)}) %all-gather.13.cloned.1.call-update) | async-done | bytes 1179664 | tf_op jit(solution)/shard_map/all_gather | solution.py:77
  158.7 11.7 copy.302
  252.5 24.2 %all_to_all.60 = bf16[16,32,768]{2,1,0:T(8,128)(2,1)S(1)} all-to-all(bf16[16,32,768]{2,1,0:T(8,128)(2,1)S(1)} %bitcast.623), channel_id=1, replica_groups=mesh['section'=2,'dp'=16] {'dp'}, dimensions={0} | all-to-all | bytes 1572864 | tf_op jit(solution)/shard_map/all_to_all | solution.py:180
  290.7 47.7 %all-gather.7 = bf16[1,768,16]{2,0,1:T(2,128)(2,1)S(1)} all-gather(bf16[1,48,16]{2,0,1:T(2,128)(2,1)S(1)} %copy.242), channel_id=9, replica_groups=mesh['section'=2,'dp'=16] {'dp'}, dimensions={1}, use_global_device_ids=true | all-gather | bytes 26112 | tf_op jit(solution)/shard_map/all_gather | solution.py:82
  455.0 11.0 all-to-all-start.2
  692.3 10.2 collective-permute-done.23
  703.9 12.5 collective-permute-done.24
  736.9 19.4 %all-to-all-start.4 = ((bf16[16,32,768]{2,1,0:T(8,128)(2,1)}), bf16[16,32,768]{2,1,0:T(8,128)(2,1)}, u32[]{:S(2)}, u32[]{:S(2)}) async-start(bf16[16,32,768]{2,1,0:T(8,128)(2,1)} %bitcast.622), calls=%async_computation.4 | async-start | bytes 1572864 | tf_op jit(solution)/shard_map/all_to_all | solution.py:180
  764.7 10.0 collective-permute-done.27
  795.0 13.9 all-to-all-start.5
  828.7 23.1 %all_to_all.61 = bf16[16,32,768]{2,1,0:T(8,128)(2,1)S(1)} all-to-all(bf16[16,32,768]{2,1,0:T(8,128)(2,1)S(1)} %bitcast.620), channel_id=1, replica_groups=mesh['section'=2,'dp'=16] {'dp'}, dimensions={0} | all-to-all | bytes 1572864 | tf_op jit(solution)/shard_map/all_to_all | solution.py:251
  938.2 10.4 collective-permute-done.34
  950.0 12.2 collective-permute-done.35
  963.9 13.5 collective-permute-done.36
  1055.1 11.7 all-to-all-done.11
  1141.4 10.3 fusion.80
  1196.2 10.2 fusion.81
  1217.4 12.0 add_bitcast_fusion.1
  1231.5 16.4 add_bitcast_fusion
  1263.9 80.6 %all-reduce.6 = (f32[768]{0:T(1024)S(1)}, f32[768]{0:T(1024)S(1)}, f32[384]{0:T(512)S(1)}) all-reduce(f32[768]{0:T(1024)S(1)} %add_add_fusion.5, f32[768]{0:T(1024)S(1)} %copy-done.226, f32[384]{0:T(512)S(1)} %copy-done.240), channel_id=30, replica_groups=mesh['section'=2,'dp'=16] {'dp'}, use_global_device_ids=true, to_apply=%region_78.79.clone | all-reduce | flops 1920 | bytes 15360
  1348.3 100.3 %reduce-scatter.14.cloned.1.call-done = f32[48,768]{1,0:T(8,128)} async-done(((f32[768,768]{1,0:T(8,128)}), f32[48,768]{1,0:T(8,128)}) %reduce-scatter.14.cloned.1.call-update) | async-done | bytes 147472 | tf_op jit(solution)/shard_map/reduce_scatter | solution.py:386
  1448.6 133.0 %reduce-scatter.10.cloned.1.call-done = f32[48,768]{1,0:T(8,128)} async-done(((f32[768,768]{1,0:T(8,128)}), f32[48,768]{1,0:T(8,128)}) %reduce-scatter.10.cloned.1.call-update) | async-done | bytes 147472 | tf_op jit(solution)/shard_map/reduce_scatter | solution.py:384
  1581.6 132.3 %reduce-scatter.12.cloned.1.call-done = f32[48,768]{1,0:T(8,128)} async-done(((f32[768,768]{1,0:T(8,128)}), f32[48,768]{1,0:T(8,128)}) %reduce-scatter.12.cloned.1.call-update) | async-done | bytes 147472 | tf_op jit(solution)/shard_map/reduce_scatter | solution.py:385
  (1021 shorter events, 873.1 us)
Async XLA Ops:
  7.2 62.7 %all-gather.15.cloned.1.call-start = ((), (), s32[]{:S(2)}) async-start(), calls=%async_computation.18 | async-start | bytes 1253376 | tf_op jit(solution)/shard_map/all_gather | solution.py:78
  7.9 119.7 %all-gather.13.cloned.1.call-start = ((), (), s32[]{:S(2)}) async-start(), calls=%async_computation.17 | async-start | bytes 1253376 | tf_op jit(solution)/shard_map/all_gather | solution.py:77
  8.7 182.0 %all-gather.17.cloned.1.call-start = ((), (), s32[]{:S(2)}) async-start(), calls=%async_computation.19 | async-start | bytes 1253376 | tf_op jit(solution)/shard_map/all_gather | solution.py:76
  9.4 239.9 %all-gather.19.cloned.1.call-start = ((), (), s32[]{:S(2)}) async-start(), calls=%async_computation.20 | async-start | bytes 1253376 | tf_op jit(solution)/shard_map/all_gather | solution.py:79
  152.1 22.5 %collective-permute-start.2 = (bf16[128,1536]{1,0:T(8,128)(2,1)}, bf16[128,1536]{1,0:T(8,128)(2,1)}, u32[]{:S(2)}, u32[]{:S(2)}) collective-permute-start(bf16[128,1536]{1,0:T(8,128)(2,1)} %collective-permute-done.1), channel_id=1, source_target_pairs={{0,1},{1,2},{2,3},{3,4},{4,5},{5,6},{6,7},{7,8},{8,9},{9,10},{10,1... | collective-permute-start | bytes 1179656 | tf_op jit(solution)/shard_map/ppermute | solution.py:19
  174.6 20.1 %collective-permute-start.3 = (bf16[128,1536]{1,0:T(8,128)(2,1)}, bf16[128,1536]{1,0:T(8,128)(2,1)}, u32[]{:S(2)}, u32[]{:S(2)}) collective-permute-start(bf16[128,1536]{1,0:T(8,128)(2,1)} %collective-permute-done.2), channel_id=1, source_target_pairs={{0,1},{1,2},{2,3},{3,4},{4,5},{5,6},{6,7},{7,8},{8,9},{9,10},{10,1... | collective-permute-start | bytes 1179656 | tf_op jit(solution)/shard_map/ppermute | solution.py:19
  286.8 53.6 %all-to-all-start.1 = ((bf16[16,32,768]{2,1,0:T(8,128)(2,1)}), bf16[16,32,768]{2,1,0:T(8,128)(2,1)S(1)}, u32[]{:S(2)}, u32[]{:S(2)}) async-start(bf16[16,32,768]{2,1,0:T(8,128)(2,1)} %bitcast.22), calls=%async_computation.1 | async-start | bytes 1572864 | tf_op jit(solution)/shard_map/all_to_all | solution.py:192
  455.0 34.6 %all-to-all-start.2 = ((bf16[16,32,768]{2,1,0:T(8,128)(2,1)}), bf16[16,32,768]{2,1,0:T(8,128)(2,1)}, u32[]{:S(2)}, u32[]{:S(2)}) async-start(bf16[16,32,768]{2,1,0:T(8,128)(2,1)} %bitcast.621), calls=%async_computation.2 | async-start | bytes 1572864 | tf_op jit(solution)/shard_map/all_to_all | solution.py:180
  489.6 21.4 %all-to-all-start.6 = ((bf16[16,32,768]{2,1,0:T(8,128)(2,1)}), bf16[16,32,768]{2,1,0:T(8,128)(2,1)}, u32[]{:S(2)}, u32[]{:S(2)}) async-start(bf16[16,32,768]{2,1,0:T(8,128)(2,1)} %bitcast.619), calls=%async_computation.6 | async-start | bytes 1572864 | tf_op jit(solution)/shard_map/all_to_all | solution.py:251
  510.9 20.4 %all-to-all-start.3 = ((bf16[16,32,768]{2,1,0:T(8,128)(2,1)}), bf16[16,32,768]{2,1,0:T(8,128)(2,1)}, u32[]{:S(2)}, u32[]{:S(2)}) async-start(bf16[16,32,768]{2,1,0:T(8,128)(2,1)} %bitcast.658), calls=%async_computation.3 | async-start | bytes 1572864 | tf_op jit(solution)/shard_map/all_to_all | solution.py:192
  544.4 56.3 %all-to-all-start.7 = ((bf16[16,32,768]{2,1,0:T(8,128)(2,1)}), bf16[16,32,768]{2,1,0:T(8,128)(2,1)}, u32[]{:S(2)}, u32[]{:S(2)}) async-start(bf16[16,32,768]{2,1,0:T(8,128)(2,1)} %bitcast.654), calls=%async_computation.7 | async-start | bytes 1572864 | tf_op jit(solution)/shard_map/all_to_all | solution.py:264
  734.4 25.7 %collective-permute-start.26 = (bf16[128,1536]{0,1:T(8,128)(2,1)}, bf16[128,1536]{0,1:T(8,128)(2,1)}, u32[]{:S(2)}, u32[]{:S(2)}) collective-permute-start(bf16[128,1536]{0,1:T(8,128)(2,1)} %fusion.281), channel_id=1, source_target_pairs={{1,0},{2,1},{3,2},{4,3},{5,4},{6,5},{7,6},{8,7},{9,8},{10,9},{11,1... | collective-permute-start | bytes 1179656 | tf_op jit(solution)/shard_map/ppermute | solution.py:19
  736.9 39.2 %all-to-all-start.4 = ((bf16[16,32,768]{2,1,0:T(8,128)(2,1)}), bf16[16,32,768]{2,1,0:T(8,128)(2,1)}, u32[]{:S(2)}, u32[]{:S(2)}) async-start(bf16[16,32,768]{2,1,0:T(8,128)(2,1)} %bitcast.622), calls=%async_computation.4 | async-start | bytes 1572864 | tf_op jit(solution)/shard_map/all_to_all | solution.py:180
  786.8 22.2 %collective-permute-start.29 = (bf16[128,1536]{0,1:T(8,128)(2,1)}, bf16[128,1536]{0,1:T(8,128)(2,1)}, u32[]{:S(2)}, u32[]{:S(2)}) collective-permute-start(bf16[128,1536]{0,1:T(8,128)(2,1)} %fusion.270), channel_id=1, source_target_pairs={{1,0},{2,1},{3,2},{4,3},{5,4},{6,5},{7,6},{8,7},{9,8},{10,9},{11,1... | collective-permute-start | bytes 1179656 | tf_op jit(solution)/shard_map/ppermute | solution.py:19
  795.0 27.2 %all-to-all-start.5 = ((bf16[16,32,768]{2,1,0:T(8,128)(2,1)}), bf16[16,32,768]{2,1,0:T(8,128)(2,1)}, u32[]{:S(2)}, u32[]{:S(2)}) async-start(bf16[16,32,768]{2,1,0:T(8,128)(2,1)} %bitcast.656), calls=%async_computation.5 | async-start | bytes 1572864 | tf_op jit(solution)/shard_map/all_to_all | solution.py:192
  865.3 22.3 %all-to-all-start.9 = ((bf16[16,32,768]{2,1,0:T(8,128)(2,1)}), bf16[16,32,768]{2,1,0:T(8,128)(2,1)}, u32[]{:S(2)}, u32[]{:S(2)}) async-start(bf16[16,32,768]{2,1,0:T(8,128)(2,1)} %bitcast.74), calls=%async_computation.9 | async-start | bytes 1572864 | tf_op jit(solution)/shard_map/all_to_all | solution.py:264
  1003.8 26.5 %all-to-all-start.10 = ((bf16[16,32,768]{2,1,0:T(8,128)(2,1)}), bf16[16,32,768]{2,1,0:T(8,128)(2,1)}, u32[]{:S(2)}, u32[]{:S(2)}) async-start(bf16[16,32,768]{2,1,0:T(8,128)(2,1)} %bitcast.618), calls=%async_computation.10 | async-start | bytes 1572864 | tf_op jit(solution)/shard_map/all_to_all | solution.py:251
  1042.9 23.9 %all-to-all-start.11 = ((bf16[16,32,768]{2,1,0:T(8,128)(2,1)}), bf16[16,32,768]{2,1,0:T(8,128)(2,1)}, u32[]{:S(2)}, u32[]{:S(2)}) async-start(bf16[16,32,768]{2,1,0:T(8,128)(2,1)} %bitcast.655), calls=%async_computation.11 | async-start | bytes 1572864 | tf_op jit(solution)/shard_map/all_to_all | solution.py:264
  1048.1 168.0 %reduce-scatter.16.cloned.1.call-start = ((), (), s32[]{:S(2)}) async-start(), calls=%async_computation.25 | async-start | bytes 417792
  1055.0 293.3 %reduce-scatter.8.cloned.1.call-start = ((), (), s32[]{:S(2)}) async-start(), calls=%async_computation.21 | async-start | bytes 2506752 | tf_op jit(solution)/shard_map/reduce_scatter | solution.py:383
  1086.9 361.7 %reduce-scatter.14.cloned.1.call-start = ((), (), s32[]{:S(2)}) async-start(), calls=%async_computation.24 | async-start | bytes 2506752 | tf_op jit(solution)/shard_map/reduce_scatter | solution.py:386
  1130.7 450.9 %reduce-scatter.10.cloned.1.call-start = ((), (), s32[]{:S(2)}) async-start(), calls=%async_computation.22 | async-start | bytes 2506752 | tf_op jit(solution)/shard_map/reduce_scatter | solution.py:384
  1139.6 19.7 %collective-permute-start.43 = (bf16[128,1536]{0,1:T(8,128)(2,1)S(1)}, bf16[128,1536]{0,1:T(8,128)(2,1)S(1)}, u32[]{:S(2)}, u32[]{:S(2)}) collective-permute-start(bf16[128,1536]{0,1:T(8,128)(2,1)S(1)} %fusion.244), channel_id=1, source_target_pairs={{1,0},{2,1},{3,2},{4,3},{5,4},{6,5},{7,6},{8,7},{9,8},{10,9},{11,1... | collective-permute-start | bytes 1179656 | tf_op jit(solution)/shard_map/ppermute | solution.py:19
  1185.6 528.3 %reduce-scatter.12.cloned.1.call-start = ((), (), s32[]{:S(2)}) async-start(), calls=%async_computation.23 | async-start | bytes 2506752 | tf_op jit(solution)/shard_map/reduce_scatter | solution.py:385
  (316 other events, 4557.4 us)
Sparse Core Ops, SparseCore 0:
  10.8 59.0 all-gather.14
  72.7 54.9 all-gather.12
  130.5 60.1 all-gather.16
  193.3 55.9 all-gather.18
  1055.2 128.3 reduce-scatter.15
  1189.7 126.7 reduce-scatter.7
  1321.9 126.6 reduce-scatter.13
  1454.9 126.6 reduce-scatter.9
  1587.1 126.7 reduce-scatter.11
where the time goes:
time: 1730 us; the launch traced here: 1720 us
  waiting for transfers between devices  718 us (42%)
  matrix products  288 us (17%)
  blocking collectives  221 us (13%)
  starting transfers between devices  220 us (13%)
  local copies, waits for them, and re-layouts  165 us (10%)
  other arithmetic  87.9 us (5%)
  between operations  20.8 us (1%)
    ppermute x46, waiting for transfers between devices, from_behind(): return lax.ppermute(block, axis, route)  242 us
    ppermute x46, starting transfers between devices, from_behind(): return lax.ppermute(block, axis, route)  137 us
    reduce_scatter x1, waiting for transfers between devices, on_device(): lax.psum_scatter(partials[1], 'dp', scatter_dimension=0, tiled=True)  133 us
    reduce_scatter x1, waiting for transfers between devices, on_device(): lax.psum_scatter(partials[2], 'dp', scatter_dimension=0, tiled=True)  132 us
    unnamed x2, blocking collectives  126 us
    reduce_scatter x1, waiting for transfers between devices, on_device(): lax.psum_scatter(partials[3], 'dp', scatter_dimension=0, tiled=True)  100 us
    dot_general x27, matrix products, first_contract(): lax.dot_general(left, right, (((0,), (0,)), ((), ())), preferred_element_...  98.8 us
    unnamed x586, local copies, waits for them, and re-layouts  69.7 us
  transfers between devices with their start and end apart: 65, of which 51 were waited for; matrix products, arithmetic and copies ran while one was open for 21% of the time, Pallas kernels for 0%

commit v1 on v0

v1 whole, which is shorter than its diff:
```python
import functools

import jax
import jax.numpy as jnp
from jax import lax
from jax.experimental import pallas as pl
from jax.experimental.pallas import tpu as pltpu
from jax.sharding import PartitionSpec as P

HEADS = 12
HEAD_DIM = 64
BUCKETS = 32
SEQ_LEN = 1024

PAIR = 2 * HEAD_DIM
TILE = 256
BLOCKS = SEQ_LEN // TILE
REACH = SEQ_LEN + TILE

epsilon = 1e-06
score_scale = 0.125
bf16 = jnp.bfloat16
f32 = jnp.float32


def product(left, right):
    return jnp.dot(left, right, preferred_element_type=f32)


def first_contract(left, right):
    return lax.dot_general(left, right, (((0,), (0,)), ((), ())), preferred_element_type=f32)


def last_contract(left, right):
    return lax.dot_general(left, right, (((1,), (1,)), ((), ())), preferred_element_type=f32)


def norm_parts(values):
    scale = lax.rsqrt(jnp.mean(values * values, axis=-1, keepdims=True) + epsilon)
    return (values * scale, scale)


def norm_back(delta_out, unit, scale, gain):
    inner = delta_out * gain
    delta_in = scale * (inner - unit * jnp.mean(inner * unit, axis=-1, keepdims=True))
    return (delta_in, jnp.sum(delta_out * unit, axis=0))


def bias_tile(bias_ref, head, step):
    start = SEQ_LEN - TILE - TILE * step
    line = bias_ref[head : head + 1, start : start + 2 * TILE]
    spread = jnp.broadcast_to(line, (TILE, 2 * TILE))
    return pltpu.roll(spread, TILE + 1, 1, stride=1, stride_axis=0)[:, :TILE]


def block_scores(qkv_ref, tiles, head, block):
    low = HEAD_DIM * head
    seen = TILE * (block + 1)
    query = qkv_ref[TILE * block : seen, low : low + HEAD_DIM]
    key = qkv_ref[0:seen, PAIR + low : PAIR + low + HEAD_DIM]
    raw = last_contract(query, key) * score_scale
    bias = jnp.concatenate([tiles[head, block - j] for j in range(block + 1)], axis=1)
    rows = lax.broadcasted_iota(jnp.int32, (TILE, seen), 0) + TILE * block
    columns = lax.broadcasted_iota(jnp.int32, (TILE, seen), 1)
    scores = jnp.where(columns <= rows, raw + bias, -1e30)
    top = jnp.max(scores, axis=-1, keepdims=True)
    weights = jnp.exp(scores - top)
    weights = weights * (1.0 / jnp.sum(weights, axis=-1, keepdims=True))
    return query, key, weights


def attend_kernel(qkv_ref, bias_ref, out_ref, tiles):
    for head in range(2):
        low = HEAD_DIM * head
        for step in range(BLOCKS):
            tiles[head, step] = bias_tile(bias_ref, head, step)
        for block in range(BLOCKS):
            seen = TILE * (block + 1)
            _, _, weights = block_scores(qkv_ref, tiles, head, block)
            value = qkv_ref[0:seen, 2 * PAIR + low : 2 * PAIR + low + HEAD_DIM]
            out_ref[TILE * block : seen, low : low + HEAD_DIM] = product(
                weights.astype(bf16), value
            ).astype(bf16)


def attend_back_kernel(qkv_ref, bias_ref, delta_ref, grad_ref, line_ref, tiles, sums, keys, values):
    line_ref[...] = jnp.zeros_like(line_ref)
    for head in range(2):
        low = HEAD_DIM * head
        for step in range(BLOCKS):
            tiles[head, step] = bias_tile(bias_ref, head, step)
            sums[step] = jnp.zeros((TILE, TILE), f32)
        keys[...] = jnp.zeros_like(keys)
        values[...] = jnp.zeros_like(values)
        for block in range(BLOCKS):
            seen = TILE * (block + 1)
            query, key, weights = block_scores(qkv_ref, tiles, head, block)
            value = qkv_ref[0:seen, 2 * PAIR + low : 2 * PAIR + low + HEAD_DIM]
            delta = delta_ref[TILE * block : seen, low : low + HEAD_DIM]
            delta_weights = last_contract(delta, value)
            inner = jnp.sum(weights * delta_weights, axis=-1, keepdims=True)
            delta_scores = (weights * (delta_weights - inner)).astype(bf16)
            grad_ref[TILE * block : seen, low : low + HEAD_DIM] = (
                product(delta_scores, key) * score_scale
            ).astype(bf16)
            keys[0:seen, :] += first_contract(delta_scores, query)
            values[0:seen, :] += first_contract(weights.astype(bf16), delta)
            for j in range(block + 1):
                sums[block - j] += delta_scores[:, TILE * j : TILE * (j + 1)].astype(f32)
        grad_ref[:, PAIR + low : PAIR + low + HEAD_DIM] = (keys[...] * score_scale).astype(bf16)
        grad_ref[:, 2 * PAIR + low : 2 * PAIR + low + HEAD_DIM] = values[...].astype(bf16)
        for step in range(BLOCKS):
            start = SEQ_LEN - TILE - TILE * step
            eight = jnp.zeros((8, 2 * TILE), f32)
            for group in range(TILE // 8):
                part = sums[step, 8 * group : 8 * group + 8, :]
                part = jnp.concatenate([part, jnp.zeros_like(part)], axis=1)
                eight = eight + pltpu.roll(part, TILE - 1 - 8 * group, 1)
            line = eight[0:1]
            for row in range(1, 8):
                line = line + pltpu.roll(eight, 2 * TILE - row, 1)[row : row + 1]
            line_ref[head : head + 1, start : start + 2 * TILE] += line


def attend(qkv, bias):
    return pl.pallas_call(
        attend_kernel,
        out_shape=jax.ShapeDtypeStruct((SEQ_LEN, PAIR), bf16),
        in_specs=[pl.BlockSpec(memory_space=pltpu.VMEM)] * 2,
        out_specs=pl.BlockSpec(memory_space=pltpu.VMEM),
        scratch_shapes=[pltpu.VMEM((2, BLOCKS, TILE, TILE), f32)],
        compiler_params=pltpu.CompilerParams(vmem_limit_bytes=40 * 1024 * 1024),
        cost_estimate=pl.CostEstimate(
            flops=2 * SEQ_LEN * SEQ_LEN * PAIR * 2,
            bytes_accessed=SEQ_LEN * PAIR * 8,
            transcendentals=SEQ_LEN * SEQ_LEN,
        ),
    )(qkv, bias)


def attend_back(qkv, bias, delta):
    return pl.pallas_call(
        attend_back_kernel,
        out_shape=(
            jax.ShapeDtypeStruct((SEQ_LEN, 3 * PAIR), bf16),
            jax.ShapeDtypeStruct((8, REACH), f32),
        ),
        in_specs=[pl.BlockSpec(memory_space=pltpu.VMEM)] * 3,
        out_specs=(pl.BlockSpec(memory_space=pltpu.VMEM),) * 2,
        scratch_shapes=[
            pltpu.VMEM((2, BLOCKS, TILE, TILE), f32),
            pltpu.VMEM((BLOCKS, TILE, TILE), f32),
            pltpu.VMEM((SEQ_LEN, HEAD_DIM), f32),
            pltpu.VMEM((SEQ_LEN, HEAD_DIM), f32),
        ],
        compiler_params=pltpu.CompilerParams(vmem_limit_bytes=40 * 1024 * 1024),
        cost_estimate=pl.CostEstimate(
            flops=5 * SEQ_LEN * SEQ_LEN * PAIR * 2,
            bytes_accessed=SEQ_LEN * PAIR * 16,
            transcendentals=SEQ_LEN * SEQ_LEN,
        ),
    )(qkv, bias, delta)


def on_device(
    tokens,
    cotangent,
    routes,
    rel_bucket,
    query_weight,
    key_weight,
    value_weight,
    output_weight,
    mixer_gain,
    feed_gain,
    router_weight,
    bias_table,
    expert_in,
    expert_out,
):
    core = lax.axis_index("section")
    place_dp = lax.axis_index("dp")
    devices = lax.axis_size("dp")
    micro = tokens.shape[0]
    rows = tokens.shape[1]
    width = tokens.shape[2]
    span = SEQ_LEN // rows
    seat = place_dp % span
    slots = max(2, 4 * rows // devices)
    experts = devices
    share = width // devices
    table_share = BUCKETS * HEADS // devices
    used = HEADS // 2
    lanes = 3 * PAIR
    circles = [list(range(i, i + span)) for i in range(0, devices, span)]
    zero = core == 0

    def swap(value):
        return lax.ppermute(value, "section", [(0, 1), (1, 0)])

    def to_sections(own):
        other = swap(own)
        return jnp.where(zero, own, other), jnp.where(zero, other, own)

    def own_of(values):
        return jnp.where(zero, values[0], values[1]), jnp.where(zero, values[1], values[0])

    def exchange(value):
        return lax.all_to_all(value, "dp", 0, 0, tiled=True)

    def exchange_near(value):
        return lax.all_to_all(value, "dp", 0, 0, tiled=True, axis_index_groups=circles)

    def gather_near(value):
        spread = jnp.broadcast_to(value[None], (span,) + value.shape)
        return exchange_near(spread).reshape(SEQ_LEN, -1)

    def by_pairs(weight):
        padded = jnp.pad(weight, ((0, 0), (0, span * PAIR - width)))
        return jnp.transpose(padded.reshape(share, span, PAIR), (1, 0, 2))

    small = jnp.concatenate(
        [mixer_gain[0], feed_gain[0], router_weight[0].reshape(-1), bias_table[0]]
    )
    small_rows = 8 * (-(-small.shape[0] // (8 * lanes)))
    small_pad = small_rows * lanes - small.shape[0]
    small = jnp.pad(small, (0, small_pad)).reshape(1, small_rows, lanes)
    pairs_weight = jnp.concatenate(
        [by_pairs(query_weight[0]), by_pairs(key_weight[0]), by_pairs(value_weight[0])], axis=2
    )
    pairs_weight = jnp.concatenate(
        [pairs_weight, jnp.broadcast_to(small, (span,) + small.shape[1:])], axis=1
    )
    pairs_weight = jnp.concatenate([pairs_weight] * (devices // span), axis=0)
    front = to_sections(exchange(pairs_weight))
    context = jnp.where(zero, tokens[0], tokens[1])
    target = jnp.where(zero, cotangent[0], cotangent[1])
    full_first = gather_near(context)
    output_full = to_sections(
        exchange(jnp.broadcast_to(output_weight, (devices, share, width))).reshape(width, width)
    )
    inner_full = to_sections(expert_in[0, 0])
    outer_full = to_sections(expert_out[0, 0])
    route_mine, route_theirs = own_of((routes[0, 0], routes[0, 1]))
    route_other = swap(route_theirs)
    route_full = (
        jnp.where(zero, route_mine, route_other),
        jnp.where(zero, route_other, route_mine),
    )

    bucket_numbers = jnp.arange(BUCKETS, dtype=jnp.int32)
    reverse = jnp.concatenate([rel_bucket[::-1], jnp.full((TILE,), -1, jnp.int32)])
    bucket_hot = (bucket_numbers[:, None] == reverse[None, :]).astype(f32)
    slot_index = jnp.arange(experts * slots, dtype=jnp.int32)
    expert_index = jnp.arange(experts, dtype=jnp.int32)

    sections = []
    for section in range(2):
        block = front[section]
        attention = block[:, :share].reshape(width, lanes)
        flat_small = block[:, share:].reshape(devices, small_rows * lanes)
        cut = [share, 2 * share, (2 + experts) * share, (2 + experts) * share + table_share]
        gain_mixer = flat_small[:, : cut[0]].reshape(width).astype(f32)
        gain_feed = flat_small[:, cut[0] : cut[1]].reshape(width).astype(f32)
        router = flat_small[:, cut[1] : cut[2]].reshape(width, experts)
        table = flat_small[:, cut[2] : cut[3]].reshape(BUCKETS, HEADS).astype(f32)
        table = jnp.pad(table, ((0, 0), (0, 2 * span - HEADS)))
        mine = lax.dynamic_slice_in_dim(table, 2 * seat, 2, axis=1)
        bias = lax.dot_general(
            mine, bucket_hot, (((0,), (0,)), ((), ())), precision=lax.Precision.HIGHEST
        )
        bias = jnp.pad(bias, ((0, 6), (0, 0)))
        route = route_full[section]
        flat = route.reshape(-1)
        hot = (flat[:, None] == expert_index[None, :]).astype(jnp.int32)
        place = jnp.sum((jnp.cumsum(hot, axis=0) - hot) * hot, axis=1)
        spot = (flat * slots + place).reshape(rows, 2)
        placings = [
            (slot_index[:, None] == spot[:, c][None, :]).astype(bf16) for c in range(2)
        ]
        choose = (route[:, :, None] == expert_index[None, None, :]).astype(f32)
        sections.append(
            {
                "attention": attention,
                "gain_mixer": gain_mixer,
                "gain_feed": gain_feed,
                "router": router,
                "bias": bias,
                "placings": placings,
                "placing": placings[0] + placings[1],
                "choose": choose,
                "output": output_full[section],
                "inner": inner_full[section],
                "outer": outer_full[section],
            }
        )

    def dispatch(p, values):
        out = product(p["placing"], values).astype(bf16)
        return exchange(out.reshape(experts, slots, width)).reshape(experts * slots, width)

    def collect(p, returned):
        return [first_contract(p["placings"][c], returned) for c in range(2)]

    def mixer(p, full, own):
        unit, _ = norm_parts(full.astype(f32))
        normed = (unit * p["gain_mixer"]).astype(bf16)
        qkv = product(normed, p["attention"]).astype(bf16)
        heads = attend(qkv, p["bias"])
        mixed = exchange_near(heads.reshape(span, rows, PAIR))
        mixed = jnp.transpose(mixed[:used], (1, 0, 2)).reshape(rows, width)
        hidden = own.astype(f32) + product(mixed, p["output"])
        unit_feed, scale_feed = norm_parts(hidden)
        normed_feed = (unit_feed * p["gain_feed"]).astype(bf16)
        chances = jax.nn.softmax(product(normed_feed, p["router"]), axis=-1)
        chosen = jnp.sum(chances[:, None, :] * p["choose"], axis=-1)
        gate = chosen / jnp.sum(chosen, axis=1, keepdims=True)
        return {
            "own": own,
            "normed": normed,
            "qkv": qkv,
            "mixed": mixed,
            "hidden": hidden,
            "unit_feed": unit_feed,
            "scale_feed": scale_feed,
            "normed_feed": normed_feed,
            "chances": chances,
            "chosen": chosen,
            "gate": gate,
        }

    def finish(cache, back):
        gate = cache["gate"]
        return (cache["hidden"] + (gate[:, 0:1] * back[0] + gate[:, 1:2] * back[1])).astype(bf16)

    def mixer_back(p, cache, delta_feed, delta_gate, delta_out):
        chosen, chances = cache["chosen"], cache["chances"]
        total = jnp.sum(chosen, axis=1, keepdims=True)
        delta_chosen = delta_gate / total - jnp.sum(
            delta_gate * chosen, axis=1, keepdims=True
        ) / (total * total)
        delta_chances = jnp.sum(delta_chosen[:, :, None] * p["choose"], axis=1)
        delta_logits = (
            chances * (delta_chances - jnp.sum(chances * delta_chances, axis=-1, keepdims=True))
        ).astype(bf16)
        sum_router = first_contract(cache["normed_feed"], delta_logits)
        delta_feed = delta_feed + last_contract(delta_logits, p["router"])
        delta_hidden, sum_feed = norm_back(
            delta_feed, cache["unit_feed"], cache["scale_feed"], p["gain_feed"]
        )
        delta_hidden = delta_hidden + delta_out
        delta_branch = delta_hidden.astype(bf16)
        sum_output = first_contract(cache["mixed"], delta_branch)
        delta_mixed = last_contract(delta_branch, p["output"]).astype(bf16)
        delta_mixed = jnp.pad(delta_mixed, ((0, 0), (0, span * PAIR - width)))
        delta_mixed = jnp.transpose(delta_mixed.reshape(rows, span, PAIR), (1, 0, 2))
        delta_heads = exchange_near(delta_mixed).reshape(SEQ_LEN, PAIR)
        delta_qkv, line = attend_back(cache["qkv"], p["bias"], delta_heads)
        parts = last_contract(delta_qkv, p["attention"]).astype(bf16)
        parts = exchange_near(parts.reshape(span, rows, width))
        delta_normed = jnp.sum(parts.astype(f32), axis=0)
        unit, scale = norm_parts(cache["own"].astype(f32))
        delta_in, sum_mixer = norm_back(delta_normed, unit, scale, p["gain_mixer"])
        delta_in = (delta_in + delta_hidden).astype(bf16)
        sum_attention = first_contract(cache["normed"], delta_qkv)
        sum_table = lax.dot_general(
            bucket_hot, line[:2], (((1,), (1,)), ((), ())), precision=lax.Precision.HIGHEST
        )
        sum_table = lax.dynamic_update_slice_in_dim(
            jnp.zeros((BUCKETS, 2 * span), f32), sum_table, 2 * seat, axis=1
        )[:, :HEADS]
        blocks = jnp.concatenate(
            [
                sum_mixer.reshape(devices, share),
                sum_feed.reshape(devices, share),
                sum_router.reshape(devices, share * experts),
                sum_table.reshape(devices, table_share),
                jnp.zeros((devices, small_pad), f32),
            ],
            axis=1,
        ).reshape(devices, small_rows, lanes)
        sums = jnp.concatenate([sum_attention.reshape(devices, share, lanes), blocks], axis=1)
        return delta_in, sums.astype(bf16), sum_output.astype(bf16)

    p0, p1 = sections
    cache0 = mixer(p0, full_first, context)
    arrived0 = dispatch(p0, cache0["normed_feed"])
    before0 = product(arrived0, p0["inner"])
    activated0 = jax.nn.gelu(before0).astype(bf16)
    result0 = product(activated0, p0["outer"]).astype(bf16)
    back0 = collect(p0, exchange(result0.reshape(experts, slots, width)).reshape(-1, width))
    output0 = finish(cache0, back0)

    arrived_target = dispatch(p1, target)
    delta_act = last_contract(arrived_target, p1["outer"])
    cache1 = mixer(p1, gather_near(output0), output0)
    arrived1 = dispatch(p1, cache1["normed_feed"])
    gate_slots = sum(
        jnp.sum(p1["placings"][c].astype(f32) * cache1["gate"][:, c][None, :], axis=1)
        for c in range(2)
    )
    gate_slots = exchange(gate_slots.reshape(experts, slots)).reshape(-1, 1)
    before1 = product(arrived1, p1["inner"])
    activated1, gelu_back1 = jax.vjp(jax.nn.gelu, before1)
    activated1 = activated1.astype(bf16)
    delta_before1 = gelu_back1(delta_act)[0]
    leaving1 = last_contract(delta_before1.astype(bf16), p1["inner"]).astype(bf16)
    result1 = product(activated1, p1["outer"]).astype(bf16)
    inner_gate = jnp.sum(arrived_target.astype(f32) * result1.astype(f32), axis=-1)
    home1 = collect(p1, exchange(leaving1.reshape(experts, slots, width)).reshape(-1, width))
    inner_gate = exchange(inner_gate.reshape(experts, slots)).reshape(-1)
    delta_gate1 = jnp.stack(
        [
            jnp.sum(p1["placings"][c].astype(f32) * inner_gate[:, None], axis=0)
            for c in range(2)
        ],
        axis=1,
    )
    gate1 = cache1["gate"]
    delta_feed1 = gate1[:, 0:1] * home1[0] + gate1[:, 1:2] * home1[1]
    delta_in1, sums1, sum_output1 = mixer_back(
        p1, cache1, delta_feed1, delta_gate1, target.astype(f32)
    )
    back1 = collect(p1, exchange(result1.reshape(experts, slots, width)).reshape(-1, width))
    output1 = finish(cache1, back1)
    operands1 = (
        activated1,
        (gate_slots * arrived_target.astype(f32)).astype(bf16),
        arrived1,
        (gate_slots * delta_before1).astype(bf16),
    )

    delta_out0 = delta_in1.astype(f32)
    gate0 = cache0["gate"]
    delta_back = [(gate0[:, c : c + 1] * delta_out0).astype(bf16) for c in range(2)]
    outgoing = product(p0["placings"][0], delta_back[0]) + product(p0["placings"][1], delta_back[1])
    arrived_delta = exchange(
        outgoing.astype(bf16).reshape(experts, slots, width)
    ).reshape(-1, width)
    _, gelu_back0 = jax.vjp(jax.nn.gelu, before0)
    delta_before0 = gelu_back0(last_contract(arrived_delta, p0["outer"]))[0].astype(bf16)
    leaving0 = last_contract(delta_before0, p0["inner"]).astype(bf16)
    home0 = collect(p0, exchange(leaving0.reshape(experts, slots, width)).reshape(-1, width))
    delta_gate0 = jnp.stack([jnp.sum(delta_out0 * back0[c], axis=-1) for c in range(2)], axis=1)
    delta_in0, sums0, sum_output0 = mixer_back(
        p0, cache0, home0[0] + home0[1], delta_gate0, delta_out0
    )
    operands0 = (activated0, arrived_delta, arrived0, delta_before0)

    totals = []
    joined = []
    for left, right in zip(operands0, operands1):
        mine, theirs = own_of((left, right))
        joined.append(jnp.concatenate([mine, swap(theirs)], axis=0))
    grad_outer = first_contract(joined[0], joined[1])
    grad_inner = first_contract(joined[2], joined[3])

    def reduced(first, second):
        mine, theirs = own_of((first, second))
        both = (mine.astype(f32) + swap(theirs).astype(f32)).astype(bf16)
        return exchange(both).astype(f32)

    sums = reduced(sums0, sums1)
    attention_sums = sums[:, :share].reshape(devices // span, span, share, 3, PAIR)
    attention_sums = jnp.sum(attention_sums, axis=0)[:used]
    attention_sums = jnp.transpose(attention_sums, (2, 1, 0, 3)).reshape(3, share, width)
    small_sums = jnp.sum(sums[:, share:], axis=0).reshape(-1)
    totals = [small_sums[:share], small_sums[share : 2 * share]]
    totals.append(small_sums[2 * share : (2 + experts) * share].reshape(share, experts))
    end = (2 + experts) * share
    totals.append(small_sums[end : end + table_share])
    output_sums = reduced(
        sum_output0.reshape(devices, share, width), sum_output1.reshape(devices, share, width)
    )
    output_sums = jnp.sum(output_sums, axis=0)

    def by_micro(first, second):
        mine, theirs = own_of((first, second))
        other = swap(theirs)
        return jnp.stack([jnp.where(zero, mine, other), jnp.where(zero, other, mine)])[None]

    return (
        by_micro(output0, output1),
        by_micro(delta_in0, delta_in1),
        attention_sums[0][None],
        attention_sums[1][None],
        attention_sums[2][None],
        output_sums[None],
        totals[0][None],
        totals[1][None],
        totals[2][None],
        totals[3][None],
        grad_inner[None, None],
        grad_outer[None, None],
    )


def solution(mesh):
    in_specs = (
        P(None, "dp", None),
        P(None, "dp", None),
        P("section", None, "dp", None),
        P(),
        P("section", "dp", None),
        P("section", "dp", None),
        P("section", "dp", None),
        P("section", "dp", None),
        P("section", "dp"),
        P("section", "dp"),
        P("section", "dp", None),
        P("section", "dp"),
        P("section", "dp", None, None),
        P("section", "dp", None, None),
    )
    out_specs = (
        P("section", None, "dp", None),
        P("section", None, "dp", None),
        P("section", "dp", None),
        P("section", "dp", None),
        P("section", "dp", None),
        P("section", "dp", None),
        P("section", "dp"),
        P("section", "dp"),
        P("section", "dp", None),
        P("section", "dp"),
        P("section", "dp", None, None),
        P("section", "dp", None, None),
    )
    return jax.shard_map(
        on_device, mesh=mesh, in_specs=in_specs, out_specs=out_specs, check_vma=False
    )
```

time: 1730 us -> 612 us (0.35)
  waiting for transfers between devices: 718 us -> 217 us
  blocking collectives: 221 us -> 37.5 us
  matrix products: 288 us -> 132 us
  local copies, waits for them, and re-layouts: 165 us -> 43.5 us
  starting transfers between devices: 220 us -> 102 us
  other arithmetic: 87.9 us -> 38.9 us
  Pallas kernels: 0 us -> 28 us
  between operations: 20.8 us -> 2.99 us
    reduce_scatter x4 -> x0, waiting for transfers between devices: 366 us -> none  [the longest x1 133 us: on_device(): lax.psum_scatter(partials[1], 'dp', scatter_dimension=0, tiled=True)]
    ppermute x46 -> x13, waiting for transfers between devices: 242 us -> 6.04 us  [swap(): return lax.ppermute(value, 'section', [(0, 1), (1, 0)])]
    all_to_all x10 -> x20, waiting for transfers between devices: 35.2 us -> 211 us  [the longest x13 154 us: exchange(): return lax.all_to_all(value, 'dp', 0, 0, tiled=True)]
    ppermute x46 -> x13, starting transfers between devices: 137 us -> 2.95 us  [swap(): return lax.ppermute(value, 'section', [(0, 1), (1, 0)])]
    unnamed x2 -> x0, blocking collectives: 126 us -> none
    dot_general x52 -> x19, matrix products: 132 us -> 50.5 us  [the longest x15 49.5 us: product(): return jnp.dot(left, right, preferred_element_type=f32)]
    all_gather x4 -> x0, waiting for transfers between devices: 72.7 us -> none  [the longest x1 55.3 us: on_device(): lax.all_gather(key_weight[0], 'dp', axis=0, tiled=True)]
    dot_general x27 -> x16, matrix products: 98.8 us -> 37.2 us  [first_contract(): lax.dot_general(left, right, (((0,), (0,)), ((), ())), preferred_element_...]
  transfers between devices with their start and end apart: 65 -> 33, of which waited for: 51 -> 21; matrix products, arithmetic and copies ran while one was open for 21% -> 23% of each run, Pallas kernels for 0% -> 2%
where the time goes in v1:
time: 612 us; the launch traced here: 602 us
  waiting for transfers between devices  217 us (35%)
  matrix products  132 us (22%)
  starting transfers between devices  102 us (17%)
  local copies, waits for them, and re-layouts  43.5 us (7%)
  other arithmetic  38.9 us (6%)
  blocking collectives  37.5 us (6%)
  Pallas kernels  28 us (5%)
    all_to_all x13, waiting for transfers between devices, exchange(): return lax.all_to_all(value, 'dp', 0, 0, tiled=True)  154 us
    all_to_all x13, starting transfers between devices, exchange(): return lax.all_to_all(value, 'dp', 0, 0, tiled=True)  67.8 us
    all_to_all x7, waiting for transfers between devices, exchange_near(): lax.all_to_all(value, 'dp', 0, 0, tiled=True, axis_index_groups=circles)  57.1 us
    dot_general x15, matrix products, product(): return jnp.dot(left, right, preferred_element_type=f32)  49.5 us
    dot_general x10, matrix products, last_contract(): lax.dot_general(left, right, (((1,), (1,)), ((), ())), preferred_element_...  44.3 us
    dot_general x16, matrix products, first_contract(): lax.dot_general(left, right, (((0,), (0,)), ((), ())), preferred_element_...  37.2 us
    all_to_all x7, starting transfers between devices, exchange_near(): lax.all_to_all(value, 'dp', 0, 0, tiled=True, axis_index_groups=circles)  31.6 us
    all_to_all x1, blocking collectives, exchange(): return lax.all_to_all(value, 'dp', 0, 0, tiled=True)  27.5 us
  transfers between devices with their start and end apart: 33, of which 21 were waited for; matrix products, arithmetic and copies ran while one was open for 23% of the time, Pallas kernels for 2%

profile of v1, /device:TPU:0, one launch (start us, length us, event | category | flops | bytes accessed | tf_op | source)
XLA Modules:
  0.0 602.2 jit_solution(15519238377448368501)
XLA Ops:
  4.3 27.5 %all_to_all.115 = bf16[16,56,384]{2,1,0:T(8,128)(2,1)S(1)} all-to-all(bf16[16,56,384]{2,1,0:T(8,128)(2,1)S(1)} %maximum_maximum_fusion), channel_id=1, replica_groups=mesh['section'=2,'dp'=16] {'dp'}, dimensions={0} | all-to-all | bytes 1376256 | tf_op jit(solution)/shard_map/all_to_all | solution.py:209
  38.3 25.0 %all-to-all-done.3 = bf16[16,48,768]{2,1,0:T(8,128)(2,1)S(1)} async-done(((bf16[16,48,768]{2,1,0:T(8,128)(2,1)}), bf16[16,48,768]{2,1,0:T(8,128)(2,1)S(1)}, u32[]{:S(2)}, u32[]{:S(2)}) %all-to-all-start.3) | async-done | bytes 1179680 | tf_op jit(solution)/shard_map/all_to_all | solution.py:209
  123.8 18.5 %all-to-all-done.4 = bf16[16,32,768]{2,1,0:T(8,128)(2,1)S(1)} async-done(((bf16[16,32,768]{2,1,0:T(8,128)(2,1)}), bf16[16,32,768]{2,1,0:T(8,128)(2,1)S(1)}, u32[]{:S(2)}, u32[]{:S(2)}) %all-to-all-start.4) | async-done | bytes 786464 | tf_op jit(solution)/shard_map/all_to_all | solution.py:209
  147.3 9.4 %fusion.50 = bf16[512,768]{1,0:T(8,128)(2,1)} fusion(bf16[3072,768]{1,0:T(8,128)(2,1)} %collective-permute-done.4, pred[]{:T(512)S(6)} %eq.154, bf16[1,1,3072,768]{3,2,1,0:T(8,128)(2,1)} %param.27, f32[512,3072]{1,0:T(8,128)S(1)} %fusion.35), kind=kOutput, calls=%fused_computation.80 | convolution fusion | flops 2432827392 | bytes 16515073 | tf_op jit(solution)/shard_map/dot_general | solution.py:27
  163.5 18.2 %all-to-all-done.5 = bf16[16,32,768]{2,1,0:T(8,128)(2,1)S(1)} async-done(((bf16[16,32,768]{2,1,0:T(8,128)(2,1)}), bf16[16,32,768]{2,1,0:T(8,128)(2,1)S(1)}, u32[]{:S(2)}, u32[]{:S(2)}) %all-to-all-start.5) | async-done | bytes 786464 | tf_op jit(solution)/shard_map/all_to_all | solution.py:209
  191.1 19.7 %all-to-all-done.6 = bf16[8,128,768]{1,2,0:T(8,128)(2,1)} async-done(((bf16[8,128,768]{1,2,0:T(8,128)(2,1)}), bf16[8,128,768]{1,2,0:T(8,128)(2,1)}, u32[]{:S(2)}, u32[]{:S(2)}) %all-to-all-start.6) | async-done | bytes 1572896 | tf_op jit(solution)/shard_map/all_to_all | solution.py:212
  243.0 14.5 %all-to-all-done.8 = bf16[16,32,768]{2,1,0:T(8,128)(2,1)S(1)} async-done(((bf16[16,32,768]{2,1,0:T(8,128)(2,1)}), bf16[16,32,768]{2,1,0:T(8,128)(2,1)S(1)}, u32[]{:S(2)}, u32[]{:S(2)}) %all-to-all-start.8) | async-done | bytes 786464 | tf_op jit(solution)/shard_map/all_to_all | solution.py:209
  263.5 12.3 %broadcast_select_fusion.5 = (bf16[512,3072]{1,0:T(8,128)(2,1)}, bf16[512,3072]{1,0:T(8,128)(2,1)}, f32[512,3072]{1,0:T(8,128)}) fusion(pred[]{:T(512)S(6)} %eq.154, f32[512,3072]{1,0:T(8,128)} %copy-done.93, bf16[512,768]{1,0:T(8,128)(2,1)} %bitcast.310, bf16[768,3072]{1,0:T(8,128)(2,1)} %collective-permute-done.3, bf16[1,1,768,3072]{3,2,1,0:T(8,128)(2,1)} %param.26), kind=kOutput, calls=%fused_computation.49 | convolution fusion | flops 2449735680 | bytes 29097984 | tf_op jit(solution)/shard_map/dot_general | solution.py:27
  282.1 10.5 %fusion.41 = (f32[512]{0:T(512)S(1)}, bf16[512,768]{1,0:T(8,128)(2,1)}) fusion(bf16[16,32,768]{2,1,0:T(8,128)(2,1)S(1)} %all-to-all-done.10, bf16[3072,768]{1,0:T(8,128)(2,1)} %collective-permute-done.4, pred[]{:T(512)S(6)} %eq.154, bf16[1,1,3072,768]{3,2,1,0:T(8,128)(2,1)} %param.27, f32[512,3072]{1,0:T(8,128)} %get-tuple-element.174), kind=kOutput, calls=%fused_computation.66 | convolution fusion | flops 2434399744 | bytes 17303552 | tf_op jit(solution)/shard_map/dot_general | solution.py:27
  298.2 9.4 %fusion.12 = f32[512,3072]{1,0:T(8,128)S(1)} fusion(f32[512,3072]{1,0:T(8,128)} %get-tuple-element.174, bf16[512,768]{1,0:T(8,128)(2,1)S(1)} %bitcast.307, bf16[3072,768]{1,0:T(8,128)(2,1)} %collective-permute-done.4, pred[]{:T(512)S(6)} %eq.154, bf16[1,1,3072,768]{3,2,1,0:T(8,128)(2,1)} %param.27), kind=kOutput, calls=%fused_computation.16 | convolution fusion | flops 2448162816 | bytes 22806528 | tf_op jit(solution)/shard_map/dot_general | solution.py:35
  310.4 7.3 %fusion.52 = bf16[512,768]{1,0:T(8,128)(2,1)} fusion(bf16[768,3072]{1,0:T(8,128)(2,1)} %collective-permute-done.3, pred[]{:T(512)S(6)} %eq.154, f32[512,3072]{1,0:T(8,128)S(1)} %fusion.12, bf16[1,1,768,3072]{3,2,1,0:T(8,128)(2,1)} %param.26), kind=kOutput, calls=%fused_computation.82 | convolution fusion | flops 2420244480 | bytes 16515073 | tf_op jit(solution)/shard_map/dot_general | solution.py:35
  317.7 7.3 %all-to-all-start.11 = ((bf16[16,32,768]{2,1,0:T(8,128)(2,1)}), bf16[16,32,768]{2,1,0:T(8,128)(2,1)S(1)}, u32[]{:S(2)}, u32[]{:S(2)}) async-start(bf16[16,32,768]{2,1,0:T(8,128)(2,1)} %bitcast.326), calls=%async_computation.11 | async-start | bytes 1572864 | tf_op jit(solution)/shard_map/all_to_all | solution.py:209
  326.7 13.4 %all-to-all-done.11 = bf16[16,32,768]{2,1,0:T(8,128)(2,1)S(1)} async-done(((bf16[16,32,768]{2,1,0:T(8,128)(2,1)}), bf16[16,32,768]{2,1,0:T(8,128)(2,1)S(1)}, u32[]{:S(2)}, u32[]{:S(2)}) %all-to-all-start.11) | async-done | bytes 786464 | tf_op jit(solution)/shard_map/all_to_all | solution.py:209
  343.4 10.0 %all_to_all.116 = bf16[8,128,128]{2,1,0:T(8,128)(2,1)S(1)} all-to-all(bf16[8,128,128]{2,1,0:T(8,128)(2,1)S(1)} %bitcast_bitcast_fusion.1), channel_id=1, replica_groups={{0,1,2,3,4,5,6,7},{8,9,10,11,12,13,14,15},{16,17,18,19,20,21,22,23},{24..., dimensions={0} | all-to-all | bytes 524288 | tf_op jit(solution)/shard_map/all_to_all | solution.py:212
  353.3 9.1 %shard_map.231 = (bf16[1024,384]{1,0:T(8,128)(2,1)S(1)}, f32[8,1280]{1,0:T(8,128)S(1)}) custom-call(bf16[1024,384]{1,0:T(8,128)(2,1)S(1)} %convolution_convert_fusion.4.qkv_ref, f32[8,1280]{1,0:T(8,128)S(1)} %pad.51.bias_ref, bf16[1024,128]{1,0:T(8,128)(2,1)S(1)} %bitcast.292), custom_call_target="tpu_custom_call" | custom-call | flops 1342177280 | bytes 2097152 | tf_op jit(solution)/shard_map/pallas_call | solution.py:142
  369.9 15.9 %all-to-all-done.14 = bf16[8,128,768]{2,1,0:T(8,128)(2,1)} async-done(((bf16[8,128,768]{2,1,0:T(8,128)(2,1)}), bf16[8,128,768]{2,1,0:T(8,128)(2,1)}, u32[]{:S(2)}, u32[]{:S(2)}) %all-to-all-start.14) | async-done | bytes 1572896 | tf_op jit(solution)/shard_map/all_to_all | solution.py:212
  412.8 8.8 %all-to-all-done.15 = bf16[16,32,768]{2,1,0:T(8,128)(2,1)} async-done(((bf16[16,32,768]{2,1,0:T(8,128)(2,1)}), bf16[16,32,768]{2,1,0:T(8,128)(2,1)}, u32[]{:S(2)}, u32[]{:S(2)}) %all-to-all-start.15) | async-done | bytes 786464 | tf_op jit(solution)/shard_map/all_to_all | solution.py:209
  421.6 12.4 %broadcast_select_fusion.7 = (bf16[512,3072]{1,0:T(8,128)(2,1)}, bf16[512,3072]{1,0:T(8,128)(2,1)}, bf16[512,3072]{1,0:T(8,128)(2,1)S(1)}) fusion(pred[]{:T(512)S(6)} %eq.154, f32[512,3072]{1,0:T(8,128)} %copy-done.94, f32[512]{0:T(512)S(1)} %mul.655, f32[512,3072]{1,0:T(8,128)} %copy-done.93, bf16[512,768]{1,0:T(8,128)(2,1)} %bitcast.54, ...), kind=kOutput, calls=%fused_computation.51 | convolution fusion | flops 2456027136 | bytes 32245760 | tf_op jit(solution)/shard_map/dot_general | solution.py:35
  449.1 15.9 %all-to-all-done.16 = bf16[16,32,768]{2,1,0:T(8,128)(2,1)} async-done(((bf16[16,32,768]{2,1,0:T(8,128)(2,1)}), bf16[16,32,768]{2,1,0:T(8,128)(2,1)}, u32[]{:S(2)}, u32[]{:S(2)}) %all-to-all-start.16) | async-done | bytes 786464 | tf_op jit(solution)/shard_map/all_to_all | solution.py:209
  476.8 14.0 %all-to-all-done.9 = bf16[16,32,768]{2,1,0:T(8,128)(2,1)} async-done(((bf16[16,32,768]{2,1,0:T(8,128)(2,1)}), bf16[16,32,768]{2,1,0:T(8,128)(2,1)}, u32[]{:S(2)}, u32[]{:S(2)}) %all-to-all-start.9) | async-done | bytes 786464 | tf_op jit(solution)/shard_map/all_to_all | solution.py:209
  501.6 9.2 %shard_map.232 = (bf16[1024,384]{1,0:T(8,128)(2,1)S(1)}, f32[8,1280]{1,0:T(8,128)S(1)}) custom-call(bf16[1024,384]{1,0:T(8,128)(2,1)S(1)} %convolution_convert_fusion.5.qkv_ref, f32[8,1280]{1,0:T(8,128)S(1)} %pad.48.bias_ref, bf16[1024,128]{1,0:T(8,128)(2,1)S(1)} %bitcast.291), custom_call_target="tpu_custom_call" | custom-call | flops 1342177280 | bytes 2097152 | tf_op jit(solution)/shard_map/pallas_call | solution.py:142
  547.1 10.0 %fusion.21 = f32[1,1,3072,768]{3,2,1,0:T(8,128)} fusion(bf16[512,3072]{1,0:T(8,128)(2,1)} %collective-permute-done.11, bf16[512,3072]{1,0:T(8,128)(2,1)} %get-tuple-element.121, bf16[512,768]{1,0:T(8,128)(2,1)} %collective-permute-done.12, bf16[512,768]{1,0:T(8,128)(2,1)} %get-tuple-element.127), kind=kOutput, calls=%fused_computation.28 | convolution fusion | flops 4847566848 | bytes 17301504 | tf_op jit(solution)/shard_map/dot_general | solution.py:31
  559.4 11.3 %all-to-all-done.20 = bf16[16,48,768]{2,1,0:T(8,128)(2,1)S(1)} async-done(((bf16[16,48,768]{2,1,0:T(8,128)(2,1)}), bf16[16,48,768]{2,1,0:T(8,128)(2,1)S(1)}, u32[]{:S(2)}, u32[]{:S(2)}) %all-to-all-start.20) | async-done | bytes 1179680 | tf_op jit(solution)/shard_map/all_to_all | solution.py:209
  578.0 9.8 %fusion.24 = f32[1,1,768,3072]{3,2,1,0:T(8,128)} fusion(bf16[512,3072]{1,0:T(8,128)(2,1)} %collective-permute-done.10, bf16[512,3072]{1,0:T(8,128)(2,1)} %get-tuple-element.123, bf16[512,768]{1,0:T(8,128)(2,1)} %collective-permute-done.9, bf16[512,768]{1,0:T(8,128)(2,1)} %get-tuple-element.129), kind=kOutput, calls=%fused_computation.29 | convolution fusion | flops 4847566848 | bytes 17301504 | tf_op jit(solution)/shard_map/dot_general | solution.py:31
  (466 shorter events, 279.6 us)
Async XLA Ops:
  33.8 29.6 %all-to-all-start.3 = ((bf16[16,48,768]{2,1,0:T(8,128)(2,1)}), bf16[16,48,768]{2,1,0:T(8,128)(2,1)S(1)}, u32[]{:S(2)}, u32[]{:S(2)}) async-start(bf16[16,48,768]{2,1,0:T(8,128)(2,1)} %broadcast_in_dim.32), calls=%async_computation.3 | async-start | bytes 2359296 | tf_op jit(solution)/shard_map/all_to_all | solution.py:209
  64.9 25.6 %all-to-all-start = ((bf16[8,128,768]{1,2,0:T(8,128)(2,1)}), bf16[8,128,768]{1,2,0:T(8,128)(2,1)}, u32[]{:S(2)}, u32[]{:S(2)}) async-start(bf16[8,128,768]{1,2,0:T(8,128)(2,1)} %broadcast_in_dim.28), calls=%async_computation | async-start | bytes 3145728 | tf_op jit(solution)/shard_map/all_to_all | solution.py:212
  70.7 76.6 %collective-permute-start.4 = (bf16[3072,768]{1,0:T(8,128)(2,1)}, bf16[3072,768]{1,0:T(8,128)(2,1)}, u32[]{:S(2)}, u32[]{:S(2)}) collective-permute-start(bf16[3072,768]{1,0:T(8,128)(2,1)} %bitcast.360), channel_id=1, source_target_pairs={{0,16},{16,0},{1,17},{17,1},{2,18},{18,2},{3,19},{19,3},{4,20},{20... | collective-permute-start | bytes 14155784 | tf_op jit(solution)/shard_map/ppermute | solution.py:199
  71.2 52.6 %collective-permute-start.3 = (bf16[768,3072]{1,0:T(8,128)(2,1)}, bf16[768,3072]{1,0:T(8,128)(2,1)}, u32[]{:S(2)}, u32[]{:S(2)}) collective-permute-start(bf16[768,3072]{1,0:T(8,128)(2,1)} %bitcast.361), channel_id=1, source_target_pairs={{0,16},{16,0},{1,17},{17,1},{2,18},{18,2},{3,19},{19,3},{4,20},{20... | collective-permute-start | bytes 14155784 | tf_op jit(solution)/shard_map/ppermute | solution.py:199
  83.5 32.2 %collective-permute-start.1 = (bf16[768,768]{1,0:T(8,128)(2,1)S(1)}, bf16[768,768]{1,0:T(8,128)(2,1)S(1)}, u32[]{:S(2)}, u32[]{:S(2)}) collective-permute-start(bf16[768,768]{1,0:T(8,128)(2,1)S(1)} %bitcast.295), channel_id=1, source_target_pairs={{0,16},{16,0},{1,17},{17,1},{2,18},{18,2},{3,19},{19,3},{4,20},{20... | collective-permute-start | bytes 3538952 | tf_op jit(solution)/shard_map/ppermute | solution.py:199
  119.6 22.7 %all-to-all-start.4 = ((bf16[16,32,768]{2,1,0:T(8,128)(2,1)}), bf16[16,32,768]{2,1,0:T(8,128)(2,1)S(1)}, u32[]{:S(2)}, u32[]{:S(2)}) async-start(bf16[16,32,768]{2,1,0:T(8,128)(2,1)} %bitcast.21), calls=%async_computation.4 | async-start | bytes 1572864 | tf_op jit(solution)/shard_map/all_to_all | solution.py:209
  156.6 25.1 %all-to-all-start.5 = ((bf16[16,32,768]{2,1,0:T(8,128)(2,1)}), bf16[16,32,768]{2,1,0:T(8,128)(2,1)S(1)}, u32[]{:S(2)}, u32[]{:S(2)}) async-start(bf16[16,32,768]{2,1,0:T(8,128)(2,1)} %bitcast.25), calls=%async_computation.5 | async-start | bytes 1572864 | tf_op jit(solution)/shard_map/all_to_all | solution.py:209
  185.2 25.6 %all-to-all-start.6 = ((bf16[8,128,768]{1,2,0:T(8,128)(2,1)}), bf16[8,128,768]{1,2,0:T(8,128)(2,1)}, u32[]{:S(2)}, u32[]{:S(2)}) async-start(bf16[8,128,768]{1,2,0:T(8,128)(2,1)} %broadcast_in_dim.33), calls=%async_computation.6 | async-start | bytes 3145728 | tf_op jit(solution)/shard_map/all_to_all | solution.py:212
  234.6 22.9 %all-to-all-start.8 = ((bf16[16,32,768]{2,1,0:T(8,128)(2,1)}), bf16[16,32,768]{2,1,0:T(8,128)(2,1)S(1)}, u32[]{:S(2)}, u32[]{:S(2)}) async-start(bf16[16,32,768]{2,1,0:T(8,128)(2,1)} %bitcast.35), calls=%async_computation.8 | async-start | bytes 1572864 | tf_op jit(solution)/shard_map/all_to_all | solution.py:209
  258.4 23.7 %all-to-all-start.10 = ((bf16[16,32,768]{2,1,0:T(8,128)(2,1)}), bf16[16,32,768]{2,1,0:T(8,128)(2,1)S(1)}, u32[]{:S(2)}, u32[]{:S(2)}) async-start(bf16[16,32,768]{2,1,0:T(8,128)(2,1)} %bitcast.44), calls=%async_computation.10 | async-start | bytes 1572864 | tf_op jit(solution)/shard_map/all_to_all | solution.py:209
  293.3 24.4 %all-to-all-start.12 = ((f32[16,1,32]{2,1,0:T(1,128)}), f32[16,1,32]{2,1,0:T(1,128)S(1)}, u32[]{:S(2)}, u32[]{:S(2)}) async-start(f32[16,1,32]{2,1,0:T(1,128)} %all_to_all.82), calls=%async_computation.12 | async-start | bytes 16384 | tf_op jit(solution)/shard_map/all_to_all | solution.py:209
  317.7 22.4 %all-to-all-start.11 = ((bf16[16,32,768]{2,1,0:T(8,128)(2,1)}), bf16[16,32,768]{2,1,0:T(8,128)(2,1)S(1)}, u32[]{:S(2)}, u32[]{:S(2)}) async-start(bf16[16,32,768]{2,1,0:T(8,128)(2,1)} %bitcast.326), calls=%async_computation.11 | async-start | bytes 1572864 | tf_op jit(solution)/shard_map/all_to_all | solution.py:209
  364.7 21.1 %all-to-all-start.14 = ((bf16[8,128,768]{2,1,0:T(8,128)(2,1)}), bf16[8,128,768]{2,1,0:T(8,128)(2,1)}, u32[]{:S(2)}, u32[]{:S(2)}) async-start(bf16[8,128,768]{2,1,0:T(8,128)(2,1)} %bitcast.318), calls=%async_computation.14 | async-start | bytes 3145728 | tf_op jit(solution)/shard_map/all_to_all | solution.py:212
  397.8 23.8 %all-to-all-start.15 = ((bf16[16,32,768]{2,1,0:T(8,128)(2,1)}), bf16[16,32,768]{2,1,0:T(8,128)(2,1)}, u32[]{:S(2)}, u32[]{:S(2)}) async-start(bf16[16,32,768]{2,1,0:T(8,128)(2,1)} %bitcast.308), calls=%async_computation.15 | async-start | bytes 1572864 | tf_op jit(solution)/shard_map/all_to_all | solution.py:209
  440.1 24.9 %all-to-all-start.16 = ((bf16[16,32,768]{2,1,0:T(8,128)(2,1)}), bf16[16,32,768]{2,1,0:T(8,128)(2,1)}, u32[]{:S(2)}, u32[]{:S(2)}) async-start(bf16[16,32,768]{2,1,0:T(8,128)(2,1)} %bitcast.327), calls=%async_computation.16 | async-start | bytes 1572864 | tf_op jit(solution)/shard_map/all_to_all | solution.py:209
  447.3 130.8 %collective-permute-start.9 = (bf16[512,768]{1,0:T(8,128)(2,1)}, bf16[512,768]{1,0:T(8,128)(2,1)}, u32[]{:S(2)}, u32[]{:S(2)}) collective-permute-start(bf16[512,768]{1,0:T(8,128)(2,1)} %get-tuple-element.130), channel_id=1, source_target_pairs={{0,16},{16,0},{1,17},{17,1},{2,18},{18,2},{3,19},{19,3},{4,20},{20... | collective-permute-start | bytes 2359304 | tf_op jit(solution)/shard_map/ppermute | solution.py:199
  447.7 99.4 %collective-permute-start.11 = (bf16[512,3072]{1,0:T(8,128)(2,1)}, bf16[512,3072]{1,0:T(8,128)(2,1)}, u32[]{:S(2)}, u32[]{:S(2)}) collective-permute-start(bf16[512,3072]{1,0:T(8,128)(2,1)} %get-tuple-element.122), channel_id=1, source_target_pairs={{0,16},{16,0},{1,17},{17,1},{2,18},{18,2},{3,19},{19,3},{4,20},{20... | collective-permute-start | bytes 9437192 | tf_op jit(solution)/shard_map/ppermute | solution.py:199
  465.1 25.8 %all-to-all-start.9 = ((bf16[16,32,768]{2,1,0:T(8,128)(2,1)}), bf16[16,32,768]{2,1,0:T(8,128)(2,1)}, u32[]{:S(2)}, u32[]{:S(2)}) async-start(bf16[16,32,768]{2,1,0:T(8,128)(2,1)} %bitcast.325), calls=%async_computation.9 | async-start | bytes 1572864 | tf_op jit(solution)/shard_map/all_to_all | solution.py:209
  498.7 19.9 %collective-permute-start.5 = (bf16[128,768]{1,0:T(8,128)(2,1)}, bf16[128,768]{1,0:T(8,128)(2,1)}, u32[]{:S(2)}, u32[]{:S(2)}) collective-permute-start(bf16[128,768]{1,0:T(8,128)(2,1)} %get-tuple-element.167), channel_id=1, source_target_pairs={{0,16},{16,0},{1,17},{17,1},{2,18},{18,2},{3,19},{19,3},{4,20},{20... | collective-permute-start | bytes 589832 | tf_op jit(solution)/shard_map/ppermute | solution.py:199
  514.0 23.9 %all-to-all-start.18 = ((bf16[8,128,768]{2,1,0:T(8,128)(2,1)}), bf16[8,128,768]{2,1,0:T(8,128)(2,1)}, u32[]{:S(2)}, u32[]{:S(2)}) async-start(bf16[8,128,768]{2,1,0:T(8,128)(2,1)} %bitcast.317), calls=%async_computation.18 | async-start | bytes 3145728 | tf_op jit(solution)/shard_map/all_to_all | solution.py:212
  530.2 47.8 %collective-permute-start.10 = (bf16[512,3072]{1,0:T(8,128)(2,1)}, bf16[512,3072]{1,0:T(8,128)(2,1)}, u32[]{:S(2)}, u32[]{:S(2)}) collective-permute-start(bf16[512,3072]{1,0:T(8,128)(2,1)} %get-tuple-element.124), channel_id=1, source_target_pairs={{0,16},{16,0},{1,17},{17,1},{2,18},{18,2},{3,19},{19,3},{4,20},{20... | collective-permute-start | bytes 9437192 | tf_op jit(solution)/shard_map/ppermute | solution.py:199
  537.9 32.8 %all-to-all-start.20 = ((bf16[16,48,768]{2,1,0:T(8,128)(2,1)}), bf16[16,48,768]{2,1,0:T(8,128)(2,1)S(1)}, u32[]{:S(2)}, u32[]{:S(2)}) async-start(bf16[16,48,768]{2,1,0:T(8,128)(2,1)} %fusion.33), calls=%async_computation.20 | async-start | bytes 2359296 | tf_op jit(solution)/shard_map/all_to_all | solution.py:209
  558.0 30.7 %collective-permute-start.6 = (bf16[128,768]{1,0:T(8,128)(2,1)}, bf16[128,768]{1,0:T(8,128)(2,1)S(1)}, u32[]{:S(2)}, u32[]{:S(2)}) collective-permute-start(bf16[128,768]{1,0:T(8,128)(2,1)} %get-tuple-element.114), channel_id=1, source_target_pairs={{0,16},{16,0},{1,17},{17,1},{2,18},{18,2},{3,19},{19,3},{4,20},{20... | collective-permute-start | bytes 589832 | tf_op jit(solution)/shard_map/ppermute | solution.py:199
  570.7 24.8 %all-to-all-start.19 = ((bf16[16,56,384]{2,1,0:T(8,128)(2,1)}), bf16[16,56,384]{2,1,0:T(8,128)(2,1)S(1)}, u32[]{:S(2)}, u32[]{:S(2)}) async-start(bf16[16,56,384]{2,1,0:T(8,128)(2,1)} %add_convert_fusion.1), calls=%async_computation.19 | async-start | bytes 1376256 | tf_op jit(solution)/shard_map/all_to_all | solution.py:209
  (105 other events, 1720.0 us)

commit v2 on v1

--- a/solution.py
+++ b/solution.py
@@ -1,5 +1,3 @@
-import functools
-
 import jax
 import jax.numpy as jnp
 from jax import lax
@@ -131,7 +129,7 @@
         scratch_shapes=[pltpu.VMEM((2, BLOCKS, TILE, TILE), f32)],
         compiler_params=pltpu.CompilerParams(vmem_limit_bytes=40 * 1024 * 1024),
         cost_estimate=pl.CostEstimate(
-            flops=2 * SEQ_LEN * SEQ_LEN * PAIR * 2,
+            flops=48 * SEQ_LEN * SEQ_LEN * PAIR,
             bytes_accessed=SEQ_LEN * PAIR * 8,
             transcendentals=SEQ_LEN * SEQ_LEN,
         ),
@@ -155,11 +153,152 @@
         ],
         compiler_params=pltpu.CompilerParams(vmem_limit_bytes=40 * 1024 * 1024),
         cost_estimate=pl.CostEstimate(
-            flops=5 * SEQ_LEN * SEQ_LEN * PAIR * 2,
+            flops=96 * SEQ_LEN * SEQ_LEN * PAIR,
             bytes_accessed=SEQ_LEN * PAIR * 16,
             transcendentals=SEQ_LEN * SEQ_LEN,
         ),
     )(qkv, bias, delta)
+
+
+CHUNK = 512
+PART = 256
+gelu_root = 0.7978845608028654
+gelu_cube = 0.044715
+
+
+def gelu_parts(before):
+    square = before * before
+    bend = jnp.tanh(gelu_root * before * (1.0 + gelu_cube * square))
+    half = 0.5 * (1.0 + bend)
+    slope = half + (0.5 * gelu_root) * before * (1.0 - bend * bend) * (
+        1.0 + (3.0 * gelu_cube) * square
+    )
+    return before * half, slope
+
+
+def add_product(total, value):
+    @pl.when(pl.program_id(0) == 0)
+    def _():
+        total[...] = value
+
+    @pl.when(pl.program_id(0) > 0)
+    def _():
+        total[...] += value
+
+
+def pick(choice_ref, refs):
+    return jnp.where(choice_ref[0] == 1, refs[0][...], refs[1][...])
+
+
+def parts_of(value, axis):
+    return jnp.split(value, CHUNK // PART, axis=axis)
+
+
+def forward_kernel(
+    choice_ref, in_ref, inner_0, inner_1, outer_0, outer_1, act_ref, slope_ref, out_ref, total
+):
+    values = in_ref[...]
+    inner = parts_of(pick(choice_ref, (inner_0, inner_1)), 1)
+    outer = parts_of(pick(choice_ref, (outer_0, outer_1)), 0)
+    befores = [product(values, part) for part in inner]
+    value = 0.0
+    for i, before in enumerate(befores):
+        act, slope = gelu_parts(before)
+        act = act.astype(bf16)
+        act_ref[:, PART * i : PART * (i + 1)] = act
+        slope_ref[:, PART * i : PART * (i + 1)] = slope.astype(bf16)
+        value = value + product(act, outer[i])
+    add_product(total, value)
+
+    @pl.when(pl.program_id(0) == pl.num_programs(0) - 1)
+    def _():
+        out_ref[...] = total[...].astype(bf16)
+
+
+def backward_kernel(
+    choice_ref, delta_ref, slope_ref, inner_0, inner_1, outer_0, outer_1, pre_ref, out_ref, total
+):
+    inner = pick(choice_ref, (inner_0, inner_1))
+    outer = pick(choice_ref, (outer_0, outer_1))
+    pre = last_contract(delta_ref[...], outer) * slope_ref[...].astype(f32)
+    pre = pre.astype(bf16)
+    pre_ref[...] = pre
+    add_product(total, last_contract(pre, inner))
+
+    @pl.when(pl.program_id(0) == pl.num_programs(0) - 1)
+    def _():
+        out_ref[...] = total[...].astype(bf16)
+
+
+def both_kernel(
+    choice_ref,
+    in_ref,
+    delta_ref,
+    inner_0,
+    inner_1,
+    outer_0,
+    outer_1,
+    act_ref,
+    pre_ref,
+    out_ref,
+    back_ref,
+    total,
+    back,
+):
+    values, delta = in_ref[...], delta_ref[...]
+    inner = parts_of(pick(choice_ref, (inner_0, inner_1)), 1)
+    outer = parts_of(pick(choice_ref, (outer_0, outer_1)), 0)
+    befores = [product(values, part) for part in inner]
+    deltas = [last_contract(delta, part) for part in outer]
+    value, value_back = 0.0, 0.0
+    for i, before in enumerate(befores):
+        act, slope = gelu_parts(before)
+        act = act.astype(bf16)
+        act_ref[:, PART * i : PART * (i + 1)] = act
+        pre = (deltas[i] * slope).astype(bf16)
+        pre_ref[:, PART * i : PART * (i + 1)] = pre
+        value_back = value_back + last_contract(pre, inner[i])
+        value = value + product(act, outer[i])
+    add_product(back, value_back)
+    add_product(total, value)
+
+    @pl.when(pl.program_id(0) == pl.num_programs(0) - 1)
+    def _():
+        out_ref[...] = total[...].astype(bf16)
+        back_ref[...] = back[...].astype(bf16)
+
+
+def expert_call(kernel, held, streamed, weights, wide, narrow):
+    choice, inner, outer = weights
+    rows, width = held[0].shape
+    hidden = inner[0].shape[1]
+    whole = pl.BlockSpec((rows, width), lambda i, c: (0, 0))
+    cut = pl.BlockSpec((rows, CHUNK), lambda i, c: (0, i))
+    return pl.pallas_call(
+        kernel,
+        grid_spec=pltpu.PrefetchScalarGridSpec(
+            num_scalar_prefetch=1,
+            grid=(hidden // CHUNK,),
+            in_specs=[whole] * len(held)
+            + [cut] * len(streamed)
+            + [
+                pl.BlockSpec((width, CHUNK), lambda i, c: (0, i * c[0])),
+                pl.BlockSpec((width, CHUNK), lambda i, c: (0, i * (1 - c[0]))),
+                pl.BlockSpec((CHUNK, width), lambda i, c: (i * c[0], 0)),
+                pl.BlockSpec((CHUNK, width), lambda i, c: (i * (1 - c[0]), 0)),
+            ],
+            out_specs=[cut] * wide + [whole] * narrow,
+            scratch_shapes=[pltpu.VMEM((rows, width), f32)] * narrow,
+        ),
+        out_shape=[jax.ShapeDtypeStruct((rows, hidden), bf16)] * wide
+        + [jax.ShapeDtypeStruct((rows, width), bf16)] * narrow,
+        compiler_params=pltpu.CompilerParams(vmem_limit_bytes=48 * 1024 * 1024),
+        cost_estimate=pl.CostEstimate(
+            flops=12 * narrow * rows * width * hidden,
+            bytes_accessed=4 * width * hidden + 2 * rows * hidden * (wide + len(streamed)),
+            transcendentals=rows * hidden,
+        ),
+    )(choice, *held, *streamed, *inner, *outer)
 
 
 def on_device(
@@ -205,6 +344,10 @@
     def own_of(values):
         return jnp.where(zero, values[0], values[1]), jnp.where(zero, values[1], values[0])
 
+    def after(value, first):
+        element = first[(0,) * first.ndim].astype(f32)
+        return value + (element * 0.0).astype(value.dtype)
+
     def exchange(value):
         return lax.all_to_all(value, "dp", 0, 0, tiled=True)
 
@@ -215,32 +358,50 @@
         spread = jnp.broadcast_to(value[None], (span,) + value.shape)
         return exchange_near(spread).reshape(SEQ_LEN, -1)
 
-    def by_pairs(weight):
-        padded = jnp.pad(weight, ((0, 0), (0, span * PAIR - width)))
-        return jnp.transpose(padded.reshape(share, span, PAIR), (1, 0, 2))
-
+    def by_pairs(values):
+        count = values.shape[0]
+        padded = jnp.pad(values, ((0, 0), (0, span * PAIR - width)))
+        return jnp.transpose(padded.reshape(count, span, PAIR), (1, 0, 2))
+
+    def three_by_pairs(left, middle, right):
+        return jnp.concatenate([by_pairs(left), by_pairs(middle), by_pairs(right)], axis=2)
+
+    context = jnp.where(zero, tokens[0], tokens[1])
+    target = jnp.where(zero, cotangent[0], cotangent[1])
+    full_first = gather_near(context)
+
+    dense_own = lax.all_gather(
+        jnp.concatenate(
+            [query_weight[0], key_weight[0], value_weight[0], output_weight[0]], axis=1
+        ),
+        "dp",
+        axis=0,
+        tiled=True,
+    )
     small = jnp.concatenate(
         [mixer_gain[0], feed_gain[0], router_weight[0].reshape(-1), bias_table[0]]
     )
     small_rows = 8 * (-(-small.shape[0] // (8 * lanes)))
     small_pad = small_rows * lanes - small.shape[0]
     small = jnp.pad(small, (0, small_pad)).reshape(1, small_rows, lanes)
+    half = share // 2
+    pairs_weight = three_by_pairs(query_weight[0], key_weight[0], value_weight[0])
+    passed = lax.ppermute(pairs_weight[:, half:], "section", [(0, 1)])
     pairs_weight = jnp.concatenate(
-        [by_pairs(query_weight[0]), by_pairs(key_weight[0]), by_pairs(value_weight[0])], axis=2
-    )
-    pairs_weight = jnp.concatenate(
-        [pairs_weight, jnp.broadcast_to(small, (span,) + small.shape[1:])], axis=1
+        [
+            jnp.where(zero, pairs_weight[:, :half], passed),
+            jnp.broadcast_to(small, (span,) + small.shape[1:]),
+        ],
+        axis=1,
     )
     pairs_weight = jnp.concatenate([pairs_weight] * (devices // span), axis=0)
+    pairs_weight, full_first = lax.optimization_barrier((pairs_weight, full_first))
     front = to_sections(exchange(pairs_weight))
-    context = jnp.where(zero, tokens[0], tokens[1])
-    target = jnp.where(zero, cotangent[0], cotangent[1])
-    full_first = gather_near(context)
-    output_full = to_sections(
-        exchange(jnp.broadcast_to(output_weight, (devices, share, width))).reshape(width, width)
-    )
-    inner_full = to_sections(expert_in[0, 0])
-    outer_full = to_sections(expert_out[0, 0])
+    attention_first = jnp.concatenate([front[0][:, :half], front[1][:, :half]], axis=1).reshape(
+        width, lanes
+    )
+    inner_own, outer_own = expert_in[0, 0], expert_out[0, 0]
+    inner_other, outer_other = swap(inner_own), swap(outer_own)
     route_mine, route_theirs = own_of((routes[0, 0], routes[0, 1]))
     route_other = swap(route_theirs)
     route_full = (
@@ -256,9 +417,7 @@
 
     sections = []
     for section in range(2):
-        block = front[section]
-        attention = block[:, :share].reshape(width, lanes)
-        flat_small = block[:, share:].reshape(devices, small_rows * lanes)
+        flat_small = front[section][:, half:].reshape(devices, small_rows * lanes)
         cut = [share, 2 * share, (2 + experts) * share, (2 + experts) * share + table_share]
         gain_mixer = flat_small[:, : cut[0]].reshape(width).astype(f32)
         gain_feed = flat_small[:, cut[0] : cut[1]].reshape(width).astype(f32)
@@ -281,7 +440,6 @@
         choose = (route[:, :, None] == expert_index[None, None, :]).astype(f32)
         sections.append(
             {
-                "attention": attention,
                 "gain_mixer": gain_mixer,
                 "gain_feed": gain_feed,
                 "router": router,
@@ -289,9 +447,11 @@
                 "placings": placings,
                 "placing": placings[0] + placings[1],
                 "choose": choose,
-                "output": output_full[section],
-                "inner": inner_full[section],
-                "outer": outer_full[section],
+                "weights": (
+                    (core == section).astype(jnp.int32).reshape(1),
+                    (inner_own, inner_other),
+                    (outer_own, outer_other),
+                ),
             }
         )
 
@@ -299,14 +459,39 @@
         out = product(p["placing"], values).astype(bf16)
         return exchange(out.reshape(experts, slots, width)).reshape(experts * slots, width)
 
+    def rows_from_all(values, route):
+        named = jnp.pad(route.astype(bf16), ((0, 0), (0, PAIR - 2)))
+        every = lax.all_gather(jnp.concatenate([values, named], axis=1), "dp", axis=0)
+        taken = every[:, :, width : width + 2].astype(jnp.int32) == place_dp
+        taken = jnp.any(taken, axis=-1).astype(jnp.int32)
+        rank = jnp.cumsum(taken, axis=1) - taken
+        places = jnp.arange(slots, dtype=jnp.int32)[None, :, None]
+        hot = (rank[:, None, :] == places) & (taken[:, None, :] == 1)
+        rows_in = jnp.einsum(
+            "ksr,krd->ksd", hot.astype(bf16), every[:, :, :width], preferred_element_type=f32
+        )
+        return rows_in.astype(bf16).reshape(experts * slots, width)
+
     def collect(p, returned):
         return [first_contract(p["placings"][c], returned) for c in range(2)]
 
-    def mixer(p, full, own):
-        unit, _ = norm_parts(full.astype(f32))
-        normed = (unit * p["gain_mixer"]).astype(bf16)
-        qkv = product(normed, p["attention"]).astype(bf16)
-        heads = attend(qkv, p["bias"])
+    def with_line(values, line):
+        line = line.reshape(experts, slots)
+        high = lax.reduce_precision(line, 8, 7)
+        line = jnp.concatenate([high, line - high], axis=1).astype(bf16)
+        line = jnp.pad(line, ((0, 0), (0, width - 2 * slots)))
+        return jnp.concatenate([values.reshape(experts, slots, width), line[:, None]], axis=1)
+
+    def cut_line(values):
+        line = values[:, slots, : 2 * slots].astype(f32)
+        line = line[:, :slots] + line[:, slots:]
+        return values[:, :slots].reshape(experts * slots, width), line.reshape(-1, 1)
+
+    def normed_mixer(p, values):
+        unit, _ = norm_parts(values.astype(f32))
+        return (unit * p["gain_mixer"]).astype(bf16)
+
+    def mixer(p, qkv, heads, own):
         mixed = exchange_near(heads.reshape(span, rows, PAIR))
         mixed = jnp.transpose(mixed[:used], (1, 0, 2)).reshape(rows, width)
         hidden = own.astype(f32) + product(mixed, p["output"])
@@ -317,7 +502,6 @@
         gate = chosen / jnp.sum(chosen, axis=1, keepdims=True)
         return {
             "own": own,
-            "normed": normed,
             "qkv": qkv,
             "mixed": mixed,
             "hidden": hidden,
@@ -333,7 +517,7 @@
         gate = cache["gate"]
         return (cache["hidden"] + (gate[:, 0:1] * back[0] + gate[:, 1:2] * back[1])).astype(bf16)
 
-    def mixer_back(p, cache, delta_feed, delta_gate, delta_out):
+    def mixer_back(p, cache, delta_feed, delta_gate, delta_out, beside):
         chosen, chances = cache["chosen"], cache["chances"]
         total = jnp.sum(chosen, axis=1, keepdims=True)
         delta_chosen = delta_gate / total - jnp.sum(
@@ -350,15 +534,14 @@
         )
         delta_hidden = delta_hidden + delta_out
         delta_branch = delta_hidden.astype(bf16)
-        sum_output = first_contract(cache["mixed"], delta_branch)
         delta_mixed = last_contract(delta_branch, p["output"]).astype(bf16)
-        delta_mixed = jnp.pad(delta_mixed, ((0, 0), (0, span * PAIR - width)))
-        delta_mixed = jnp.transpose(delta_mixed.reshape(rows, span, PAIR), (1, 0, 2))
-        delta_heads = exchange_near(delta_mixed).reshape(SEQ_LEN, PAIR)
+        delta_heads = exchange_near(by_pairs(delta_mixed)).reshape(SEQ_LEN, PAIR)
+        beside = after(beside, delta_heads)
+        sum_output = first_contract(cache["mixed"], after(delta_branch, delta_heads))
         delta_qkv, line = attend_back(cache["qkv"], p["bias"], delta_heads)
-        parts = last_contract(delta_qkv, p["attention"]).astype(bf16)
-        parts = exchange_near(parts.reshape(span, rows, width))
-        delta_normed = jnp.sum(parts.astype(f32), axis=0)
+        parts = exchange_near(delta_qkv.reshape(span, rows, lanes))
+        parts = jnp.transpose(parts[:used].reshape(used, rows, 3, PAIR), (1, 2, 0, 3))
+        delta_normed = last_contract(parts.reshape(rows, 3 * width), p["qkv"])
         unit, scale = norm_parts(cache["own"].astype(f32))
         delta_in, sum_mixer = norm_back(delta_normed, unit, scale, p["gain_mixer"])
         delta_in = (delta_in + delta_hidden).astype(bf16)
@@ -379,56 +562,64 @@
             ],
             axis=1,
         ).reshape(devices, small_rows, lanes)
-        sums = jnp.concatenate([sum_attention.reshape(devices, share, lanes), blocks], axis=1)
-        return delta_in, sums.astype(bf16), sum_output.astype(bf16)
+        sums = (
+            sum_attention.reshape(devices, share, lanes),
+            blocks,
+        )
+        sums = jnp.concatenate(sums, axis=1)
+        return delta_in, sums, sum_output, beside
+
+    def half_columns(sums):
+        mine, theirs = own_of((sums[:, : width // 2], sums[:, width // 2 :]))
+        return mine + swap(theirs.astype(bf16)).astype(f32)
 
     p0, p1 = sections
-    cache0 = mixer(p0, full_first, context)
+    normed0 = normed_mixer(p0, full_first)
+    qkv0 = product(normed0, attention_first).astype(bf16)
+    heads0 = attend(qkv0, p0["bias"])
+    p0["output"], p1["output"] = to_sections(after(dense_own[:, 3 * width :], heads0))
+    cache0 = mixer(p0, qkv0, heads0, context)
+    cache0["normed"] = normed0
     arrived0 = dispatch(p0, cache0["normed_feed"])
-    before0 = product(arrived0, p0["inner"])
-    activated0 = jax.nn.gelu(before0).astype(bf16)
-    result0 = product(activated0, p0["outer"]).astype(bf16)
-    back0 = collect(p0, exchange(result0.reshape(experts, slots, width)).reshape(-1, width))
+    arrived_target = rows_from_all(target, route_full[1])
+    activated0, slope0, result0 = expert_call(
+        forward_kernel, [arrived0], [], p0["weights"], 2, 1
+    )
+    returned0 = exchange(result0.reshape(experts, slots, width)).reshape(-1, width)
+    p0["qkv"], p1["qkv"] = to_sections(after(dense_own[:, : 3 * width], result0))
+    back0 = collect(p0, returned0)
     output0 = finish(cache0, back0)
 
-    arrived_target = dispatch(p1, target)
-    delta_act = last_contract(arrived_target, p1["outer"])
-    cache1 = mixer(p1, gather_near(output0), output0)
-    arrived1 = dispatch(p1, cache1["normed_feed"])
+    qkv1 = product(normed_mixer(p1, output0), p1["qkv"]).astype(bf16)
+    qkv1 = exchange_near(
+        three_by_pairs(qkv1[:, :width], qkv1[:, width : 2 * width], qkv1[:, 2 * width :])
+    ).reshape(SEQ_LEN, lanes)
+    cache1 = mixer(p1, qkv1, attend(qkv1, p1["bias"]), output0)
+    gate1 = cache1["gate"]
     gate_slots = sum(
-        jnp.sum(p1["placings"][c].astype(f32) * cache1["gate"][:, c][None, :], axis=1)
-        for c in range(2)
-    )
-    gate_slots = exchange(gate_slots.reshape(experts, slots)).reshape(-1, 1)
-    before1 = product(arrived1, p1["inner"])
-    activated1, gelu_back1 = jax.vjp(jax.nn.gelu, before1)
-    activated1 = activated1.astype(bf16)
-    delta_before1 = gelu_back1(delta_act)[0]
-    leaving1 = last_contract(delta_before1.astype(bf16), p1["inner"]).astype(bf16)
-    result1 = product(activated1, p1["outer"]).astype(bf16)
+        jnp.sum(p1["placings"][c].astype(f32) * gate1[:, c][None, :], axis=1) for c in range(2)
+    )
+    outgoing1 = product(p1["placing"], cache1["normed_feed"]).astype(bf16)
+    arrived1, gate_slots = cut_line(exchange(with_line(outgoing1, gate_slots)))
+    delta1 = (gate_slots * arrived_target.astype(f32)).astype(bf16)
+    full_second = lax.all_gather(
+        output0, "dp", axis=0, tiled=True, axis_index_groups=circles
+    )
+    activated1, before1, result1, leaving1 = expert_call(
+        both_kernel, [arrived1, delta1], [], p1["weights"], 2, 2
+    )
+    cache1["normed"] = normed_mixer(p1, after(full_second, result1))
     inner_gate = jnp.sum(arrived_target.astype(f32) * result1.astype(f32), axis=-1)
-    home1 = collect(p1, exchange(leaving1.reshape(experts, slots, width)).reshape(-1, width))
-    inner_gate = exchange(inner_gate.reshape(experts, slots)).reshape(-1)
+    home1, inner_gate = cut_line(exchange(with_line(leaving1, inner_gate)))
+    home1 = collect(p1, home1)
     delta_gate1 = jnp.stack(
-        [
-            jnp.sum(p1["placings"][c].astype(f32) * inner_gate[:, None], axis=0)
-            for c in range(2)
-        ],
-        axis=1,
-    )
-    gate1 = cache1["gate"]
-    delta_feed1 = gate1[:, 0:1] * home1[0] + gate1[:, 1:2] * home1[1]
-    delta_in1, sums1, sum_output1 = mixer_back(
-        p1, cache1, delta_feed1, delta_gate1, target.astype(f32)
+        [jnp.sum(p1["placings"][c].astype(f32) * inner_gate, axis=0) for c in range(2)], axis=1
+    )
+    delta_in1, sums1, sum_output1, result1 = mixer_back(
+        p1, cache1, home1[0] + home1[1], delta_gate1, target.astype(f32), result1
     )
     back1 = collect(p1, exchange(result1.reshape(experts, slots, width)).reshape(-1, width))
     output1 = finish(cache1, back1)
-    operands1 = (
-        activated1,
-        (gate_slots * arrived_target.astype(f32)).astype(bf16),
-        arrived1,
-        (gate_slots * delta_before1).astype(bf16),
-    )
 
     delta_out0 = delta_in1.astype(f32)
     gate0 = cache0["gate"]
@@ -437,17 +628,22 @@
     arrived_delta = exchange(
         outgoing.astype(bf16).reshape(experts, slots, width)
     ).reshape(-1, width)
-    _, gelu_back0 = jax.vjp(jax.nn.gelu, before0)
-    delta_before0 = gelu_back0(last_contract(arrived_delta, p0["outer"]))[0].astype(bf16)
-    leaving0 = last_contract(delta_before0, p0["inner"]).astype(bf16)
+    output_half1 = lax.psum_scatter(
+        half_columns(sum_output1), "dp", scatter_dimension=0, tiled=True
+    )
+    before0, leaving0 = expert_call(
+        backward_kernel, [arrived_delta], [slope0], p0["weights"], 1, 1
+    )
     home0 = collect(p0, exchange(leaving0.reshape(experts, slots, width)).reshape(-1, width))
     delta_gate0 = jnp.stack([jnp.sum(delta_out0 * back0[c], axis=-1) for c in range(2)], axis=1)
-    delta_in0, sums0, sum_output0 = mixer_back(
-        p0, cache0, home0[0] + home0[1], delta_gate0, delta_out0
-    )
-    operands0 = (activated0, arrived_delta, arrived0, delta_before0)
-
-    totals = []
+    delta_in0, sums0, sum_output0, _ = mixer_back(
+        p0, cache0, home0[0] + home0[1], delta_gate0, delta_out0, result0
+    )
+    output_half0 = half_columns(sum_output0).astype(bf16).reshape(devices, share, width // 2)
+    output_half0 = jnp.sum(exchange(output_half0).astype(f32), axis=0)
+
+    operands0 = (activated0, arrived_delta, arrived0, before0)
+    operands1 = (activated1, delta1, arrived1, before1)
     joined = []
     for left, right in zip(operands0, operands1):
         mine, theirs = own_of((left, right))
@@ -455,24 +651,21 @@
     grad_outer = first_contract(joined[0], joined[1])
     grad_inner = first_contract(joined[2], joined[3])
 
-    def reduced(first, second):
-        mine, theirs = own_of((first, second))
-        both = (mine.astype(f32) + swap(theirs).astype(f32)).astype(bf16)
-        return exchange(both).astype(f32)
-
-    sums = reduced(sums0, sums1)
+    mine, theirs = own_of((sums0, sums1))
+    sums = exchange((mine + swap(theirs.astype(bf16)).astype(f32)).astype(bf16)).astype(f32)
     attention_sums = sums[:, :share].reshape(devices // span, span, share, 3, PAIR)
     attention_sums = jnp.sum(attention_sums, axis=0)[:used]
     attention_sums = jnp.transpose(attention_sums, (2, 1, 0, 3)).reshape(3, share, width)
     small_sums = jnp.sum(sums[:, share:], axis=0).reshape(-1)
+    mine, theirs = own_of((output_half0, output_half1))
+    other = swap(theirs)
+    output_sums = jnp.concatenate(
+        [jnp.where(zero, mine, other), jnp.where(zero, other, mine)], axis=1
+    )
     totals = [small_sums[:share], small_sums[share : 2 * share]]
     totals.append(small_sums[2 * share : (2 + experts) * share].reshape(share, experts))
     end = (2 + experts) * share
     totals.append(small_sums[end : end + table_share])
-    output_sums = reduced(
-        sum_output0.reshape(devices, share, width), sum_output1.reshape(devices, share, width)
-    )
-    output_sums = jnp.sum(output_sums, axis=0)
 
     def by_micro(first, second):
         mine, theirs = own_of((first, second))

time: 612 us -> 580 us (0.948)
  matrix products: 132 us -> 59 us
  Pallas kernels: 28 us -> 70.3 us
  blocking collectives: 37.5 us -> 0 us
  other arithmetic: 38.9 us -> 58.1 us
  between operations: 2.99 us -> 19.8 us
    all_to_all x13 -> x10, waiting for transfers between devices: 154 us -> 101 us  [exchange(): return lax.all_to_all(value, 'dp', 0, 0, tiled=True)]
    all_gather x0 -> x3, waiting for transfers between devices: none -> 52 us  [the longest x1 31.6 us: on_device(): lax.all_gather(jnp.concatenate([query_weight[0], key_weight[0], value_wei...]
    pallas_call x0 -> x3, Pallas kernels: none -> 42.5 us  [expert_call(): pl.pallas_call(kernel, grid_spec=pltpu.PrefetchScalarGridSpec(num_scalar_...]
    dot_general x15 -> x10, matrix products: 49.5 us -> 11.1 us  [product(): return jnp.dot(left, right, preferred_element_type=f32)]
    all_to_all x2 -> x0, blocking collectives: 37.5 us -> none  [the longest x1 27.5 us: exchange(): return lax.all_to_all(value, 'dp', 0, 0, tiled=True)]
    dot_general x10 -> x6, matrix products: 44.3 us -> 9.62 us  [last_contract(): lax.dot_general(left, right, (((1,), (1,)), ((), ())), preferred_element_...]
    all_to_all x13 -> x10, starting transfers between devices: 67.8 us -> 54.9 us  [exchange(): return lax.all_to_all(value, 'dp', 0, 0, tiled=True)]
    all_to_all x7 -> x8, starting transfers between devices: 31.6 us -> 42.2 us  [exchange_near(): lax.all_to_all(value, 'dp', 0, 0, tiled=True, axis_index_groups=circles)]
  transfers between devices with their start and end apart: 33 -> 39, of which waited for: 21 -> 20; matrix products, arithmetic and copies ran while one was open for 23% -> 24% of each run, Pallas kernels for 2% -> 7%
where the time goes in v2:
time: 580 us; the launch traced here: 569 us
  waiting for transfers between devices  217 us (37%)
  starting transfers between devices  101 us (17%)
  Pallas kernels  70.3 us (12%)
  matrix products  59 us (10%)
  other arithmetic  58.1 us (10%)
  local copies, waits for them, and re-layouts  44.3 us (8%)
  between operations  19.8 us (3%)
    all_to_all x10, waiting for transfers between devices, exchange(): return lax.all_to_all(value, 'dp', 0, 0, tiled=True)  101 us
    all_to_all x8, waiting for transfers between devices, exchange_near(): lax.all_to_all(value, 'dp', 0, 0, tiled=True, axis_index_groups=circles)  60.3 us
    all_to_all x10, starting transfers between devices, exchange(): return lax.all_to_all(value, 'dp', 0, 0, tiled=True)  54.9 us
    pallas_call x3, Pallas kernels, expert_call(): pl.pallas_call(kernel, grid_spec=pltpu.PrefetchScalarGridSpec(num_scalar_...  42.5 us
    all_to_all x8, starting transfers between devices, exchange_near(): lax.all_to_all(value, 'dp', 0, 0, tiled=True, axis_index_groups=circles)  42.2 us
    dot_general x16, matrix products, first_contract(): lax.dot_general(left, right, (((0,), (0,)), ((), ())), preferred_element_...  35 us
    all_gather x1, waiting for transfers between devices, on_device(): lax.all_gather(jnp.concatenate([query_weight[0], key_weight[0], value_wei...  31.6 us
    all_gather x1, waiting for transfers between devices, rows_from_all(): lax.all_gather(jnp.concatenate([values, named], axis=1), 'dp', axis=0)  20.4 us
  transfers between devices with their start and end apart: 39, of which 20 were waited for; matrix products, arithmetic and copies ran while one was open for 24% of the time, Pallas kernels for 7%

profile of v2, /device:TPU:0, one launch (start us, length us, event | category | flops | bytes accessed | tf_op | source)
XLA Modules:
  0.0 569.4 jit_solution(4370576548560568404)
XLA Ops:
  21.8 22.8 %all-to-all-done = bf16[8,128,768]{2,1,0:T(8,128)(2,1)S(1)} async-done(((bf16[8,128,768]{2,1,0:T(8,128)(2,1)}), bf16[8,128,768]{2,1,0:T(8,128)(2,1)S(1)}, u32[]{:S(2)}, u32[]{:S(2)}) %all-to-all-start) | async-done | bytes 1572896 | tf_op jit(solution)/shard_map/all_to_all | solution.py:355
  56.4 11.2 %all-to-all-done.1 = bf16[16,32,384]{2,1,0:T(8,128)(2,1)S(1)} async-done(((bf16[16,32,384]{2,1,0:T(8,128)(2,1)}), bf16[16,32,384]{2,1,0:T(8,128)(2,1)S(1)}, u32[]{:S(2)}, u32[]{:S(2)}) %all-to-all-start.1) | async-done | bytes 393248 | tf_op jit(solution)/shard_map/all_to_all | solution.py:352
  77.6 31.6 %all-gather.5.cloned.1.call-done = bf16[768,3072]{1,0:T(8,128)(2,1)} async-done(((bf16[48,3072]{1,0:T(8,128)(2,1)}), bf16[768,3072]{1,0:T(8,128)(2,1)}) %all-gather.5.cloned.1.call-update) | async-done | bytes 4718608 | tf_op jit(solution)/shard_map/all_gather | solution.py:373
  130.4 19.9 %all-to-all-done.3 = bf16[16,32,768]{2,1,0:T(8,128)(2,1)S(1)} async-done(((bf16[16,32,768]{2,1,0:T(8,128)(2,1)}), bf16[16,32,768]{2,1,0:T(8,128)(2,1)S(1)}, u32[]{:S(2)}, u32[]{:S(2)}) %all-to-all-start.3) | async-done | bytes 786464 | tf_op jit(solution)/shard_map/all_to_all | solution.py:352
  150.3 13.7 %shard_map.230 = (bf16[512,3072]{1,0:T(8,128)(2,1)S(1)}, bf16[512,3072]{1,0:T(8,128)(2,1)}, bf16[512,768]{1,0:T(8,128)(2,1)}) custom-call(s32[1]{0:T(128)} %bitcast.21.choice_ref, bf16[512,768]{1,0:T(8,128)(2,1)S(1)} %bitcast.256, bf16[768,3072]{1,0:T(8,128)(2,1)} %bitcast.338, bf16[768,3072]{1,0:T(8,128)(2,1)} %collective-permute-done.4.inner_1, ...), custom_call_target="tpu_custom_call" | custom-call | flops 14495514624 | bytes 15728640 | tf_op jit(solution)/shard_map/pallas_call | solution.py:277
  184.3 11.7 %all-to-all-done.4 = bf16[16,32,768]{2,1,0:T(8,128)(2,1)S(1)} async-done(((bf16[16,32,768]{2,1,0:T(8,128)(2,1)}), bf16[16,32,768]{2,1,0:T(8,128)(2,1)S(1)}, u32[]{:S(2)}, u32[]{:S(2)}) %all-to-all-start.4) | async-done | bytes 786464 | tf_op jit(solution)/shard_map/all_to_all | solution.py:352
  202.8 6.7 %all-to-all-start.5 = ((bf16[8,128,384]{2,1,0:T(8,128)(2,1)}), bf16[8,128,384]{2,1,0:T(8,128)(2,1)S(1)}, u32[]{:S(2)}, u32[]{:S(2)}) async-start(bf16[8,128,384]{2,1,0:T(8,128)(2,1)} %pad_maximum_fusion.4), calls=%async_computation.5 | async-start | bytes 1572864 | tf_op jit(solution)/shard_map/all_to_all | solution.py:355
  210.7 14.0 %all-to-all-done.5 = bf16[8,128,384]{2,1,0:T(8,128)(2,1)S(1)} async-done(((bf16[8,128,384]{2,1,0:T(8,128)(2,1)}), bf16[8,128,384]{2,1,0:T(8,128)(2,1)S(1)}, u32[]{:S(2)}, u32[]{:S(2)}) %all-to-all-start.5) | async-done | bytes 786464 | tf_op jit(solution)/shard_map/all_to_all | solution.py:355
  235.2 10.5 %all-to-all-done.6 = bf16[8,128,128]{1,2,0:T(8,128)(2,1)S(1)} async-done(((bf16[8,128,128]{1,2,0:T(8,128)(2,1)}), bf16[8,128,128]{1,2,0:T(8,128)(2,1)S(1)}, u32[]{:S(2)}, u32[]{:S(2)}) %all-to-all-start.6) | async-done | bytes 262176 | tf_op jit(solution)/shard_map/all_to_all | solution.py:355
  255.5 20.4 %all-gather.9.cloned.1.call-done = bf16[2048,896]{1,0:T(8,128)(2,1)} async-done(((bf16[128,896]{1,0:T(8,128)(2,1)}), bf16[2048,896]{1,0:T(8,128)(2,1)}) %all-gather.9.cloned.1.call-update) | async-done | bytes 3670032 | tf_op jit(solution)/shard_map/all_gather | solution.py:464
  281.0 17.3 %shard_map.232 = (bf16[512,3072]{1,0:T(8,128)(2,1)}, bf16[512,3072]{1,0:T(8,128)(2,1)}, bf16[512,768]{1,0:T(8,128)(2,1)S(1)}, bf16[512,768]{1,0:T(8,128)(2,1)S(1)}) custom-call(s32[1]{0:T(128)} %bitcast.39.choice_ref, bf16[512,768]{1,0:T(8,128)(2,1)S(1)} %bitcast.257, bf16[512,768]{1,0:T(8,128)(2,1)S(1)} %fusion.25.delta_ref, bf16[768,3072]{1,0:T(8,128)(2,1)} %bitcast.339, ...), custom_call_target="tpu_custom_call" | custom-call | flops 28991029248 | bytes 15728640 | tf_op jit(solution)/shard_map/pallas_call | solution.py:277
  304.8 21.4 %all-to-all-done.8 = bf16[16,33,768]{2,1,0:T(8,128)(2,1)S(1)} async-done(((bf16[16,33,768]{2,1,0:T(8,128)(2,1)}), bf16[16,33,768]{2,1,0:T(8,128)(2,1)S(1)}, u32[]{:S(2)}, u32[]{:S(2)}) %all-to-all-start.8) | async-done | bytes 811040 | tf_op jit(solution)/shard_map/all_to_all | solution.py:352
  332.1 8.5 %all-to-all-start.9 = ((bf16[8,128,128]{2,1,0:T(8,128)(2,1)}), bf16[8,128,128]{2,1,0:T(8,128)(2,1)S(1)}, u32[]{:S(2)}, u32[]{:S(2)}) async-start(bf16[8,128,128]{2,1,0:T(8,128)(2,1)} %bitcast_bitcast_fusion.1), calls=%async_computation.9 | async-start | bytes 524288 | tf_op jit(solution)/shard_map/all_to_all | solution.py:355
  343.2 6.4 %all-to-all-done.9 = bf16[8,128,128]{2,1,0:T(8,128)(2,1)S(1)} async-done(((bf16[8,128,128]{2,1,0:T(8,128)(2,1)}), bf16[8,128,128]{2,1,0:T(8,128)(2,1)S(1)}, u32[]{:S(2)}, u32[]{:S(2)}) %all-to-all-start.9) | async-done | bytes 262176 | tf_op jit(solution)/shard_map/all_to_all | solution.py:355
  349.6 9.1 %shard_map.233 = (bf16[1024,384]{1,0:T(8,128)(2,1)S(1)}, f32[8,1280]{1,0:T(8,128)S(1)}) custom-call(bf16[1024,384]{1,0:T(8,128)(2,1)S(1)} %bitcast.260, f32[8,1280]{1,0:T(8,128)S(1)} %pad.74.bias_ref, bf16[1024,128]{1,0:T(8,128)(2,1)S(1)} %bitcast.263), custom_call_target="tpu_custom_call" | custom-call | flops 12884901888 | bytes 2097152 | tf_op jit(solution)/shard_map/pallas_call | solution.py:140
  396.2 13.5 %all-to-all-done.12 = bf16[16,32,768]{2,1,0:T(8,128)(2,1)S(1)} async-done(((bf16[16,32,768]{2,1,0:T(8,128)(2,1)}), bf16[16,32,768]{2,1,0:T(8,128)(2,1)S(1)}, u32[]{:S(2)}, u32[]{:S(2)}) %all-to-all-start.12) | async-done | bytes 786464 | tf_op jit(solution)/shard_map/all_to_all | solution.py:352
  416.4 11.5 %shard_map.234 = (bf16[512,3072]{1,0:T(8,128)(2,1)S(1)}, bf16[512,768]{1,0:T(8,128)(2,1)}) custom-call(s32[1]{0:T(128)} %bitcast.21.choice_ref, bf16[512,768]{1,0:T(8,128)(2,1)S(1)} %bitcast.255, bf16[512,3072]{1,0:T(8,128)(2,1)} %get-tuple-element.33.slope_ref, bf16[768,3072]{1,0:T(8,128)(2,1)} %bitcast.340, ...), custom_call_target="tpu_custom_call" | custom-call | flops 14495514624 | bytes 15728640 | tf_op jit(solution)/shard_map/pallas_call | solution.py:277
  429.6 6.7 %all-to-all-done.10 = bf16[16,32,768]{2,1,0:T(8,128)(2,1)} async-done(((bf16[16,32,768]{2,1,0:T(8,128)(2,1)}), bf16[16,32,768]{2,1,0:T(8,128)(2,1)}, u32[]{:S(2)}, u32[]{:S(2)}) %all-to-all-start.10) | async-done | bytes 786464 | tf_op jit(solution)/shard_map/all_to_all | solution.py:352
  448.9 12.3 %all-to-all-done.13 = bf16[16,32,768]{2,1,0:T(8,128)(2,1)S(1)} async-done(((bf16[16,32,768]{2,1,0:T(8,128)(2,1)}), bf16[16,32,768]{2,1,0:T(8,128)(2,1)S(1)}, u32[]{:S(2)}, u32[]{:S(2)}) %all-to-all-start.13) | async-done | bytes 786464 | tf_op jit(solution)/shard_map/all_to_all | solution.py:352
  476.8 9.2 %shard_map.235 = (bf16[1024,384]{1,0:T(8,128)(2,1)S(1)}, f32[8,1280]{1,0:T(8,128)S(1)}) custom-call(bf16[1024,384]{1,0:T(8,128)(2,1)S(1)} %copy-done.5, f32[8,1280]{1,0:T(8,128)S(1)} %pad.68.bias_ref, bf16[1024,128]{1,0:T(8,128)(2,1)S(1)} %bitcast.267), custom_call_target="tpu_custom_call" | custom-call | flops 12884901888 | bytes 2097152 | tf_op jit(solution)/shard_map/pallas_call | solution.py:140
  506.1 6.4 %all-to-all-start.17 = ((bf16[16,48,384]{2,1,0:T(8,128)(2,1)}), bf16[16,48,384]{2,1,0:T(8,128)(2,1)}, u32[]{:S(2)}, u32[]{:S(2)}) async-start(bf16[16,48,384]{2,1,0:T(8,128)(2,1)} %bitcast.88), calls=%async_computation.17 | async-start | bytes 1179648 | tf_op jit(solution)/shard_map/all_to_all | solution.py:352
  519.4 9.5 %fusion.8 = f32[1,1,3072,768]{3,2,1,0:T(8,128)} fusion(bf16[512,3072]{1,0:T(8,128)(2,1)} %collective-permute-done.15, bf16[512,3072]{1,0:T(8,128)(2,1)S(1)} %copy-done.37, bf16[512,768]{1,0:T(8,128)(2,1)} %collective-permute-done.16, bf16[512,768]{1,0:T(8,128)(2,1)} %get-tuple-element.123), kind=kOutput, calls=%fused_computation.8 | convolution fusion | flops 4847566848 | bytes 17301504 | tf_op jit(solution)/shard_map/dot_general | solution.py:29
  531.4 6.9 %all-to-all-start.16 = ((bf16[16,56,384]{2,1,0:T(8,128)(2,1)}), bf16[16,56,384]{2,1,0:T(8,128)(2,1)S(1)}, u32[]{:S(2)}, u32[]{:S(2)}) async-start(bf16[16,56,384]{2,1,0:T(8,128)(2,1)} %add_convert_fusion.1), calls=%async_computation.16 | async-start | bytes 1376256 | tf_op jit(solution)/shard_map/all_to_all | solution.py:352
  538.3 9.8 %fusion.11 = f32[1,1,768,3072]{3,2,1,0:T(8,128)} fusion(bf16[512,3072]{1,0:T(8,128)(2,1)} %collective-permute-done.14, bf16[512,3072]{1,0:T(8,128)(2,1)} %get-tuple-element.121, bf16[512,768]{1,0:T(8,128)(2,1)} %collective-permute-done.13, bf16[512,768]{1,0:T(8,128)(2,1)} %get-tuple-element.125), kind=kOutput, calls=%fused_computation.9 | convolution fusion | flops 4847566848 | bytes 17301504 | tf_op jit(solution)/shard_map/dot_general | solution.py:29
  (567 shorter events, 238.7 us)
Async XLA Ops:
  7.2 102.0 %all-gather.5.cloned.1.call-start = ((), (), s32[]{:S(2)}) async-start(), calls=%async_computation.19 | async-start | bytes 5013504 | tf_op jit(solution)/shard_map/all_gather | solution.py:373
  12.6 31.9 %all-to-all-start = ((bf16[8,128,768]{2,1,0:T(8,128)(2,1)}), bf16[8,128,768]{2,1,0:T(8,128)(2,1)S(1)}, u32[]{:S(2)}, u32[]{:S(2)}) async-start(bf16[8,128,768]{2,1,0:T(8,128)(2,1)} %broadcast_in_dim.28), calls=%async_computation | async-start | bytes 3145728 | tf_op jit(solution)/shard_map/all_to_all | solution.py:355
  45.4 22.2 %all-to-all-start.1 = ((bf16[16,32,384]{2,1,0:T(8,128)(2,1)}), bf16[16,32,384]{2,1,0:T(8,128)(2,1)S(1)}, u32[]{:S(2)}, u32[]{:S(2)}) async-start(bf16[16,32,384]{2,1,0:T(8,128)(2,1)} %copy.126), calls=%async_computation.1 | async-start | bytes 786432 | tf_op jit(solution)/shard_map/all_to_all | solution.py:352
  51.7 78.7 %collective-permute-start.4 = (bf16[768,3072]{1,0:T(8,128)(2,1)}, bf16[768,3072]{1,0:T(8,128)(2,1)}, u32[]{:S(2)}, u32[]{:S(2)}) collective-permute-start(bf16[768,3072]{1,0:T(8,128)(2,1)} %bitcast.337), channel_id=1, source_target_pairs={{0,16},{16,0},{1,17},{17,1},{2,18},{18,2},{3,19},{19,3},{4,20},{20... | collective-permute-start | bytes 14155784 | tf_op jit(solution)/shard_map/ppermute | solution.py:338
  52.2 78.2 %collective-permute-start.5 = (bf16[3072,768]{1,0:T(8,128)(2,1)}, bf16[3072,768]{1,0:T(8,128)(2,1)}, u32[]{:S(2)}, u32[]{:S(2)}) collective-permute-start(bf16[3072,768]{1,0:T(8,128)(2,1)} %bitcast.341), channel_id=1, source_target_pairs={{0,16},{16,0},{1,17},{17,1},{2,18},{18,2},{3,19},{19,3},{4,20},{20... | collective-permute-start | bytes 14155784 | tf_op jit(solution)/shard_map/ppermute | solution.py:338
  126.5 23.8 %all-to-all-start.3 = ((bf16[16,32,768]{2,1,0:T(8,128)(2,1)}), bf16[16,32,768]{2,1,0:T(8,128)(2,1)S(1)}, u32[]{:S(2)}, u32[]{:S(2)}) async-start(bf16[16,32,768]{2,1,0:T(8,128)(2,1)} %bitcast.287), calls=%async_computation.3 | async-start | bytes 1572864 | tf_op jit(solution)/shard_map/all_to_all | solution.py:352
  168.3 29.2 %collective-permute-start.6 = (bf16[768,2304]{1,0:T(8,128)(2,1)}, bf16[768,2304]{1,0:T(8,128)(2,1)}, u32[]{:S(2)}, u32[]{:S(2)}) collective-permute-start(bf16[768,2304]{1,0:T(8,128)(2,1)} %slice_add_fusion), channel_id=1, source_target_pairs={{0,16},{16,0},{1,17},{17,1},{2,18},{18,2},{3,19},{19,3},{4,20},{20... | collective-permute-start | bytes 10616840 | tf_op jit(solution)/shard_map/ppermute | solution.py:338
  169.6 26.4 %all-to-all-start.4 = ((bf16[16,32,768]{2,1,0:T(8,128)(2,1)}), bf16[16,32,768]{2,1,0:T(8,128)(2,1)S(1)}, u32[]{:S(2)}, u32[]{:S(2)}) async-start(bf16[16,32,768]{2,1,0:T(8,128)(2,1)} %bitcast.26), calls=%async_computation.4 | async-start | bytes 1572864 | tf_op jit(solution)/shard_map/all_to_all | solution.py:352
  174.7 101.3 %all-gather.9.cloned.1.call-start = ((), (), s32[]{:S(2)}) async-start(), calls=%async_computation.22 | async-start | bytes 3899392 | tf_op jit(solution)/shard_map/all_gather | solution.py:464
  202.8 21.8 %all-to-all-start.5 = ((bf16[8,128,384]{2,1,0:T(8,128)(2,1)}), bf16[8,128,384]{2,1,0:T(8,128)(2,1)S(1)}, u32[]{:S(2)}, u32[]{:S(2)}) async-start(bf16[8,128,384]{2,1,0:T(8,128)(2,1)} %pad_maximum_fusion.4), calls=%async_computation.5 | async-start | bytes 1572864 | tf_op jit(solution)/shard_map/all_to_all | solution.py:355
  250.1 30.0 %all-to-all-start.7 = ((bf16[16,33,768]{2,1,0:T(8,128)(2,1)}), bf16[16,33,768]{2,1,0:T(8,128)(2,1)S(1)}, u32[]{:S(2)}, u32[]{:S(2)}) async-start(bf16[16,33,768]{2,1,0:T(8,128)(2,1)} %pad_maximum_fusion.2), calls=%async_computation.7 | async-start | bytes 1966080 | tf_op jit(solution)/shard_map/all_to_all | solution.py:352
  299.8 26.4 %all-to-all-start.8 = ((bf16[16,33,768]{2,1,0:T(8,128)(2,1)}), bf16[16,33,768]{2,1,0:T(8,128)(2,1)S(1)}, u32[]{:S(2)}, u32[]{:S(2)}) async-start(bf16[16,33,768]{2,1,0:T(8,128)(2,1)} %pad_maximum_fusion.3), calls=%async_computation.8 | async-start | bytes 1966080 | tf_op jit(solution)/shard_map/all_to_all | solution.py:352
  304.1 66.2 %all-gather.7.cloned.1.call-start = ((), (), s32[]{:S(2)}) async-start(), calls=%async_computation.20 | async-start | bytes 1769472 | tf_op jit(solution)/shard_map/all_gather | solution.py:605
  343.2 195.0 %collective-permute-start.13 = (bf16[512,768]{1,0:T(8,128)(2,1)}, bf16[512,768]{1,0:T(8,128)(2,1)}, u32[]{:S(2)}, u32[]{:S(2)}) collective-permute-start(bf16[512,768]{1,0:T(8,128)(2,1)} %get-tuple-element.126), channel_id=1, source_target_pairs={{0,16},{16,0},{1,17},{17,1},{2,18},{18,2},{3,19},{19,3},{4,20},{20... | collective-permute-start | bytes 2359304 | tf_op jit(solution)/shard_map/ppermute | solution.py:338
  370.2 148.7 %collective-permute-start.15 = (bf16[512,3072]{1,0:T(8,128)(2,1)}, bf16[512,3072]{1,0:T(8,128)(2,1)}, u32[]{:S(2)}, u32[]{:S(2)}) collective-permute-start(bf16[512,3072]{1,0:T(8,128)(2,1)} %get-tuple-element.120), channel_id=1, source_target_pairs={{0,16},{16,0},{1,17},{17,1},{2,18},{18,2},{3,19},{19,3},{4,20},{20... | collective-permute-start | bytes 9437192 | tf_op jit(solution)/shard_map/ppermute | solution.py:338
  383.7 26.0 %all-to-all-start.12 = ((bf16[16,32,768]{2,1,0:T(8,128)(2,1)}), bf16[16,32,768]{2,1,0:T(8,128)(2,1)S(1)}, u32[]{:S(2)}, u32[]{:S(2)}) async-start(bf16[16,32,768]{2,1,0:T(8,128)(2,1)} %bitcast.288), calls=%async_computation.12 | async-start | bytes 1572864 | tf_op jit(solution)/shard_map/all_to_all | solution.py:352
  389.6 159.7 %reduce-scatter.2.cloned.1.call-start = ((), (), s32[]{:S(2)}) async-start(), calls=%async_computation.21 | async-start | bytes 1253376 | tf_op jit(solution)/shard_map/reduce_scatter | solution.py:631
  409.7 26.6 %all-to-all-start.10 = ((bf16[16,32,768]{2,1,0:T(8,128)(2,1)}), bf16[16,32,768]{2,1,0:T(8,128)(2,1)}, u32[]{:S(2)}, u32[]{:S(2)}) async-start(bf16[16,32,768]{2,1,0:T(8,128)(2,1)} %bitcast.58), calls=%async_computation.10 | async-start | bytes 1572864 | tf_op jit(solution)/shard_map/all_to_all | solution.py:352
  436.3 24.9 %all-to-all-start.13 = ((bf16[16,32,768]{2,1,0:T(8,128)(2,1)}), bf16[16,32,768]{2,1,0:T(8,128)(2,1)S(1)}, u32[]{:S(2)}, u32[]{:S(2)}) async-start(bf16[16,32,768]{2,1,0:T(8,128)(2,1)} %bitcast.69), calls=%async_computation.13 | async-start | bytes 1572864 | tf_op jit(solution)/shard_map/all_to_all | solution.py:352
  475.7 62.5 %collective-permute-start.14 = (bf16[512,3072]{1,0:T(8,128)(2,1)}, bf16[512,3072]{1,0:T(8,128)(2,1)}, u32[]{:S(2)}, u32[]{:S(2)}) collective-permute-start(bf16[512,3072]{1,0:T(8,128)(2,1)} %get-tuple-element.122), channel_id=1, source_target_pairs={{0,16},{16,0},{1,17},{17,1},{2,18},{18,2},{3,19},{19,3},{4,20},{20... | collective-permute-start | bytes 9437192 | tf_op jit(solution)/shard_map/ppermute | solution.py:338
  487.1 18.9 %all-to-all-start.15 = ((bf16[8,128,384]{1,2,0:T(8,128)(2,1)}), bf16[8,128,384]{1,2,0:T(8,128)(2,1)S(1)}, u32[]{:S(2)}, u32[]{:S(2)}) async-start(bf16[8,128,384]{1,2,0:T(8,128)(2,1)} %copy.144), calls=%async_computation.15 | async-start | bytes 1572864 | tf_op jit(solution)/shard_map/all_to_all | solution.py:355
  498.8 20.1 %collective-permute-start.16 = (bf16[512,768]{1,0:T(8,128)(2,1)}, bf16[512,768]{1,0:T(8,128)(2,1)}, u32[]{:S(2)}, u32[]{:S(2)}) collective-permute-start(bf16[512,768]{1,0:T(8,128)(2,1)} %get-tuple-element.124), channel_id=1, source_target_pairs={{0,16},{16,0},{1,17},{17,1},{2,18},{18,2},{3,19},{19,3},{4,20},{20... | collective-permute-start | bytes 2359304 | tf_op jit(solution)/shard_map/ppermute | solution.py:338
  506.1 25.3 %all-to-all-start.17 = ((bf16[16,48,384]{2,1,0:T(8,128)(2,1)}), bf16[16,48,384]{2,1,0:T(8,128)(2,1)}, u32[]{:S(2)}, u32[]{:S(2)}) async-start(bf16[16,48,384]{2,1,0:T(8,128)(2,1)} %bitcast.88), calls=%async_computation.17 | async-start | bytes 1179648 | tf_op jit(solution)/shard_map/all_to_all | solution.py:352
  531.4 24.9 %all-to-all-start.16 = ((bf16[16,56,384]{2,1,0:T(8,128)(2,1)}), bf16[16,56,384]{2,1,0:T(8,128)(2,1)S(1)}, u32[]{:S(2)}, u32[]{:S(2)}) async-start(bf16[16,56,384]{2,1,0:T(8,128)(2,1)} %add_convert_fusion.1), calls=%async_computation.16 | async-start | bytes 1376256 | tf_op jit(solution)/shard_map/all_to_all | solution.py:352
  (136 other events, 1314.9 us)
Sparse Core Ops, SparseCore 0:
  11.4 97.7 all-gather.4
  178.2 97.6 all-gather.8
  306.4 50.6 all-gather.6
  396.3 134.9 reduce-scatter.1

commit v3 on v2

--- a/solution.py
+++ b/solution.py
@@ -1,3 +1,5 @@
+import functools
+
 import jax
 import jax.numpy as jnp
 from jax import lax
@@ -299,6 +301,27 @@
             transcendentals=rows * hidden,
         ),
     )(choice, *held, *streamed, *inner, *outer)
+
+
+def add_pairs_kernel(span, in_ref, *out_refs):
+    share, width = out_refs[0].shape
+    for part, out_ref in enumerate(out_refs):
+        for pair in range(width // PAIR):
+            total = 0.0
+            for source in range(pair, in_ref.shape[0], span):
+                block = in_ref[source, 0:share, PAIR * part : PAIR * (part + 1)]
+                total = total + block.astype(f32)
+            out_ref[:, PAIR * pair : PAIR * (pair + 1)] = total
+
+
+def add_pairs(blocks, span, share):
+    return pl.pallas_call(
+        functools.partial(add_pairs_kernel, span),
+        out_shape=[jax.ShapeDtypeStruct((share, HEADS * HEAD_DIM), f32)] * 3,
+        in_specs=[pl.BlockSpec(memory_space=pltpu.VMEM)],
+        out_specs=[pl.BlockSpec(memory_space=pltpu.VMEM)] * 3,
+        compiler_params=pltpu.CompilerParams(vmem_limit_bytes=32 * 1024 * 1024),
+    )(blocks)
 
 
 def on_device(
@@ -455,22 +478,8 @@
             }
         )
 
-    def dispatch(p, values):
-        out = product(p["placing"], values).astype(bf16)
-        return exchange(out.reshape(experts, slots, width)).reshape(experts * slots, width)
-
-    def rows_from_all(values, route):
-        named = jnp.pad(route.astype(bf16), ((0, 0), (0, PAIR - 2)))
-        every = lax.all_gather(jnp.concatenate([values, named], axis=1), "dp", axis=0)
-        taken = every[:, :, width : width + 2].astype(jnp.int32) == place_dp
-        taken = jnp.any(taken, axis=-1).astype(jnp.int32)
-        rank = jnp.cumsum(taken, axis=1) - taken
-        places = jnp.arange(slots, dtype=jnp.int32)[None, :, None]
-        hot = (rank[:, None, :] == places) & (taken[:, None, :] == 1)
-        rows_in = jnp.einsum(
-            "ksr,krd->ksd", hot.astype(bf16), every[:, :, :width], preferred_element_type=f32
-        )
-        return rows_in.astype(bf16).reshape(experts * slots, width)
+    def outgoing_of(p, values):
+        return product(p["placing"], values).astype(bf16).reshape(experts, slots, width)
 
     def collect(p, returned):
         return [first_contract(p["placings"][c], returned) for c in range(2)]
@@ -491,9 +500,11 @@
         unit, _ = norm_parts(values.astype(f32))
         return (unit * p["gain_mixer"]).astype(bf16)
 
-    def mixer(p, qkv, heads, own):
+    def spread_heads(heads):
         mixed = exchange_near(heads.reshape(span, rows, PAIR))
-        mixed = jnp.transpose(mixed[:used], (1, 0, 2)).reshape(rows, width)
+        return jnp.transpose(mixed[:used], (1, 0, 2)).reshape(rows, width)
+
+    def mixer(p, qkv, mixed, own):
         hidden = own.astype(f32) + product(mixed, p["output"])
         unit_feed, scale_feed = norm_parts(hidden)
         normed_feed = (unit_feed * p["gain_feed"]).astype(bf16)
@@ -537,15 +548,18 @@
         delta_mixed = last_contract(delta_branch, p["output"]).astype(bf16)
         delta_heads = exchange_near(by_pairs(delta_mixed)).reshape(SEQ_LEN, PAIR)
         beside = after(beside, delta_heads)
-        sum_output = first_contract(cache["mixed"], after(delta_branch, delta_heads))
+        sum_output = first_contract(cache["mixed"], delta_branch)
         delta_qkv, line = attend_back(cache["qkv"], p["bias"], delta_heads)
         parts = exchange_near(delta_qkv.reshape(span, rows, lanes))
         parts = jnp.transpose(parts[:used].reshape(used, rows, 3, PAIR), (1, 2, 0, 3))
         delta_normed = last_contract(parts.reshape(rows, 3 * width), p["qkv"])
         unit, scale = norm_parts(cache["own"].astype(f32))
         delta_in, sum_mixer = norm_back(delta_normed, unit, scale, p["gain_mixer"])
+        if "attention" in p:
+            heads_part = last_contract(delta_qkv, p["attention"])
+            sum_mixer = jnp.sum(heads_part * norm_parts(cache["full"].astype(f32))[0], axis=0)
         delta_in = (delta_in + delta_hidden).astype(bf16)
-        sum_attention = first_contract(cache["normed"], delta_qkv)
+        sum_attention = first_contract(cache["normed"](delta_qkv), delta_qkv)
         sum_table = lax.dot_general(
             bucket_hot, line[:2], (((1,), (1,)), ((), ())), precision=lax.Precision.HIGHEST
         )
@@ -562,12 +576,8 @@
             ],
             axis=1,
         ).reshape(devices, small_rows, lanes)
-        sums = (
-            sum_attention.reshape(devices, share, lanes),
-            blocks,
-        )
-        sums = jnp.concatenate(sums, axis=1)
-        return delta_in, sums, sum_output, beside
+        sums = jnp.concatenate([sum_attention.reshape(devices, share, lanes), blocks], axis=1)
+        return delta_in, sums, sum_output, beside, parts
 
     def half_columns(sums):
         mine, theirs = own_of((sums[:, : width // 2], sums[:, width // 2 :]))
@@ -576,17 +586,20 @@
     p0, p1 = sections
     normed0 = normed_mixer(p0, full_first)
     qkv0 = product(normed0, attention_first).astype(bf16)
-    heads0 = attend(qkv0, p0["bias"])
-    p0["output"], p1["output"] = to_sections(after(dense_own[:, 3 * width :], heads0))
-    cache0 = mixer(p0, qkv0, heads0, context)
-    cache0["normed"] = normed0
-    arrived0 = dispatch(p0, cache0["normed_feed"])
-    arrived_target = rows_from_all(target, route_full[1])
+    mixed0 = spread_heads(attend(qkv0, p0["bias"]))
+    p0["output"], p1["output"] = to_sections(after(dense_own[:, 3 * width :], mixed0))
+    cache0 = mixer(p0, qkv0, mixed0, context)
+    cache0["normed"], cache0["full"] = lambda _: normed0, full_first
+    p0["attention"] = attention_first
+    outgoing0 = [outgoing_of(p0, cache0["normed_feed"]), outgoing_of(p1, target)]
+    arrived0 = exchange(jnp.concatenate(outgoing0, axis=1))
+    arrived_target = arrived0[:, slots:].reshape(experts * slots, width)
+    arrived0 = arrived0[:, :slots].reshape(experts * slots, width)
     activated0, slope0, result0 = expert_call(
         forward_kernel, [arrived0], [], p0["weights"], 2, 1
     )
     returned0 = exchange(result0.reshape(experts, slots, width)).reshape(-1, width)
-    p0["qkv"], p1["qkv"] = to_sections(after(dense_own[:, : 3 * width], result0))
+    p0["qkv"], p1["qkv"] = to_sections(dense_own[:, : 3 * width])
     back0 = collect(p0, returned0)
     output0 = finish(cache0, back0)
 
@@ -594,28 +607,27 @@
     qkv1 = exchange_near(
         three_by_pairs(qkv1[:, :width], qkv1[:, width : 2 * width], qkv1[:, 2 * width :])
     ).reshape(SEQ_LEN, lanes)
-    cache1 = mixer(p1, qkv1, attend(qkv1, p1["bias"]), output0)
+    cache1 = mixer(p1, qkv1, spread_heads(attend(qkv1, p1["bias"])), output0)
     gate1 = cache1["gate"]
     gate_slots = sum(
         jnp.sum(p1["placings"][c].astype(f32) * gate1[:, c][None, :], axis=1) for c in range(2)
     )
-    outgoing1 = product(p1["placing"], cache1["normed_feed"]).astype(bf16)
+    outgoing1 = outgoing_of(p1, cache1["normed_feed"])
     arrived1, gate_slots = cut_line(exchange(with_line(outgoing1, gate_slots)))
     delta1 = (gate_slots * arrived_target.astype(f32)).astype(bf16)
-    full_second = lax.all_gather(
-        output0, "dp", axis=0, tiled=True, axis_index_groups=circles
-    )
+    full_second = gather_near(after(output0, arrived1))
     activated1, before1, result1, leaving1 = expert_call(
         both_kernel, [arrived1, delta1], [], p1["weights"], 2, 2
     )
-    cache1["normed"] = normed_mixer(p1, after(full_second, result1))
+    cache1["normed"] = lambda later: normed_mixer(p1, after(full_second, later))
+    leaving1 = after(leaving1, full_second)
     inner_gate = jnp.sum(arrived_target.astype(f32) * result1.astype(f32), axis=-1)
     home1, inner_gate = cut_line(exchange(with_line(leaving1, inner_gate)))
     home1 = collect(p1, home1)
     delta_gate1 = jnp.stack(
         [jnp.sum(p1["placings"][c].astype(f32) * inner_gate, axis=0) for c in range(2)], axis=1
     )
-    delta_in1, sums1, sum_output1, result1 = mixer_back(
+    delta_in1, sums1, sum_output1, result1, _ = mixer_back(
         p1, cache1, home1[0] + home1[1], delta_gate1, target.astype(f32), result1
     )
     back1 = collect(p1, exchange(result1.reshape(experts, slots, width)).reshape(-1, width))
@@ -636,11 +648,10 @@
     )
     home0 = collect(p0, exchange(leaving0.reshape(experts, slots, width)).reshape(-1, width))
     delta_gate0 = jnp.stack([jnp.sum(delta_out0 * back0[c], axis=-1) for c in range(2)], axis=1)
-    delta_in0, sums0, sum_output0, _ = mixer_back(
+    delta_in0, sums0, sum_output0, _, parts0 = mixer_back(
         p0, cache0, home0[0] + home0[1], delta_gate0, delta_out0, result0
     )
     output_half0 = half_columns(sum_output0).astype(bf16).reshape(devices, share, width // 2)
-    output_half0 = jnp.sum(exchange(output_half0).astype(f32), axis=0)
 
     operands0 = (activated0, arrived_delta, arrived0, before0)
     operands1 = (activated1, delta1, arrived1, before1)
@@ -652,11 +663,12 @@
     grad_inner = first_contract(joined[2], joined[3])
 
     mine, theirs = own_of((sums0, sums1))
-    sums = exchange((mine + swap(theirs.astype(bf16)).astype(f32)).astype(bf16)).astype(f32)
-    attention_sums = sums[:, :share].reshape(devices // span, span, share, 3, PAIR)
-    attention_sums = jnp.sum(attention_sums, axis=0)[:used]
-    attention_sums = jnp.transpose(attention_sums, (2, 1, 0, 3)).reshape(3, share, width)
-    small_sums = jnp.sum(sums[:, share:], axis=0).reshape(-1)
+    sums = (mine + swap(theirs.astype(bf16)).astype(f32)).astype(bf16)
+    sums = exchange(after(jnp.concatenate([sums, output_half0], axis=1), parts0))
+    attention_sums = add_pairs(sums, span, share)
+    sums = sums[:, share:].astype(f32)
+    output_half0 = jnp.sum(sums[:, small_rows:], axis=0)
+    small_sums = jnp.sum(sums[:, :small_rows], axis=0).reshape(-1)
     mine, theirs = own_of((output_half0, output_half1))
     other = swap(theirs)
     output_sums = jnp.concatenate(

time: 580 us -> 574 us (0.990)
  local copies, waits for them, and re-layouts: 44.3 us -> 58.1 us
  waiting for transfers between devices: 217 us -> 207 us
  other arithmetic: 58.1 us -> 48.7 us
    all_to_all x10 -> x9, waiting for transfers between devices: 101 us -> 129 us  [exchange(): return lax.all_to_all(value, 'dp', 0, 0, tiled=True)]
    all_gather x2 -> x0, waiting for transfers between devices: 20.4 us -> none  [the longest x1 20.4 us: rows_from_all(): lax.all_gather(jnp.concatenate([values, named], axis=1), 'dp', axis=0)]
    all_gather x1, waiting for transfers between devices: 31.6 us -> 13.2 us  [on_device(): lax.all_gather(jnp.concatenate([query_weight[0], key_weight[0], value_wei...]
    unnamed x256 -> x272, local copies, waits for them, and re-layouts: 13.9 us -> 19.3 us
    dot_general x6 -> x7, matrix products: 9.62 us -> 14.5 us  [last_contract(): lax.dot_general(left, right, (((1,), (1,)), ((), ())), preferred_element_...]
    all_to_all x10 -> x9, starting transfers between devices: 54.9 us -> 50.3 us  [exchange(): return lax.all_to_all(value, 'dp', 0, 0, tiled=True)]
    all_to_all x8 -> x9, waiting for transfers between devices: 60.3 us -> 57.2 us  [exchange_near(): lax.all_to_all(value, 'dp', 0, 0, tiled=True, axis_index_groups=circles)]
    dot_general x10 -> x11, matrix products: 11.1 us -> 12.5 us  [product(): return jnp.dot(left, right, preferred_element_type=f32)]
  transfers between devices with their start and end apart: 39 -> 37, of which waited for: 20 -> 21; matrix products, arithmetic and copies ran while one was open for 24% -> 23% of each run, Pallas kernels for 7% -> 12%
where the time goes in v3:
time: 574 us; the launch traced here: 563 us
  waiting for transfers between devices  207 us (36%)
  starting transfers between devices  98.1 us (17%)
  Pallas kernels  71.5 us (12%)
  matrix products  59.6 us (10%)
  local copies, waits for them, and re-layouts  58.1 us (10%)
  other arithmetic  48.7 us (8%)
  between operations  20.5 us (4%)
    all_to_all x9, waiting for transfers between devices, exchange(): return lax.all_to_all(value, 'dp', 0, 0, tiled=True)  129 us
    all_to_all x9, waiting for transfers between devices, exchange_near(): lax.all_to_all(value, 'dp', 0, 0, tiled=True, axis_index_groups=circles)  57.2 us
    all_to_all x9, starting transfers between devices, exchange(): return lax.all_to_all(value, 'dp', 0, 0, tiled=True)  50.3 us
    all_to_all x9, starting transfers between devices, exchange_near(): lax.all_to_all(value, 'dp', 0, 0, tiled=True, axis_index_groups=circles)  43.1 us
    pallas_call x3, Pallas kernels, expert_call(): pl.pallas_call(kernel, grid_spec=pltpu.PrefetchScalarGridSpec(num_scalar_...  42.8 us
    dot_general x16, matrix products, first_contract(): lax.dot_general(left, right, (((0,), (0,)), ((), ())), preferred_element_...  31.6 us
    unnamed x272, local copies, waits for them, and re-layouts  19.3 us
    pallas_call x2, Pallas kernels, attend_back(): pl.pallas_call(attend_back_kernel, out_shape=(jax.ShapeDtypeStruct((SEQ_L...  18.2 us
  transfers between devices with their start and end apart: 37, of which 21 were waited for; matrix products, arithmetic and copies ran while one was open for 23% of the time, Pallas kernels for 12%

profile of v3, /device:TPU:0, one launch (start us, length us, event | category | flops | bytes accessed | tf_op | source)
XLA Modules:
  0.0 563.3 jit_solution(3450468493654729651)
XLA Ops:
  11.9 6.3 %all-to-all-start = ((bf16[8,128,768]{2,1,0:T(8,128)(2,1)}), bf16[8,128,768]{2,1,0:T(8,128)(2,1)S(1)}, u32[]{:S(2)}, u32[]{:S(2)}) async-start(bf16[8,128,768]{2,1,0:T(8,128)(2,1)} %broadcast_in_dim.36), calls=%async_computation | async-start | bytes 3145728 | tf_op jit(solution)/shard_map/all_to_all | solution.py:378
  21.1 22.8 %all-to-all-done = bf16[8,128,768]{2,1,0:T(8,128)(2,1)S(1)} async-done(((bf16[8,128,768]{2,1,0:T(8,128)(2,1)}), bf16[8,128,768]{2,1,0:T(8,128)(2,1)S(1)}, u32[]{:S(2)}, u32[]{:S(2)}) %all-to-all-start) | async-done | bytes 1572896 | tf_op jit(solution)/shard_map/all_to_all | solution.py:378
  51.6 15.3 %all-to-all-done.1 = bf16[16,32,384]{2,1,0:T(8,128)(2,1)S(1)} async-done(((bf16[16,32,384]{2,1,0:T(8,128)(2,1)}), bf16[16,32,384]{2,1,0:T(8,128)(2,1)S(1)}, u32[]{:S(2)}, u32[]{:S(2)}) %all-to-all-start.1) | async-done | bytes 393248 | tf_op jit(solution)/shard_map/all_to_all | solution.py:375
  77.0 6.2 %all-to-all-start.2 = ((bf16[8,128,128]{1,2,0:T(8,128)(2,1)}), bf16[8,128,128]{1,2,0:T(8,128)(2,1)S(1)}, u32[]{:S(2)}, u32[]{:S(2)}) async-start(bf16[8,128,128]{1,2,0:T(8,128)(2,1)} %copy.134), calls=%async_computation.2 | async-start | bytes 524288 | tf_op jit(solution)/shard_map/all_to_all | solution.py:378
  84.3 12.7 %all-to-all-done.2 = bf16[8,128,128]{1,2,0:T(8,128)(2,1)S(1)} async-done(((bf16[8,128,128]{1,2,0:T(8,128)(2,1)}), bf16[8,128,128]{1,2,0:T(8,128)(2,1)S(1)}, u32[]{:S(2)}, u32[]{:S(2)}) %all-to-all-start.2) | async-done | bytes 262176 | tf_op jit(solution)/shard_map/all_to_all | solution.py:378
  98.3 13.2 %all-gather.2.cloned.1.call-done = bf16[768,3072]{1,0:T(8,128)(2,1)} async-done(((bf16[48,3072]{1,0:T(8,128)(2,1)}), bf16[768,3072]{1,0:T(8,128)(2,1)}) %all-gather.2.cloned.1.call-update) | async-done | bytes 4718608 | tf_op jit(solution)/shard_map/all_gather | solution.py:396
  130.8 29.9 %all-to-all-done.3 = bf16[16,64,768]{2,1,0:T(8,128)(2,1)} async-done(((bf16[16,64,768]{2,1,0:T(8,128)(2,1)}), bf16[16,64,768]{2,1,0:T(8,128)(2,1)}, u32[]{:S(2)}, u32[]{:S(2)}) %all-to-all-start.3) | async-done | bytes 1572896 | tf_op jit(solution)/shard_map/all_to_all | solution.py:375
  163.1 13.8 %shard_map.230 = (bf16[512,3072]{1,0:T(8,128)(2,1)S(1)}, bf16[512,3072]{1,0:T(8,128)(2,1)}, bf16[512,768]{1,0:T(8,128)(2,1)}) custom-call(s32[1]{0:T(128)} %bitcast.22.choice_ref, bf16[512,768]{1,0:T(8,128)(2,1)S(1)} %bitcast.271, bf16[768,3072]{1,0:T(8,128)(2,1)} %bitcast.352, bf16[768,3072]{1,0:T(8,128)(2,1)} %collective-permute-done.4.inner_1, ...), custom_call_target="tpu_custom_call" | custom-call | flops 14495514624 | bytes 15728640 | tf_op jit(solution)/shard_map/pallas_call | solution.py:279
  178.7 8.6 %all-to-all-start.4 = ((bf16[16,32,768]{2,1,0:T(8,128)(2,1)}), bf16[16,32,768]{2,1,0:T(8,128)(2,1)S(1)}, u32[]{:S(2)}, u32[]{:S(2)}) async-start(bf16[16,32,768]{2,1,0:T(8,128)(2,1)} %bitcast.30), calls=%async_computation.4 | async-start | bytes 1572864 | tf_op jit(solution)/shard_map/all_to_all | solution.py:375
  194.8 12.1 %all-to-all-done.4 = bf16[16,32,768]{2,1,0:T(8,128)(2,1)S(1)} async-done(((bf16[16,32,768]{2,1,0:T(8,128)(2,1)}), bf16[16,32,768]{2,1,0:T(8,128)(2,1)S(1)}, u32[]{:S(2)}, u32[]{:S(2)}) %all-to-all-start.4) | async-done | bytes 786464 | tf_op jit(solution)/shard_map/all_to_all | solution.py:375
  219.8 8.5 %all-to-all-done.5 = bf16[8,128,384]{2,1,0:T(8,128)(2,1)S(1)} async-done(((bf16[8,128,384]{2,1,0:T(8,128)(2,1)}), bf16[8,128,384]{2,1,0:T(8,128)(2,1)S(1)}, u32[]{:S(2)}, u32[]{:S(2)}) %all-to-all-start.5) | async-done | bytes 786464 | tf_op jit(solution)/shard_map/all_to_all | solution.py:378
  255.9 20.9 %all-to-all-done.7 = bf16[16,33,768]{2,1,0:T(8,128)(2,1)S(1)} async-done(((bf16[16,33,768]{2,1,0:T(8,128)(2,1)}), bf16[16,33,768]{2,1,0:T(8,128)(2,1)S(1)}, u32[]{:S(2)}, u32[]{:S(2)}) %all-to-all-start.7) | async-done | bytes 811040 | tf_op jit(solution)/shard_map/all_to_all | solution.py:375
  286.3 17.4 %shard_map.232 = (bf16[512,3072]{1,0:T(8,128)(2,1)}, bf16[512,3072]{1,0:T(8,128)(2,1)}, bf16[512,768]{1,0:T(8,128)(2,1)S(1)}, bf16[512,768]{1,0:T(8,128)(2,1)S(1)}) custom-call(s32[1]{0:T(128)} %bitcast.41.choice_ref, bf16[512,768]{1,0:T(8,128)(2,1)S(1)} %bitcast.270, bf16[512,768]{1,0:T(8,128)(2,1)S(1)} %fusion.22.delta_ref, bf16[768,3072]{1,0:T(8,128)(2,1)} %bitcast.353, ...), custom_call_target="tpu_custom_call" | custom-call | flops 28991029248 | bytes 15728640 | tf_op jit(solution)/shard_map/pallas_call | solution.py:279
  309.3 6.3 %all-to-all-start.9 = ((bf16[16,33,768]{2,1,0:T(8,128)(2,1)}), bf16[16,33,768]{2,1,0:T(8,128)(2,1)}, u32[]{:S(2)}, u32[]{:S(2)}) async-start(bf16[16,33,768]{2,1,0:T(8,128)(2,1)} %pad_maximum_fusion.4), calls=%async_computation.9 | async-start | bytes 1966080 | tf_op jit(solution)/shard_map/all_to_all | solution.py:375
  317.4 19.8 %all-to-all-done.9 = bf16[16,33,768]{2,1,0:T(8,128)(2,1)} async-done(((bf16[16,33,768]{2,1,0:T(8,128)(2,1)}), bf16[16,33,768]{2,1,0:T(8,128)(2,1)}, u32[]{:S(2)}, u32[]{:S(2)}) %all-to-all-start.9) | async-done | bytes 811040 | tf_op jit(solution)/shard_map/all_to_all | solution.py:375
  355.0 9.1 %shard_map.233 = (bf16[1024,384]{1,0:T(8,128)(2,1)S(1)}, f32[8,1280]{1,0:T(8,128)S(1)}) custom-call(bf16[1024,384]{1,0:T(8,128)(2,1)S(1)} %bitcast.273, f32[8,1280]{1,0:T(8,128)S(1)} %pad.70.bias_ref, bf16[1024,128]{1,0:T(8,128)(2,1)S(1)} %bitcast.276), custom_call_target="tpu_custom_call" | custom-call | flops 12884901888 | bytes 2097152 | tf_op jit(solution)/shard_map/pallas_call | solution.py:142
  405.8 8.3 %all-to-all-done.13 = bf16[16,32,768]{2,1,0:T(8,128)(2,1)S(1)} async-done(((bf16[16,32,768]{2,1,0:T(8,128)(2,1)}), bf16[16,32,768]{2,1,0:T(8,128)(2,1)S(1)}, u32[]{:S(2)}, u32[]{:S(2)}) %all-to-all-start.13) | async-done | bytes 786464 | tf_op jit(solution)/shard_map/all_to_all | solution.py:375
  419.1 11.7 %shard_map.234 = (bf16[512,3072]{1,0:T(8,128)(2,1)S(1)}, bf16[512,768]{1,0:T(8,128)(2,1)}) custom-call(s32[1]{0:T(128)} %bitcast.22.choice_ref, bf16[512,768]{1,0:T(8,128)(2,1)S(1)} %bitcast.268, bf16[512,3072]{1,0:T(8,128)(2,1)} %get-tuple-element.36.slope_ref, bf16[768,3072]{1,0:T(8,128)(2,1)} %bitcast.354, ...), custom_call_target="tpu_custom_call" | custom-call | flops 14495514624 | bytes 15728640 | tf_op jit(solution)/shard_map/pallas_call | solution.py:279
  432.4 7.3 %all-to-all-done.11 = bf16[16,32,768]{2,1,0:T(8,128)(2,1)} async-done(((bf16[16,32,768]{2,1,0:T(8,128)(2,1)}), bf16[16,32,768]{2,1,0:T(8,128)(2,1)}, u32[]{:S(2)}, u32[]{:S(2)}) %all-to-all-start.11) | async-done | bytes 786464 | tf_op jit(solution)/shard_map/all_to_all | solution.py:375
  455.1 10.4 %all-to-all-done.14 = bf16[16,32,768]{2,1,0:T(8,128)(2,1)S(1)} async-done(((bf16[16,32,768]{2,1,0:T(8,128)(2,1)}), bf16[16,32,768]{2,1,0:T(8,128)(2,1)S(1)}, u32[]{:S(2)}, u32[]{:S(2)}) %all-to-all-start.14) | async-done | bytes 786464 | tf_op jit(solution)/shard_map/all_to_all | solution.py:375
  480.7 9.1 %shard_map.235 = (bf16[1024,384]{1,0:T(8,128)(2,1)S(1)}, f32[8,1280]{1,0:T(8,128)S(1)}) custom-call(bf16[1024,384]{1,0:T(8,128)(2,1)S(1)} %copy-done.5, f32[8,1280]{1,0:T(8,128)S(1)} %pad.64.bias_ref, bf16[1024,128]{1,0:T(8,128)(2,1)S(1)} %bitcast.278), custom_call_target="tpu_custom_call" | custom-call | flops 12884901888 | bytes 2097152 | tf_op jit(solution)/shard_map/pallas_call | solution.py:142
  511.0 6.1 %all-to-all-start.17 = ((bf16[16,104,384]{2,1,0:T(8,128)(2,1)}), bf16[16,104,384]{2,1,0:T(8,128)(2,1)S(1)}, u32[]{:S(2)}, u32[]{:S(2)}) async-start(bf16[16,104,384]{2,1,0:T(8,128)(2,1)} %maximum_add_fusion), calls=%async_computation.17 | async-start | bytes 2555904 | tf_op jit(solution)/shard_map/all_to_all | solution.py:375
  517.2 10.0 %fusion.8 = f32[1,1,3072,768]{3,2,1,0:T(8,128)} fusion(bf16[512,3072]{1,0:T(8,128)(2,1)} %collective-permute-done.15, bf16[512,3072]{1,0:T(8,128)(2,1)} %get-tuple-element.121, bf16[512,768]{1,0:T(8,128)(2,1)} %collective-permute-done.16, bf16[512,768]{1,0:T(8,128)(2,1)} %get-tuple-element.125), kind=kOutput, calls=%fused_computation.8 | convolution fusion | flops 4847566848 | bytes 17301504 | tf_op jit(solution)/shard_map/dot_general | solution.py:31
  532.6 9.2 %fusion.11 = f32[1,1,768,3072]{3,2,1,0:T(8,128)} fusion(bf16[512,3072]{1,0:T(8,128)(2,1)} %collective-permute-done.14, bf16[512,3072]{1,0:T(8,128)(2,1)S(1)} %copy-done.35, bf16[512,768]{1,0:T(8,128)(2,1)} %collective-permute-done.13, bf16[512,768]{1,0:T(8,128)(2,1)S(1)} %copy-done.56), kind=kOutput, calls=%fused_computation.9 | convolution fusion | flops 4847566848 | bytes 17301504 | tf_op jit(solution)/shard_map/dot_general | solution.py:31
  (570 shorter events, 247.9 us)
Async XLA Ops:
  7.2 104.3 %all-gather.2.cloned.1.call-start = ((), (), s32[]{:S(2)}) async-start(), calls=%async_computation.19 | async-start | bytes 5013504 | tf_op jit(solution)/shard_map/all_gather | solution.py:396
  11.9 31.9 %all-to-all-start = ((bf16[8,128,768]{2,1,0:T(8,128)(2,1)}), bf16[8,128,768]{2,1,0:T(8,128)(2,1)S(1)}, u32[]{:S(2)}, u32[]{:S(2)}) async-start(bf16[8,128,768]{2,1,0:T(8,128)(2,1)} %broadcast_in_dim.36), calls=%async_computation | async-start | bytes 3145728 | tf_op jit(solution)/shard_map/all_to_all | solution.py:378
  44.8 22.1 %all-to-all-start.1 = ((bf16[16,32,384]{2,1,0:T(8,128)(2,1)}), bf16[16,32,384]{2,1,0:T(8,128)(2,1)S(1)}, u32[]{:S(2)}, u32[]{:S(2)}) async-start(bf16[16,32,384]{2,1,0:T(8,128)(2,1)} %copy.133), calls=%async_computation.1 | async-start | bytes 786432 | tf_op jit(solution)/shard_map/all_to_all | solution.py:375
  50.8 32.3 %collective-permute-start.3 = (s32[128,2]{1,0:T(8,128)S(1)}, s32[128,2]{1,0:T(8,128)S(1)}, u32[]{:S(2)}, u32[]{:S(2)}) collective-permute-start(s32[128,2]{1,0:T(8,128)S(1)} %select_bitcast_fusion.5), channel_id=1, source_target_pairs={{0,16},{16,0},{1,17},{17,1},{2,18},{18,2},{3,19},{19,3},{4,20},{20... | collective-permute-start | bytes 3080 | tf_op jit(solution)/shard_map/ppermute | solution.py:361
  50.9 112.2 %collective-permute-start.4 = (bf16[768,3072]{1,0:T(8,128)(2,1)}, bf16[768,3072]{1,0:T(8,128)(2,1)}, u32[]{:S(2)}, u32[]{:S(2)}) collective-permute-start(bf16[768,3072]{1,0:T(8,128)(2,1)} %bitcast.351), channel_id=1, source_target_pairs={{0,16},{16,0},{1,17},{17,1},{2,18},{18,2},{3,19},{19,3},{4,20},{20... | collective-permute-start | bytes 14155784 | tf_op jit(solution)/shard_map/ppermute | solution.py:361
  51.4 111.7 %collective-permute-start.5 = (bf16[3072,768]{1,0:T(8,128)(2,1)}, bf16[3072,768]{1,0:T(8,128)(2,1)}, u32[]{:S(2)}, u32[]{:S(2)}) collective-permute-start(bf16[3072,768]{1,0:T(8,128)(2,1)} %bitcast.355), channel_id=1, source_target_pairs={{0,16},{16,0},{1,17},{17,1},{2,18},{18,2},{3,19},{19,3},{4,20},{20... | collective-permute-start | bytes 14155784 | tf_op jit(solution)/shard_map/ppermute | solution.py:361
  77.0 20.1 %all-to-all-start.2 = ((bf16[8,128,128]{1,2,0:T(8,128)(2,1)}), bf16[8,128,128]{1,2,0:T(8,128)(2,1)S(1)}, u32[]{:S(2)}, u32[]{:S(2)}) async-start(bf16[8,128,128]{1,2,0:T(8,128)(2,1)} %copy.134), calls=%async_computation.2 | async-start | bytes 524288 | tf_op jit(solution)/shard_map/all_to_all | solution.py:378
  121.4 39.3 %all-to-all-start.3 = ((bf16[16,64,768]{2,1,0:T(8,128)(2,1)}), bf16[16,64,768]{2,1,0:T(8,128)(2,1)}, u32[]{:S(2)}, u32[]{:S(2)}) async-start(bf16[16,64,768]{2,1,0:T(8,128)(2,1)} %pad_maximum_fusion), calls=%async_computation.3 | async-start | bytes 3145728 | tf_op jit(solution)/shard_map/all_to_all | solution.py:375
  130.4 78.0 %collective-permute-start.6 = (bf16[768,2304]{1,0:T(8,128)(2,1)}, bf16[768,2304]{1,0:T(8,128)(2,1)}, u32[]{:S(2)}, u32[]{:S(2)}) collective-permute-start(bf16[768,2304]{1,0:T(8,128)(2,1)} %slice.314), channel_id=1, source_target_pairs={{0,16},{16,0},{1,17},{17,1},{2,18},{18,2},{3,19},{19,3},{4,20},{20... | collective-permute-start | bytes 10616840 | tf_op jit(solution)/shard_map/ppermute | solution.py:361
  178.7 28.2 %all-to-all-start.4 = ((bf16[16,32,768]{2,1,0:T(8,128)(2,1)}), bf16[16,32,768]{2,1,0:T(8,128)(2,1)S(1)}, u32[]{:S(2)}, u32[]{:S(2)}) async-start(bf16[16,32,768]{2,1,0:T(8,128)(2,1)} %bitcast.30), calls=%async_computation.4 | async-start | bytes 1572864 | tf_op jit(solution)/shard_map/all_to_all | solution.py:375
  252.2 24.5 %all-to-all-start.7 = ((bf16[16,33,768]{2,1,0:T(8,128)(2,1)}), bf16[16,33,768]{2,1,0:T(8,128)(2,1)S(1)}, u32[]{:S(2)}, u32[]{:S(2)}) async-start(bf16[16,33,768]{2,1,0:T(8,128)(2,1)} %pad_maximum_fusion.3), calls=%async_computation.7 | async-start | bytes 1966080 | tf_op jit(solution)/shard_map/all_to_all | solution.py:375
  281.5 23.7 %all-to-all-start.8 = ((bf16[8,128,768]{2,1,0:T(8,128)(2,1)}), bf16[8,128,768]{2,1,0:T(8,128)(2,1)}, u32[]{:S(2)}, u32[]{:S(2)}) async-start(bf16[8,128,768]{2,1,0:T(8,128)(2,1)} %broadcast_in_dim.38), calls=%async_computation.8 | async-start | bytes 3145728 | tf_op jit(solution)/shard_map/all_to_all | solution.py:378
  309.3 27.9 %all-to-all-start.9 = ((bf16[16,33,768]{2,1,0:T(8,128)(2,1)}), bf16[16,33,768]{2,1,0:T(8,128)(2,1)}, u32[]{:S(2)}, u32[]{:S(2)}) async-start(bf16[16,33,768]{2,1,0:T(8,128)(2,1)} %pad_maximum_fusion.4), calls=%async_computation.9 | async-start | bytes 1966080 | tf_op jit(solution)/shard_map/all_to_all | solution.py:375
  317.4 215.1 %collective-permute-start.13 = (bf16[512,768]{1,0:T(8,128)(2,1)}, bf16[512,768]{1,0:T(8,128)(2,1)}, u32[]{:S(2)}, u32[]{:S(2)}) collective-permute-start(bf16[512,768]{1,0:T(8,128)(2,1)} %get-tuple-element.128), channel_id=1, source_target_pairs={{0,16},{16,0},{1,17},{17,1},{2,18},{18,2},{3,19},{19,3},{4,20},{20... | collective-permute-start | bytes 2359304 | tf_op jit(solution)/shard_map/ppermute | solution.py:361
  354.4 162.8 %collective-permute-start.15 = (bf16[512,3072]{1,0:T(8,128)(2,1)}, bf16[512,3072]{1,0:T(8,128)(2,1)}, u32[]{:S(2)}, u32[]{:S(2)}) collective-permute-start(bf16[512,3072]{1,0:T(8,128)(2,1)} %get-tuple-element.122), channel_id=1, source_target_pairs={{0,16},{16,0},{1,17},{17,1},{2,18},{18,2},{3,19},{19,3},{4,20},{20... | collective-permute-start | bytes 9437192 | tf_op jit(solution)/shard_map/ppermute | solution.py:361
  372.9 30.4 %collective-permute-start.11 = (bf16[768,384]{1,0:T(8,128)(2,1)}, bf16[768,384]{1,0:T(8,128)(2,1)}, u32[]{:S(2)}, u32[]{:S(2)}) collective-permute-start(bf16[768,384]{1,0:T(8,128)(2,1)} %select_convert_fusion.1), channel_id=1, source_target_pairs={{0,16},{16,0},{1,17},{17,1},{2,18},{18,2},{3,19},{19,3},{4,20},{20... | collective-permute-start | bytes 1769480 | tf_op jit(solution)/shard_map/ppermute | solution.py:361
  391.0 23.1 %all-to-all-start.13 = ((bf16[16,32,768]{2,1,0:T(8,128)(2,1)}), bf16[16,32,768]{2,1,0:T(8,128)(2,1)S(1)}, u32[]{:S(2)}, u32[]{:S(2)}) async-start(bf16[16,32,768]{2,1,0:T(8,128)(2,1)} %bitcast.295), calls=%async_computation.13 | async-start | bytes 1572864 | tf_op jit(solution)/shard_map/all_to_all | solution.py:375
  395.2 156.5 %reduce-scatter.2.cloned.1.call-start = ((), (), s32[]{:S(2)}) async-start(), calls=%async_computation.20 | async-start | bytes 1253376 | tf_op jit(solution)/shard_map/reduce_scatter | solution.py:643
  414.1 25.6 %all-to-all-start.11 = ((bf16[16,32,768]{2,1,0:T(8,128)(2,1)}), bf16[16,32,768]{2,1,0:T(8,128)(2,1)}, u32[]{:S(2)}, u32[]{:S(2)}) async-start(bf16[16,32,768]{2,1,0:T(8,128)(2,1)} %bitcast.61), calls=%async_computation.11 | async-start | bytes 1572864 | tf_op jit(solution)/shard_map/all_to_all | solution.py:375
  439.7 25.8 %all-to-all-start.14 = ((bf16[16,32,768]{2,1,0:T(8,128)(2,1)}), bf16[16,32,768]{2,1,0:T(8,128)(2,1)S(1)}, u32[]{:S(2)}, u32[]{:S(2)}) async-start(bf16[16,32,768]{2,1,0:T(8,128)(2,1)} %bitcast.72), calls=%async_computation.14 | async-start | bytes 1572864 | tf_op jit(solution)/shard_map/all_to_all | solution.py:375
  454.8 62.3 %collective-permute-start.16 = (bf16[512,768]{1,0:T(8,128)(2,1)}, bf16[512,768]{1,0:T(8,128)(2,1)}, u32[]{:S(2)}, u32[]{:S(2)}) collective-permute-start(bf16[512,768]{1,0:T(8,128)(2,1)} %get-tuple-element.126), channel_id=1, source_target_pairs={{0,16},{16,0},{1,17},{17,1},{2,18},{18,2},{3,19},{19,3},{4,20},{20... | collective-permute-start | bytes 2359304 | tf_op jit(solution)/shard_map/ppermute | solution.py:361
  476.9 29.2 %collective-permute-start.10 = (bf16[768,384]{1,0:T(8,128)(2,1)}, bf16[768,384]{1,0:T(8,128)(2,1)}, u32[]{:S(2)}, u32[]{:S(2)}) collective-permute-start(bf16[768,384]{1,0:T(8,128)(2,1)} %select_convert_fusion.2), channel_id=1, source_target_pairs={{0,16},{16,0},{1,17},{17,1},{2,18},{18,2},{3,19},{19,3},{4,20},{20... | collective-permute-start | bytes 1769480 | tf_op jit(solution)/shard_map/ppermute | solution.py:361
  506.1 26.5 %collective-permute-start.14 = (bf16[512,3072]{1,0:T(8,128)(2,1)}, bf16[512,3072]{1,0:T(8,128)(2,1)}, u32[]{:S(2)}, u32[]{:S(2)}) collective-permute-start(bf16[512,3072]{1,0:T(8,128)(2,1)} %get-tuple-element.124), channel_id=1, source_target_pairs={{0,16},{16,0},{1,17},{17,1},{2,18},{18,2},{3,19},{19,3},{4,20},{20... | collective-permute-start | bytes 9437192 | tf_op jit(solution)/shard_map/ppermute | solution.py:361
  511.0 36.3 %all-to-all-start.17 = ((bf16[16,104,384]{2,1,0:T(8,128)(2,1)}), bf16[16,104,384]{2,1,0:T(8,128)(2,1)S(1)}, u32[]{:S(2)}, u32[]{:S(2)}) async-start(bf16[16,104,384]{2,1,0:T(8,128)(2,1)} %maximum_add_fusion), calls=%async_computation.17 | async-start | bytes 2555904 | tf_op jit(solution)/shard_map/all_to_all | solution.py:375
  (142 other events, 1449.8 us)
Sparse Core Ops, SparseCore 0:
  11.4 100.0 all-gather.1
  405.8 145.8 reduce-scatter.1

commit v4 on v3

--- a/solution.py
+++ b/solution.py
@@ -199,18 +199,13 @@
 def forward_kernel(
     choice_ref, in_ref, inner_0, inner_1, outer_0, outer_1, act_ref, slope_ref, out_ref, total
 ):
-    values = in_ref[...]
-    inner = parts_of(pick(choice_ref, (inner_0, inner_1)), 1)
-    outer = parts_of(pick(choice_ref, (outer_0, outer_1)), 0)
-    befores = [product(values, part) for part in inner]
-    value = 0.0
-    for i, before in enumerate(befores):
-        act, slope = gelu_parts(before)
-        act = act.astype(bf16)
-        act_ref[:, PART * i : PART * (i + 1)] = act
-        slope_ref[:, PART * i : PART * (i + 1)] = slope.astype(bf16)
-        value = value + product(act, outer[i])
-    add_product(total, value)
+    inner = pick(choice_ref, (inner_0, inner_1))
+    outer = pick(choice_ref, (outer_0, outer_1))
+    act, slope = gelu_parts(product(in_ref[...], inner))
+    act = act.astype(bf16)
+    act_ref[...] = act
+    slope_ref[...] = slope.astype(bf16)
+    add_product(total, product(act, outer))
 
     @pl.when(pl.program_id(0) == pl.num_programs(0) - 1)
     def _():
@@ -620,8 +615,8 @@
         both_kernel, [arrived1, delta1], [], p1["weights"], 2, 2
     )
     cache1["normed"] = lambda later: normed_mixer(p1, after(full_second, later))
-    leaving1 = after(leaving1, full_second)
     inner_gate = jnp.sum(arrived_target.astype(f32) * result1.astype(f32), axis=-1)
+    inner_gate = after(inner_gate, full_second)
     home1, inner_gate = cut_line(exchange(with_line(leaving1, inner_gate)))
     home1 = collect(p1, home1)
     delta_gate1 = jnp.stack(

time: 574 us -> 572 us (level)
    unnamed x272 -> x236, local copies, waits for them, and re-layouts: 19.3 us -> 20.5 us
  transfers between devices with their start and end apart: 37 -> 37, of which waited for: 21 -> 22; matrix products, arithmetic and copies ran while one was open for 23% -> 23% of each run, Pallas kernels for 12% -> 12%
where the time goes in v4:
time: 572 us; the launch traced here: 562 us
  waiting for transfers between devices  209 us (37%)
  starting transfers between devices  97.8 us (17%)
  Pallas kernels  71.3 us (12%)
  local copies, waits for them, and re-layouts  59 us (10%)
  matrix products  57.4 us (10%)
  other arithmetic  47.1 us (8%)
  between operations  20.3 us (4%)
    all_to_all x9, waiting for transfers between devices, exchange(): return lax.all_to_all(value, 'dp', 0, 0, tiled=True)  133 us
    all_to_all x9, waiting for transfers between devices, exchange_near(): lax.all_to_all(value, 'dp', 0, 0, tiled=True, axis_index_groups=circles)  55.5 us
    all_to_all x9, starting transfers between devices, exchange(): return lax.all_to_all(value, 'dp', 0, 0, tiled=True)  49.8 us
    all_to_all x9, starting transfers between devices, exchange_near(): lax.all_to_all(value, 'dp', 0, 0, tiled=True, axis_index_groups=circles)  43.3 us
    pallas_call x3, Pallas kernels, expert_call(): pl.pallas_call(kernel, grid_spec=pltpu.PrefetchScalarGridSpec(num_scalar_...  42.6 us
    dot_general x16, matrix products, first_contract(): lax.dot_general(left, right, (((0,), (0,)), ((), ())), preferred_element_...  28.4 us
    unnamed x236, local copies, waits for them, and re-layouts  20.5 us
    pallas_call x2, Pallas kernels, attend_back(): pl.pallas_call(attend_back_kernel, out_shape=(jax.ShapeDtypeStruct((SEQ_L...  18.3 us
  transfers between devices with their start and end apart: 37, of which 22 were waited for; matrix products, arithmetic and copies ran while one was open for 23% of the time, Pallas kernels for 12%

profile of v4, /device:TPU:0, one launch (start us, length us, event | category | flops | bytes accessed | tf_op | source)
XLA Modules:
  0.0 561.6 jit_solution(4320074015636177292)
XLA Ops:
  12.6 6.3 %all-to-all-start = ((bf16[8,128,768]{2,1,0:T(8,128)(2,1)}), bf16[8,128,768]{2,1,0:T(8,128)(2,1)S(1)}, u32[]{:S(2)}, u32[]{:S(2)}) async-start(bf16[8,128,768]{2,1,0:T(8,128)(2,1)} %broadcast_in_dim.36), calls=%async_computation | async-start | bytes 3145728 | tf_op jit(solution)/shard_map/all_to_all | solution.py:373
  21.7 22.8 %all-to-all-done = bf16[8,128,768]{2,1,0:T(8,128)(2,1)S(1)} async-done(((bf16[8,128,768]{2,1,0:T(8,128)(2,1)}), bf16[8,128,768]{2,1,0:T(8,128)(2,1)S(1)}, u32[]{:S(2)}, u32[]{:S(2)}) %all-to-all-start) | async-done | bytes 1572896 | tf_op jit(solution)/shard_map/all_to_all | solution.py:373
  52.3 15.3 %all-to-all-done.1 = bf16[16,32,384]{2,1,0:T(8,128)(2,1)S(1)} async-done(((bf16[16,32,384]{2,1,0:T(8,128)(2,1)}), bf16[16,32,384]{2,1,0:T(8,128)(2,1)S(1)}, u32[]{:S(2)}, u32[]{:S(2)}) %all-to-all-start.1) | async-done | bytes 393248 | tf_op jit(solution)/shard_map/all_to_all | solution.py:370
  78.8 6.2 %all-to-all-start.2 = ((bf16[8,128,128]{1,2,0:T(8,128)(2,1)}), bf16[8,128,128]{1,2,0:T(8,128)(2,1)S(1)}, u32[]{:S(2)}, u32[]{:S(2)}) async-start(bf16[8,128,128]{1,2,0:T(8,128)(2,1)} %copy.134), calls=%async_computation.2 | async-start | bytes 524288 | tf_op jit(solution)/shard_map/all_to_all | solution.py:373
  86.2 11.7 %all-to-all-done.2 = bf16[8,128,128]{1,2,0:T(8,128)(2,1)S(1)} async-done(((bf16[8,128,128]{1,2,0:T(8,128)(2,1)}), bf16[8,128,128]{1,2,0:T(8,128)(2,1)S(1)}, u32[]{:S(2)}, u32[]{:S(2)}) %all-to-all-start.2) | async-done | bytes 262176 | tf_op jit(solution)/shard_map/all_to_all | solution.py:373
  99.7 12.3 %all-gather.2.cloned.1.call-done = bf16[768,3072]{1,0:T(8,128)(2,1)} async-done(((bf16[48,3072]{1,0:T(8,128)(2,1)}), bf16[768,3072]{1,0:T(8,128)(2,1)}) %all-gather.2.cloned.1.call-update) | async-done | bytes 4718608 | tf_op jit(solution)/shard_map/all_gather | solution.py:391
  130.6 29.7 %all-to-all-done.3 = bf16[16,64,768]{2,1,0:T(8,128)(2,1)} async-done(((bf16[16,64,768]{2,1,0:T(8,128)(2,1)}), bf16[16,64,768]{2,1,0:T(8,128)(2,1)}, u32[]{:S(2)}, u32[]{:S(2)}) %all-to-all-start.3) | async-done | bytes 1572896 | tf_op jit(solution)/shard_map/all_to_all | solution.py:370
  162.8 13.7 %shard_map.230 = (bf16[512,3072]{1,0:T(8,128)(2,1)S(1)}, bf16[512,3072]{1,0:T(8,128)(2,1)}, bf16[512,768]{1,0:T(8,128)(2,1)}) custom-call(s32[1]{0:T(128)} %bitcast.22.choice_ref, bf16[512,768]{1,0:T(8,128)(2,1)S(1)} %bitcast.271, bf16[768,3072]{1,0:T(8,128)(2,1)} %bitcast.354, bf16[768,3072]{1,0:T(8,128)(2,1)} %collective-permute-done.4.inner_1, ...), custom_call_target="tpu_custom_call" | custom-call | flops 14495514624 | bytes 15728640 | tf_op jit(solution)/shard_map/pallas_call | solution.py:274
  178.2 8.9 %all-to-all-start.4 = ((bf16[16,32,768]{2,1,0:T(8,128)(2,1)}), bf16[16,32,768]{2,1,0:T(8,128)(2,1)S(1)}, u32[]{:S(2)}, u32[]{:S(2)}) async-start(bf16[16,32,768]{2,1,0:T(8,128)(2,1)} %bitcast.30), calls=%async_computation.4 | async-start | bytes 1572864 | tf_op jit(solution)/shard_map/all_to_all | solution.py:370
  194.0 12.8 %all-to-all-done.4 = bf16[16,32,768]{2,1,0:T(8,128)(2,1)S(1)} async-done(((bf16[16,32,768]{2,1,0:T(8,128)(2,1)}), bf16[16,32,768]{2,1,0:T(8,128)(2,1)S(1)}, u32[]{:S(2)}, u32[]{:S(2)}) %all-to-all-start.4) | async-done | bytes 786464 | tf_op jit(solution)/shard_map/all_to_all | solution.py:370
  219.6 8.5 %all-to-all-done.5 = bf16[8,128,384]{2,1,0:T(8,128)(2,1)S(1)} async-done(((bf16[8,128,384]{2,1,0:T(8,128)(2,1)}), bf16[8,128,384]{2,1,0:T(8,128)(2,1)S(1)}, u32[]{:S(2)}, u32[]{:S(2)}) %all-to-all-start.5) | async-done | bytes 786464 | tf_op jit(solution)/shard_map/all_to_all | solution.py:373
  253.7 21.3 %all-to-all-done.7 = bf16[16,33,768]{2,1,0:T(8,128)(2,1)S(1)} async-done(((bf16[16,33,768]{2,1,0:T(8,128)(2,1)}), bf16[16,33,768]{2,1,0:T(8,128)(2,1)S(1)}, u32[]{:S(2)}, u32[]{:S(2)}) %all-to-all-start.7) | async-done | bytes 811040 | tf_op jit(solution)/shard_map/all_to_all | solution.py:370
  284.6 17.4 %shard_map.232 = (bf16[512,3072]{1,0:T(8,128)(2,1)}, bf16[512,3072]{1,0:T(8,128)(2,1)}, bf16[512,768]{1,0:T(8,128)(2,1)S(1)}, bf16[512,768]{1,0:T(8,128)(2,1)S(1)}) custom-call(s32[1]{0:T(128)} %bitcast.41.choice_ref, bf16[512,768]{1,0:T(8,128)(2,1)S(1)} %bitcast.270, bf16[512,768]{1,0:T(8,128)(2,1)S(1)} %fusion.22.delta_ref, bf16[768,3072]{1,0:T(8,128)(2,1)} %bitcast.355, ...), custom_call_target="tpu_custom_call" | custom-call | flops 28991029248 | bytes 15728640 | tf_op jit(solution)/shard_map/pallas_call | solution.py:274
  313.6 21.0 %all-to-all-done.9 = bf16[16,33,768]{2,1,0:T(8,128)(2,1)} async-done(((bf16[16,33,768]{2,1,0:T(8,128)(2,1)}), bf16[16,33,768]{2,1,0:T(8,128)(2,1)}, u32[]{:S(2)}, u32[]{:S(2)}) %all-to-all-start.9) | async-done | bytes 811040 | tf_op jit(solution)/shard_map/all_to_all | solution.py:370
  346.8 6.0 %broadcast_select_fusion.2 = (bf16[512,3072]{1,0:T(8,128)(2,1)}, bf16[512,3072]{1,0:T(8,128)(2,1)}) fusion(bf16[512,3072]{1,0:T(8,128)(2,1)} %copy-done, bf16[512,3072]{1,0:T(8,128)(2,1)} %get-tuple-element.47, pred[]{:T(512)S(6)} %eq.158), kind=kLoop, calls=%fused_computation.25 | loop fusion | flops 3145728 | bytes 12582913 | tf_op jit(solution)/shard_map/jit(_where)/select_n | solution.py:363
  353.4 9.1 %shard_map.233 = (bf16[1024,384]{1,0:T(8,128)(2,1)S(1)}, f32[8,1280]{1,0:T(8,128)S(1)}) custom-call(bf16[1024,384]{1,0:T(8,128)(2,1)S(1)} %bitcast.274, f32[8,1280]{1,0:T(8,128)S(1)} %pad.70.bias_ref, bf16[1024,128]{1,0:T(8,128)(2,1)S(1)} %bitcast.277), custom_call_target="tpu_custom_call" | custom-call | flops 12884901888 | bytes 2097152 | tf_op jit(solution)/shard_map/pallas_call | solution.py:142
  404.5 8.5 %all-to-all-done.13 = bf16[16,32,768]{2,1,0:T(8,128)(2,1)S(1)} async-done(((bf16[16,32,768]{2,1,0:T(8,128)(2,1)}), bf16[16,32,768]{2,1,0:T(8,128)(2,1)S(1)}, u32[]{:S(2)}, u32[]{:S(2)}) %all-to-all-start.13) | async-done | bytes 786464 | tf_op jit(solution)/shard_map/all_to_all | solution.py:370
  417.9 11.6 %shard_map.234 = (bf16[512,3072]{1,0:T(8,128)(2,1)S(1)}, bf16[512,768]{1,0:T(8,128)(2,1)}) custom-call(s32[1]{0:T(128)} %bitcast.22.choice_ref, bf16[512,768]{1,0:T(8,128)(2,1)S(1)} %bitcast.268, bf16[512,3072]{1,0:T(8,128)(2,1)} %get-tuple-element.36.slope_ref, bf16[768,3072]{1,0:T(8,128)(2,1)} %bitcast.356, ...), custom_call_target="tpu_custom_call" | custom-call | flops 14495514624 | bytes 15728640 | tf_op jit(solution)/shard_map/pallas_call | solution.py:274
  431.1 7.3 %all-to-all-done.11 = bf16[16,32,768]{2,1,0:T(8,128)(2,1)S(1)} async-done(((bf16[16,32,768]{2,1,0:T(8,128)(2,1)}), bf16[16,32,768]{2,1,0:T(8,128)(2,1)S(1)}, u32[]{:S(2)}, u32[]{:S(2)}) %all-to-all-start.11) | async-done | bytes 786464 | tf_op jit(solution)/shard_map/all_to_all | solution.py:370
  452.0 12.5 %all-to-all-done.14 = bf16[16,32,768]{2,1,0:T(8,128)(2,1)S(1)} async-done(((bf16[16,32,768]{2,1,0:T(8,128)(2,1)}), bf16[16,32,768]{2,1,0:T(8,128)(2,1)S(1)}, u32[]{:S(2)}, u32[]{:S(2)}) %all-to-all-start.14) | async-done | bytes 786464 | tf_op jit(solution)/shard_map/all_to_all | solution.py:370
  479.5 9.2 %shard_map.235 = (bf16[1024,384]{1,0:T(8,128)(2,1)S(1)}, f32[8,1280]{1,0:T(8,128)S(1)}) custom-call(bf16[1024,384]{1,0:T(8,128)(2,1)S(1)} %copy-done.6, f32[8,1280]{1,0:T(8,128)S(1)} %pad.64.bias_ref, bf16[1024,128]{1,0:T(8,128)(2,1)S(1)} %bitcast.279), custom_call_target="tpu_custom_call" | custom-call | flops 12884901888 | bytes 2097152 | tf_op jit(solution)/shard_map/pallas_call | solution.py:142
  509.1 6.2 %all-to-all-start.17 = ((bf16[16,104,384]{2,1,0:T(8,128)(2,1)}), bf16[16,104,384]{2,1,0:T(8,128)(2,1)S(1)}, u32[]{:S(2)}, u32[]{:S(2)}) async-start(bf16[16,104,384]{2,1,0:T(8,128)(2,1)} %maximum_add_fusion), calls=%async_computation.17 | async-start | bytes 2555904 | tf_op jit(solution)/shard_map/all_to_all | solution.py:370
  515.3 10.0 %fusion.8 = f32[1,1,3072,768]{3,2,1,0:T(8,128)} fusion(bf16[512,3072]{1,0:T(8,128)(2,1)} %collective-permute-done.15, bf16[512,3072]{1,0:T(8,128)(2,1)} %get-tuple-element.121, bf16[512,768]{1,0:T(8,128)(2,1)} %collective-permute-done.16, bf16[512,768]{1,0:T(8,128)(2,1)} %get-tuple-element.125), kind=kOutput, calls=%fused_computation.8 | convolution fusion | flops 4847566848 | bytes 17301504 | tf_op jit(solution)/shard_map/dot_general | solution.py:31
  530.7 9.2 %fusion.11 = f32[1,1,768,3072]{3,2,1,0:T(8,128)} fusion(bf16[512,3072]{1,0:T(8,128)(2,1)} %collective-permute-done.14, bf16[512,3072]{1,0:T(8,128)(2,1)S(1)} %copy-done.38, bf16[512,768]{1,0:T(8,128)(2,1)} %collective-permute-done.13, bf16[512,768]{1,0:T(8,128)(2,1)S(1)} %copy-done.56), kind=kOutput, calls=%fused_computation.9 | convolution fusion | flops 4847566848 | bytes 17301504 | tf_op jit(solution)/shard_map/dot_general | solution.py:31
  (534 shorter events, 244.1 us)
Async XLA Ops:
  7.2 104.9 %all-gather.2.cloned.1.call-start = ((), (), s32[]{:S(2)}) async-start(), calls=%async_computation.19 | async-start | bytes 5013504 | tf_op jit(solution)/shard_map/all_gather | solution.py:391
  12.6 31.9 %all-to-all-start = ((bf16[8,128,768]{2,1,0:T(8,128)(2,1)}), bf16[8,128,768]{2,1,0:T(8,128)(2,1)S(1)}, u32[]{:S(2)}, u32[]{:S(2)}) async-start(bf16[8,128,768]{2,1,0:T(8,128)(2,1)} %broadcast_in_dim.36), calls=%async_computation | async-start | bytes 3145728 | tf_op jit(solution)/shard_map/all_to_all | solution.py:373
  45.4 22.2 %all-to-all-start.1 = ((bf16[16,32,384]{2,1,0:T(8,128)(2,1)}), bf16[16,32,384]{2,1,0:T(8,128)(2,1)S(1)}, u32[]{:S(2)}, u32[]{:S(2)}) async-start(bf16[16,32,384]{2,1,0:T(8,128)(2,1)} %copy.133), calls=%async_computation.1 | async-start | bytes 786432 | tf_op jit(solution)/shard_map/all_to_all | solution.py:370
  51.6 33.5 %collective-permute-start.3 = (s32[128,2]{1,0:T(8,128)S(1)}, s32[128,2]{1,0:T(8,128)S(1)}, u32[]{:S(2)}, u32[]{:S(2)}) collective-permute-start(s32[128,2]{1,0:T(8,128)S(1)} %select_bitcast_fusion.5), channel_id=1, source_target_pairs={{0,16},{16,0},{1,17},{17,1},{2,18},{18,2},{3,19},{19,3},{4,20},{20... | collective-permute-start | bytes 3080 | tf_op jit(solution)/shard_map/ppermute | solution.py:356
  51.6 111.1 %collective-permute-start.4 = (bf16[768,3072]{1,0:T(8,128)(2,1)}, bf16[768,3072]{1,0:T(8,128)(2,1)}, u32[]{:S(2)}, u32[]{:S(2)}) collective-permute-start(bf16[768,3072]{1,0:T(8,128)(2,1)} %bitcast.353), channel_id=1, source_target_pairs={{0,16},{16,0},{1,17},{17,1},{2,18},{18,2},{3,19},{19,3},{4,20},{20... | collective-permute-start | bytes 14155784 | tf_op jit(solution)/shard_map/ppermute | solution.py:356
  52.1 110.6 %collective-permute-start.5 = (bf16[3072,768]{1,0:T(8,128)(2,1)}, bf16[3072,768]{1,0:T(8,128)(2,1)}, u32[]{:S(2)}, u32[]{:S(2)}) collective-permute-start(bf16[3072,768]{1,0:T(8,128)(2,1)} %bitcast.357), channel_id=1, source_target_pairs={{0,16},{16,0},{1,17},{17,1},{2,18},{18,2},{3,19},{19,3},{4,20},{20... | collective-permute-start | bytes 14155784 | tf_op jit(solution)/shard_map/ppermute | solution.py:356
  78.8 19.0 %all-to-all-start.2 = ((bf16[8,128,128]{1,2,0:T(8,128)(2,1)}), bf16[8,128,128]{1,2,0:T(8,128)(2,1)S(1)}, u32[]{:S(2)}, u32[]{:S(2)}) async-start(bf16[8,128,128]{1,2,0:T(8,128)(2,1)} %copy.134), calls=%async_computation.2 | async-start | bytes 524288 | tf_op jit(solution)/shard_map/all_to_all | solution.py:373
  121.2 39.1 %all-to-all-start.3 = ((bf16[16,64,768]{2,1,0:T(8,128)(2,1)}), bf16[16,64,768]{2,1,0:T(8,128)(2,1)}, u32[]{:S(2)}, u32[]{:S(2)}) async-start(bf16[16,64,768]{2,1,0:T(8,128)(2,1)} %pad_maximum_fusion), calls=%async_computation.3 | async-start | bytes 3145728 | tf_op jit(solution)/shard_map/all_to_all | solution.py:370
  130.1 78.1 %collective-permute-start.6 = (bf16[768,2304]{1,0:T(8,128)(2,1)}, bf16[768,2304]{1,0:T(8,128)(2,1)}, u32[]{:S(2)}, u32[]{:S(2)}) collective-permute-start(bf16[768,2304]{1,0:T(8,128)(2,1)} %slice.314), channel_id=1, source_target_pairs={{0,16},{16,0},{1,17},{17,1},{2,18},{18,2},{3,19},{19,3},{4,20},{20... | collective-permute-start | bytes 10616840 | tf_op jit(solution)/shard_map/ppermute | solution.py:356
  178.2 28.6 %all-to-all-start.4 = ((bf16[16,32,768]{2,1,0:T(8,128)(2,1)}), bf16[16,32,768]{2,1,0:T(8,128)(2,1)S(1)}, u32[]{:S(2)}, u32[]{:S(2)}) async-start(bf16[16,32,768]{2,1,0:T(8,128)(2,1)} %bitcast.30), calls=%async_computation.4 | async-start | bytes 1572864 | tf_op jit(solution)/shard_map/all_to_all | solution.py:370
  250.0 25.0 %all-to-all-start.7 = ((bf16[16,33,768]{2,1,0:T(8,128)(2,1)}), bf16[16,33,768]{2,1,0:T(8,128)(2,1)S(1)}, u32[]{:S(2)}, u32[]{:S(2)}) async-start(bf16[16,33,768]{2,1,0:T(8,128)(2,1)} %pad_maximum_fusion.3), calls=%async_computation.7 | async-start | bytes 1966080 | tf_op jit(solution)/shard_map/all_to_all | solution.py:370
  279.7 23.3 %all-to-all-start.8 = ((bf16[8,128,768]{2,1,0:T(8,128)(2,1)}), bf16[8,128,768]{2,1,0:T(8,128)(2,1)}, u32[]{:S(2)}, u32[]{:S(2)}) async-start(bf16[8,128,768]{2,1,0:T(8,128)(2,1)} %broadcast_in_dim.38), calls=%async_computation.8 | async-start | bytes 3145728 | tf_op jit(solution)/shard_map/all_to_all | solution.py:373
  306.1 28.4 %all-to-all-start.9 = ((bf16[16,33,768]{2,1,0:T(8,128)(2,1)}), bf16[16,33,768]{2,1,0:T(8,128)(2,1)}, u32[]{:S(2)}, u32[]{:S(2)}) async-start(bf16[16,33,768]{2,1,0:T(8,128)(2,1)} %pad_maximum_fusion.4), calls=%async_computation.9 | async-start | bytes 1966080 | tf_op jit(solution)/shard_map/all_to_all | solution.py:370
  313.6 217.1 %collective-permute-start.13 = (bf16[512,768]{1,0:T(8,128)(2,1)}, bf16[512,768]{1,0:T(8,128)(2,1)}, u32[]{:S(2)}, u32[]{:S(2)}) collective-permute-start(bf16[512,768]{1,0:T(8,128)(2,1)} %get-tuple-element.128), channel_id=1, source_target_pairs={{0,16},{16,0},{1,17},{17,1},{2,18},{18,2},{3,19},{19,3},{4,20},{20... | collective-permute-start | bytes 2359304 | tf_op jit(solution)/shard_map/ppermute | solution.py:356
  352.8 162.5 %collective-permute-start.15 = (bf16[512,3072]{1,0:T(8,128)(2,1)}, bf16[512,3072]{1,0:T(8,128)(2,1)}, u32[]{:S(2)}, u32[]{:S(2)}) collective-permute-start(bf16[512,3072]{1,0:T(8,128)(2,1)} %get-tuple-element.122), channel_id=1, source_target_pairs={{0,16},{16,0},{1,17},{17,1},{2,18},{18,2},{3,19},{19,3},{4,20},{20... | collective-permute-start | bytes 9437192 | tf_op jit(solution)/shard_map/ppermute | solution.py:356
  372.5 29.6 %collective-permute-start.11 = (bf16[768,384]{1,0:T(8,128)(2,1)}, bf16[768,384]{1,0:T(8,128)(2,1)}, u32[]{:S(2)}, u32[]{:S(2)}) collective-permute-start(bf16[768,384]{1,0:T(8,128)(2,1)} %select_convert_fusion.1), channel_id=1, source_target_pairs={{0,16},{16,0},{1,17},{17,1},{2,18},{18,2},{3,19},{19,3},{4,20},{20... | collective-permute-start | bytes 1769480 | tf_op jit(solution)/shard_map/ppermute | solution.py:356
  390.0 23.0 %all-to-all-start.13 = ((bf16[16,32,768]{2,1,0:T(8,128)(2,1)}), bf16[16,32,768]{2,1,0:T(8,128)(2,1)S(1)}, u32[]{:S(2)}, u32[]{:S(2)}) async-start(bf16[16,32,768]{2,1,0:T(8,128)(2,1)} %bitcast.297), calls=%async_computation.13 | async-start | bytes 1572864 | tf_op jit(solution)/shard_map/all_to_all | solution.py:370
  394.1 156.0 %reduce-scatter.2.cloned.1.call-start = ((), (), s32[]{:S(2)}) async-start(), calls=%async_computation.20 | async-start | bytes 1253376 | tf_op jit(solution)/shard_map/reduce_scatter | solution.py:638
  413.0 25.5 %all-to-all-start.11 = ((bf16[16,32,768]{2,1,0:T(8,128)(2,1)}), bf16[16,32,768]{2,1,0:T(8,128)(2,1)S(1)}, u32[]{:S(2)}, u32[]{:S(2)}) async-start(bf16[16,32,768]{2,1,0:T(8,128)(2,1)} %bitcast.61), calls=%async_computation.11 | async-start | bytes 1572864 | tf_op jit(solution)/shard_map/all_to_all | solution.py:370
  438.4 26.0 %all-to-all-start.14 = ((bf16[16,32,768]{2,1,0:T(8,128)(2,1)}), bf16[16,32,768]{2,1,0:T(8,128)(2,1)S(1)}, u32[]{:S(2)}, u32[]{:S(2)}) async-start(bf16[16,32,768]{2,1,0:T(8,128)(2,1)} %bitcast.72), calls=%async_computation.14 | async-start | bytes 1572864 | tf_op jit(solution)/shard_map/all_to_all | solution.py:370
  451.8 63.5 %collective-permute-start.16 = (bf16[512,768]{1,0:T(8,128)(2,1)}, bf16[512,768]{1,0:T(8,128)(2,1)}, u32[]{:S(2)}, u32[]{:S(2)}) collective-permute-start(bf16[512,768]{1,0:T(8,128)(2,1)} %get-tuple-element.126), channel_id=1, source_target_pairs={{0,16},{16,0},{1,17},{17,1},{2,18},{18,2},{3,19},{19,3},{4,20},{20... | collective-permute-start | bytes 2359304 | tf_op jit(solution)/shard_map/ppermute | solution.py:356
  475.7 28.2 %collective-permute-start.10 = (bf16[768,384]{1,0:T(8,128)(2,1)}, bf16[768,384]{1,0:T(8,128)(2,1)}, u32[]{:S(2)}, u32[]{:S(2)}) collective-permute-start(bf16[768,384]{1,0:T(8,128)(2,1)} %select_convert_fusion.2), channel_id=1, source_target_pairs={{0,16},{16,0},{1,17},{17,1},{2,18},{18,2},{3,19},{19,3},{4,20},{20... | collective-permute-start | bytes 1769480 | tf_op jit(solution)/shard_map/ppermute | solution.py:356
  503.9 26.8 %collective-permute-start.14 = (bf16[512,3072]{1,0:T(8,128)(2,1)}, bf16[512,3072]{1,0:T(8,128)(2,1)}, u32[]{:S(2)}, u32[]{:S(2)}) collective-permute-start(bf16[512,3072]{1,0:T(8,128)(2,1)} %get-tuple-element.124), channel_id=1, source_target_pairs={{0,16},{16,0},{1,17},{17,1},{2,18},{18,2},{3,19},{19,3},{4,20},{20... | collective-permute-start | bytes 9437192 | tf_op jit(solution)/shard_map/ppermute | solution.py:356
  509.1 36.4 %all-to-all-start.17 = ((bf16[16,104,384]{2,1,0:T(8,128)(2,1)}), bf16[16,104,384]{2,1,0:T(8,128)(2,1)S(1)}, u32[]{:S(2)}, u32[]{:S(2)}) async-start(bf16[16,104,384]{2,1,0:T(8,128)(2,1)} %maximum_add_fusion), calls=%async_computation.17 | async-start | bytes 2555904 | tf_op jit(solution)/shard_map/all_to_all | solution.py:370
  (124 other events, 1057.1 us)
Sparse Core Ops, SparseCore 0:
  11.4 100.6 all-gather.1
  404.6 145.4 reduce-scatter.1
